TPU v7x, 1024 devices: a whole 4x8x16 slice. The times are simulated.
1024 devices in a mesh: row: 4 (over y_lo, core), col: 16 (over y_hi, x), depth: 16 (over z).
Axes of the slice: x: 4, y: 8 (y_hi: 4, y_lo: 2; y = y_hi * 2 + y_lo), z: 16, core: 2. Of those that a mesh axis runs over, the one named last changes fastest.
Arguments:
- inputs: bfloat16 [3072, 12288], P(('row', 'col'), 'depth'), may hold values from -0.107910156 to 0.107910156
- weight: bfloat16 [12288, 18432], P('depth', 'col'), may hold values from -0.0546875 to 0.0546875
- grad_out: bfloat16 [3072, 18432], P(('row', 'depth'), 'col'), may hold values from -16 to 16
Outputs:
- grad_inputs: bfloat16 [3072, 12288], P(('row', 'col'), 'depth')
- grad_weight: bfloat16 [12288, 18432], P(('depth', 'row'), 'col')
All inputs are finite; a program needn't handle non-finite values.
Results may differ from a plain program's by a relative error of at most 0.001.
Values may be sent and summed in bfloat16 or wider, within the bound.
No kernel may reach another device: no remote copies, remote signals or barrier semaphores. Data moves between devices by JAX's collectives and lax.ppermute only.
A program may use at most 32 MiB of HBM per device.

v0:
```python
import jax
import jax.numpy as jnp
from jax import lax
from jax.sharding import PartitionSpec as P


def per_device(inputs, weight, grad_out):
    grad_rows = lax.all_gather(grad_out, "depth", axis=0, tiled=True)
    input_rows = lax.all_gather(inputs, "col", axis=0, tiled=True)
    part = grad_rows
    grad_inputs = lax.psum_scatter(
        lax.dot_general(part, weight, (((1,), (1,)), ((), ())), preferred_element_type=jnp.float32),
        "col",
        scatter_dimension=0,
        tiled=True,
    ).astype(jnp.bfloat16)
    part = input_rows
    grad_weight = lax.psum_scatter(
        lax.dot_general(
            part, grad_rows, (((0,), (0,)), ((), ())), preferred_element_type=jnp.float32
        ),
        "row",
        scatter_dimension=0,
        tiled=True,
    ).astype(jnp.bfloat16)
    return (grad_inputs, grad_weight)


def solution(mesh):
    placed = (P(("row", "col"), "depth"), P("depth", "col"), P(("row", "depth"), "col"))
    return jax.shard_map(
        per_device,
        mesh=mesh,
        in_specs=placed,
        out_specs=(P(("row", "col"), "depth"), P(("depth", "row"), "col")),
        check_vma=False,
    )
```

profile of v0, /device:TPU:1, one launch (start us, length us, event | category | flops | bytes accessed | tf_op | source)
XLA Modules:
  0.0 336.4 jit_solution(2344823990295237089)
XLA Ops:
  7.2 0.0 copy-start
  7.2 0.0 all-gather.3.cloned.1.call-start
  7.2 0.7 all-gather.3.cloned.1.call-update
  7.9 0.0 all-gather.5.cloned.1.call-start
  8.0 0.7 all-gather.5.cloned.1.call-update
  8.7 0.0 reduce-scatter.3.cloned.1.call-start
  8.7 77.2 %all-gather.3.cloned.1.call-done = bf16[768,1152]{1,0:T(8,128)(2,1)} async-done(((bf16[48,1152]{1,0:T(8,128)(2,1)}), bf16[768,1152]{1,0:T(8,128)(2,1)}) %all-gather.3.cloned.1.call-update) | async-done | bytes 1769488 | tf_op jit(solution)/shard_map/all_gather | solution.py:8
  85.9 0.0 copy-done
  85.9 4.6 %fusion = f32[768,768]{1,0:T(8,128)} fusion(bf16[768,1152]{1,0:T(8,128)(2,1)} %all-gather.3.cloned.1.call-done, bf16[768,1152]{1,0:T(8,128)(2,1)S(1)} %copy-done), kind=kOutput, calls=%fused_computation | convolution fusion | flops 1358954496 | bytes 5898240 | tf_op jit(solution)/shard_map/dot_general | solution.py:12
  90.6 0.0 copy-start.1
  90.6 0.0 reduce-scatter.3.cloned.1.call-update
  90.6 0.0 reduce-scatter.5.cloned.1.call-start
  90.6 75.0 %all-gather.5.cloned.1.call-done = bf16[768,768]{1,0:T(8,128)(2,1)} async-done(((bf16[48,768]{1,0:T(8,128)(2,1)}), bf16[768,768]{1,0:T(8,128)(2,1)}) %all-gather.5.cloned.1.call-update) | async-done | bytes 1179664 | tf_op jit(solution)/shard_map/all_gather | solution.py:9
  165.6 0.0 copy-done.1
  165.6 4.7 %fusion.1 = f32[768,1152]{1,0:T(8,128)} fusion(bf16[768,768]{1,0:T(8,128)(2,1)} %all-gather.5.cloned.1.call-done, bf16[768,1152]{1,0:T(8,128)(2,1)S(1)} %copy-done.1), kind=kOutput, calls=%fused_computation.1 | convolution fusion | flops 1358954496 | bytes 6488064 | tf_op jit(solution)/shard_map/dot_general | solution.py:19
  170.4 0.0 reduce-scatter.5.cloned.1.call-update
  170.4 102.8 %reduce-scatter.3.cloned.1.call-done = f32[48,768]{1,0:T(8,128)} async-done(((f32[768,768]{1,0:T(8,128)}), f32[48,768]{1,0:T(8,128)}) %reduce-scatter.3.cloned.1.call-update) | async-done | bytes 147472 | tf_op jit(solution)/shard_map/reduce_scatter | solution.py:11
  273.2 1.6 convert_element_type.6
  274.8 53.2 %reduce-scatter.5.cloned.1.call-done = f32[192,1152]{1,0:T(8,128)} async-done(((f32[768,1152]{1,0:T(8,128)}), f32[192,1152]{1,0:T(8,128)}) %reduce-scatter.5.cloned.1.call-update) | async-done | bytes 884752 | tf_op jit(solution)/shard_map/reduce_scatter | solution.py:18
  327.9 2.0 convert_element_type.7
Async XLA Ops:
  7.2 78.8 %copy-start = (bf16[768,1152]{1,0:T(8,128)(2,1)S(1)}, bf16[768,1152]{1,0:T(8,128)(2,1)}, u32[]{:S(2)}) copy-start(bf16[768,1152]{1,0:T(8,128)(2,1)} %param.4) | copy-start | bytes 5308420
  7.2 78.8 %all-gather.3.cloned.1.call-start = ((), (), s32[]{:S(2)}) async-start(), calls=%async_computation.2 | async-start | bytes 1880064 | tf_op jit(solution)/shard_map/all_gather | solution.py:8
  7.9 157.7 %all-gather.5.cloned.1.call-start = ((), (), s32[]{:S(2)}) async-start(), calls=%async_computation.4 | async-start | bytes 1253376 | tf_op jit(solution)/shard_map/all_gather | solution.py:9
  8.7 264.5 %reduce-scatter.3.cloned.1.call-start = ((), (), s32[]{:S(2)}) async-start(), calls=%async_computation.3 | async-start | bytes 2506752 | tf_op jit(solution)/shard_map/reduce_scatter | solution.py:11
  90.6 75.1 %copy-start.1 = (bf16[768,1152]{1,0:T(8,128)(2,1)S(1)}, bf16[768,1152]{1,0:T(8,128)(2,1)}, u32[]{:S(2)}) copy-start(bf16[768,1152]{1,0:T(8,128)(2,1)} %all-gather.3.cloned.1.call-done) | copy-start | bytes 5308420
  90.6 237.4 %reduce-scatter.5.cloned.1.call-start = ((), (), s32[]{:S(2)}) async-start(), calls=%async_computation.5 | async-start | bytes 4423680 | tf_op jit(solution)/shard_map/reduce_scatter | solution.py:18
Sparse Core Ops, SparseCore 0:
  10.7 75.2 all-gather.2
  90.1 75.4 all-gather.4
  171.0 102.1 reduce-scatter.2
  276.5 51.3 reduce-scatter.4
where the time goes:
time: 337 us; the launch traced here: 336 us
  waiting for transfers between devices  310 us (92%)
  between operations  13.8 us (4%)
  matrix products  9.37 us (3%)
  other arithmetic  3.53 us (1%)
    reduce_scatter x1, waiting for transfers between devices, per_device(): lax.psum_scatter(lax.dot_general(part, weight, (((1,), (1,)), ((), ())),...  103 us
    all_gather x1, waiting for transfers between devices, per_device(): grad_rows = lax.all_gather(grad_out, 'depth', axis=0, tiled=True)  77.2 us
    all_gather x1, waiting for transfers between devices, per_device(): input_rows = lax.all_gather(inputs, 'col', axis=0, tiled=True)  75 us
    reduce_scatter x1, waiting for transfers between devices, per_device(): lax.psum_scatter(lax.dot_general(part, grad_rows, (((0,), (0,)), ((), ())...  53.2 us
  transfers between devices with their start and end apart: 4, of which 4 were waited for; matrix products, arithmetic and copies ran while one was open for 3% of the time, Pallas kernels for 0%

commit v1 on v0

v1 whole, which is shorter than its diff:
```python
import functools

import jax
import jax.numpy as jnp
from jax import lax
from jax.experimental import pallas as pl
from jax.experimental.pallas import tpu as pltpu
from jax.sharding import PartitionSpec as P

F32 = jnp.float32
BF16 = jnp.bfloat16
VMEM = pl.BlockSpec(memory_space=pltpu.VMEM)
SMEM = pl.BlockSpec(memory_space=pltpu.SMEM)
ORDER = (0, 1, 3, 2)


def swap_x(value, j):
    return lax.ppermute(value, "col", [(i, i ^ j) for i in range(16)])


def swap_y(value, j):
    return lax.ppermute(value, "col", [(i, i ^ (4 * j)) for i in range(16)])


def swap_row(value, j):
    return lax.ppermute(value, "row", [(i, i ^ j) for i in range(4)])


def place(where, piece):
    return jnp.bitwise_xor(where, piece)


def grad_inputs_kernel(col_ref, grad_ref, weight_ref, send_a, send_b, keep_a, keep_b, rows):
    block = grad_ref.shape[0] // 16
    half = weight_ref.shape[0] // 2
    me = col_ref[0]
    for jx in range(4):
        for jy in range(4):
            source = pl.multiple_of(place(me, jy * 4 + jx) * block, block)
            rows[pl.ds((jx * 4 + jy) * block, block), :] = grad_ref[pl.ds(source, block), :]
    quarter = 4 * block
    for out_half, (sent, kept, sends, keeps) in enumerate(
        ((send_a, keep_a, (1, 2), (0, 3)), (send_b, keep_b, (3, 2), (0, 1)))
    ):
        part = lax.dot_general(
            rows[...],
            weight_ref[pl.ds(out_half * half, half), :],
            (((1,), (1,)), ((), ())),
            preferred_element_type=F32,
        )
        for slot, jx in enumerate(sends):
            sent[pl.ds(slot * quarter, quarter), :] = part[jx * quarter : (jx + 1) * quarter]
        for slot, jx in enumerate(keeps):
            kept[pl.ds(slot * quarter, quarter), :] = part[jx * quarter : (jx + 1) * quarter]


def grad_weight_kernel(place_ref, grad_ref, own, y1, y3, x1, x3, sent, kept, tokens, total):
    block = own.shape[0]
    me, row = place_ref[0], place_ref[1]
    lead = 0
    for ref in (own, y1, y3, x1, x3):
        for k in range(ref.shape[0] // block):
            j = ORDER[(lead + k) % 4] * 4 + ORDER[(lead + k) // 4]
            target = pl.multiple_of(place(me, j) * block, block)
            tokens[pl.ds(target, block), :] = ref[pl.ds(k * block, block), :]
        lead += ref.shape[0] // block
    total[...] = lax.dot_general(
        tokens[...], grad_ref[...], (((0,), (0,)), ((), ())), preferred_element_type=F32
    )
    rows = total.shape[0] // 4
    for jy in range(2):
        for jc, ref in ((1, sent), (0, kept)):
            source = pl.multiple_of(place(row, jy * 2 + jc) * rows, rows)
            ref[pl.ds(jy * rows, rows), :] = total[pl.ds(source, rows), :]


def per_device(inputs, weight, grad_out):
    block, width = inputs.shape
    columns = weight.shape[1]
    col, row = lax.axis_index("col"), lax.axis_index("row")
    grad_rows = lax.all_gather(grad_out, "depth", axis=0, tiled=True)

    y1 = swap_y(inputs, 1)
    y3 = swap_y(jnp.concatenate([inputs, y1]), 3)
    x1 = swap_x(jnp.concatenate([inputs, y1, y3]), 1)
    x3 = swap_x(jnp.concatenate([inputs, y1, y3, x1]), 3)

    tokens = block * 16
    piece = jax.ShapeDtypeStruct((tokens // 2, width // 2), F32)
    send_a, send_b, keep_a, keep_b = pl.pallas_call(
        grad_inputs_kernel,
        out_shape=[piece] * 4,
        in_specs=[SMEM, VMEM, VMEM],
        out_specs=[VMEM] * 4,
        scratch_shapes=[pltpu.VMEM((tokens, columns), BF16)],
        compiler_params=pltpu.CompilerParams(vmem_limit_bytes=32 << 20),
        cost_estimate=pl.CostEstimate(
            flops=2 * tokens * width * columns, bytes_accessed=6 << 20, transcendentals=0
        ),
        name="grad_inputs",
    )(col.reshape(1), grad_rows, weight)
    got_a, got_b = swap_x(send_a, 1), swap_x(send_b, 3)

    half = jax.ShapeDtypeStruct((width // 2, columns), F32)
    send_w, keep_w = pl.pallas_call(
        grad_weight_kernel,
        out_shape=[half] * 2,
        in_specs=[SMEM] + [VMEM] * 6,
        out_specs=[VMEM] * 2,
        scratch_shapes=[pltpu.VMEM((tokens, width), BF16), pltpu.VMEM((width, columns), F32)],
        compiler_params=pltpu.CompilerParams(vmem_limit_bytes=32 << 20),
        cost_estimate=pl.CostEstimate(
            flops=2 * tokens * width * columns, bytes_accessed=7 << 20, transcendentals=0
        ),
        name="grad_weight",
    )(jnp.stack([col, row]), grad_rows, inputs, y1, y3, x1, x3)
    got_w = swap_row(send_w, 1)

    quarter = tokens // 4
    sum_a, sum_b = keep_a + got_a, keep_b + got_b
    got_a, got_b = swap_x(sum_a[quarter:], 3), swap_x(sum_b[quarter:], 1)

    rows = width // 4
    sum_w = keep_w + got_w
    got_w = swap_row(sum_w[rows:], 2)

    mine = jnp.concatenate([sum_a[:quarter] + got_a, sum_b[:quarter] + got_b], axis=1)
    mine = mine.reshape(4, block, width)
    grad_inputs = mine[0] + swap_y(mine[1], 1) + swap_y(mine[2], 2) + swap_y(mine[3], 3)
    grad_weight = sum_w[:rows] + got_w
    return grad_inputs.astype(BF16), grad_weight.astype(BF16)


def solution(mesh):
    placed = (P(("row", "col"), "depth"), P("depth", "col"), P(("row", "depth"), "col"))
    return jax.shard_map(
        per_device,
        mesh=mesh,
        in_specs=placed,
        out_specs=(P(("row", "col"), "depth"), P(("depth", "row"), "col")),
        check_vma=False,
    )
```

time: 337 us -> 177 us (0.53)
  the two profiles are of different devices: /device:TPU:1 before, /device:TPU:10 now
where the time goes in v1:
time: 177 us; the launch traced here: 176 us
  waiting for transfers between devices  104 us (59%)
  starting transfers between devices  46.3 us (26%)
  between operations  14.3 us (8%)
  other arithmetic  4.75 us (3%)
  Pallas kernels  4.69 us (3%)
    ppermute x6, waiting for transfers between devices, swap_x(): return lax.ppermute(value, 'col', [(i, i ^ j) for i in range(16)])  36.6 us
    all_gather x1, waiting for transfers between devices, per_device(): grad_rows = lax.all_gather(grad_out, 'depth', axis=0, tiled=True)  36.6 us
    ppermute x5, waiting for transfers between devices, swap_y(): return lax.ppermute(value, 'col', [(i, i ^ 4 * j) for i in range(16)])  30.4 us
    ppermute x5, starting transfers between devices, swap_y(): return lax.ppermute(value, 'col', [(i, i ^ 4 * j) for i in range(16)])  22.8 us
    ppermute x6, starting transfers between devices, swap_x(): return lax.ppermute(value, 'col', [(i, i ^ j) for i in range(16)])  19.1 us
    ppermute x2, starting transfers between devices, swap_row(): return lax.ppermute(value, 'row', [(i, i ^ j) for i in range(4)])  4.36 us
  transfers between devices with their start and end apart: 14, of which 10 were waited for; matrix products, arithmetic and copies ran while one was open for 2% of the time, Pallas kernels for 1%

profile of v1, /device:TPU:10, one launch (start us, length us, event | category | flops | bytes accessed | tf_op | source)
XLA Modules:
  0.0 175.9 jit_solution(15567727009322607432)
XLA Ops:
  7.9 4.5 %collective-permute-start.7 = (bf16[48,768]{1,0:T(8,128)(2,1)}, bf16[48,768]{1,0:T(8,128)(2,1)S(1)}, u32[]{:S(2)}, u32[]{:S(2)}) collective-permute-start(bf16[48,768]{1,0:T(8,128)(2,1)} %own.1), channel_id=1, source_target_pairs={{0,64},{16,80},{32,96},{48,112},{64,0},{80,16},{96,32},{112,48},{1... | collective-permute-start | bytes 221192 | tf_op jit(solution)/shard_map/ppermute | solution.py:22
  12.4 3.3 %collective-permute-done.7.y1 = bf16[48,768]{1,0:T(8,128)(2,1)S(1)} collective-permute-done((bf16[48,768]{1,0:T(8,128)(2,1)}, bf16[48,768]{1,0:T(8,128)(2,1)S(1)}, u32[]{:S(2)}, u32[]{:S(2)}) %collective-permute-start.7) | collective-permute-done | bytes 73760 | tf_op jit(solution)/shard_map/ppermute | solution.py:22
  16.6 6.1 %collective-permute-start.8 = (bf16[96,768]{1,0:T(8,128)(2,1)S(1)}, bf16[96,768]{1,0:T(8,128)(2,1)S(1)}, u32[]{:S(2)}, u32[]{:S(2)}) collective-permute-start(bf16[96,768]{1,0:T(8,128)(2,1)S(1)} %pad_maximum_fusion.3), channel_id=1, source_target_pairs={{0,192},{16,208},{32,224},{48,240},{64,128},{80,144},{96,160},{112... | collective-permute-start | bytes 442376 | tf_op jit(solution)/shard_map/ppermute | solution.py:22
  22.7 6.4 %collective-permute-done.8.y3 = bf16[96,768]{1,0:T(8,128)(2,1)S(1)} collective-permute-done((bf16[96,768]{1,0:T(8,128)(2,1)S(1)}, bf16[96,768]{1,0:T(8,128)(2,1)S(1)}, u32[]{:S(2)}, u32[]{:S(2)}) %collective-permute-start.8) | collective-permute-done | bytes 147488 | tf_op jit(solution)/shard_map/ppermute | solution.py:22
  30.0 1.9 %collective-permute-start.9 = (bf16[192,768]{1,0:T(8,128)(2,1)S(1)}, bf16[192,768]{1,0:T(8,128)(2,1)S(1)}, u32[]{:S(2)}, u32[]{:S(2)}) collective-permute-start(bf16[192,768]{1,0:T(8,128)(2,1)S(1)} %pad_maximum_fusion.1), channel_id=1, source_target_pairs={{0,16},{16,0},{32,48},{48,32},{64,80},{80,64},{96,112},{112,96},{1... | collective-permute-start | bytes 884744 | tf_op jit(solution)/shard_map/ppermute | solution.py:18
  31.9 8.9 %collective-permute-done.9.x1 = bf16[192,768]{1,0:T(8,128)(2,1)S(1)} collective-permute-done((bf16[192,768]{1,0:T(8,128)(2,1)S(1)}, bf16[192,768]{1,0:T(8,128)(2,1)S(1)}, u32[]{:S(2)}, u32[]{:S(2)}) %collective-permute-start.9) | collective-permute-done | bytes 294944 | tf_op jit(solution)/shard_map/ppermute | solution.py:18
  41.8 3.4 %collective-permute-start.10 = (bf16[384,768]{1,0:T(8,128)(2,1)S(1)}, bf16[384,768]{1,0:T(8,128)(2,1)S(1)}, u32[]{:S(2)}, u32[]{:S(2)}) collective-permute-start(bf16[384,768]{1,0:T(8,128)(2,1)S(1)} %pad_maximum_fusion), channel_id=1, source_target_pairs={{0,48},{16,32},{32,16},{48,0},{64,112},{80,96},{96,80},{112,64},{1... | collective-permute-start | bytes 1769480 | tf_op jit(solution)/shard_map/ppermute | solution.py:18
  45.2 12.8 %collective-permute-done.10.x3 = bf16[384,768]{1,0:T(8,128)(2,1)S(1)} collective-permute-done((bf16[384,768]{1,0:T(8,128)(2,1)S(1)}, bf16[384,768]{1,0:T(8,128)(2,1)S(1)}, u32[]{:S(2)}, u32[]{:S(2)}) %collective-permute-start.10) | collective-permute-done | bytes 589856 | tf_op jit(solution)/shard_map/ppermute | solution.py:18
  58.1 36.6 %all-gather.2.cloned.1.call-done.grad_ref = bf16[768,1152]{1,0:T(8,128)(2,1)} async-done(((bf16[48,1152]{1,0:T(8,128)(2,1)}), bf16[768,1152]{1,0:T(8,128)(2,1)}) %all-gather.2.cloned.1.call-update) | async-done | bytes 1769488 | tf_op jit(solution)/shard_map/all_gather | solution.py:81
  96.1 2.6 %grad_weight.1 = (f32[384,1152]{1,0:T(8,128)S(1)}, f32[384,1152]{1,0:T(8,128)S(1)}) custom-call(s32[2]{0:T(128)S(1)} %pad_add_fusion.place_ref, bf16[768,1152]{1,0:T(8,128)(2,1)S(1)} %copy-done.2, bf16[48,768]{1,0:T(8,128)(2,1)S(1)} %copy-done, bf16[48,768]{1,0:T(8,128)(2,1)S(1)} %collective-permute-done.7.y1, ...), custom_call_target="tpu_custom_call" | custom-call | flops 1358954496 | bytes 7340032 | tf_op jit(solution)/shard_map/grad_weight/pallas_call | solution.py:105
  98.7 1.9 %collective-permute-start.11 = (f32[384,1152]{1,0:T(8,128)S(1)}, f32[384,1152]{1,0:T(8,128)S(1)}, u32[]{:S(2)}, u32[]{:S(2)}) collective-permute-start(f32[384,1152]{1,0:T(8,128)S(1)} %get-tuple-element.13), channel_id=1, source_target_pairs={{0,256},{256,0},{512,768},{768,512},{1,257},{257,1},{513,769},{769... | collective-permute-start | bytes 5308424 | tf_op jit(solution)/shard_map/ppermute | solution.py:26
  100.6 2.1 %grad_inputs.1 = (f32[384,384]{1,0:T(8,128)S(1)}, f32[384,384]{1,0:T(8,128)S(1)}, f32[384,384]{1,0:T(8,128)S(1)}, f32[384,384]{1,0:T(8,128)S(1)}) custom-call(s32[1]{0:T(128)} %bitcast.col_ref, bf16[768,1152]{1,0:T(8,128)(2,1)S(1)} %copy-done.3, bf16[768,1152]{1,0:T(8,128)(2,1)S(1)} %copy-done.1), custom_call_target="tpu_custom_call" | custom-call | flops 1358954496 | bytes 6291456 | tf_op jit(solution)/shard_map/grad_inputs/pallas_call | solution.py:90
  102.8 2.7 %collective-permute-start = (f32[384,384]{1,0:T(8,128)S(1)}, f32[384,384]{1,0:T(8,128)S(1)}, u32[]{:S(2)}, u32[]{:S(2)}) collective-permute-start(f32[384,384]{1,0:T(8,128)S(1)} %get-tuple-element.9), channel_id=1, source_target_pairs={{0,16},{16,0},{32,48},{48,32},{64,80},{80,64},{96,112},{112,96},{1... | collective-permute-start | bytes 1769480 | tf_op jit(solution)/shard_map/ppermute | solution.py:18
  105.4 3.9 %collective-permute-start.2 = (f32[384,384]{1,0:T(8,128)S(1)}, f32[384,384]{1,0:T(8,128)S(1)}, u32[]{:S(2)}, u32[]{:S(2)}) collective-permute-start(f32[384,384]{1,0:T(8,128)S(1)} %get-tuple-element.11), channel_id=1, source_target_pairs={{0,48},{16,32},{32,16},{48,0},{64,112},{80,96},{96,80},{112,64},{1... | collective-permute-start | bytes 1769480 | tf_op jit(solution)/shard_map/ppermute | solution.py:18
  109.4 11.0 %collective-permute-done = f32[384,384]{1,0:T(8,128)S(1)} collective-permute-done((f32[384,384]{1,0:T(8,128)S(1)}, f32[384,384]{1,0:T(8,128)S(1)}, u32[]{:S(2)}, u32[]{:S(2)}) %collective-permute-start) | collective-permute-done | bytes 589856 | tf_op jit(solution)/shard_map/ppermute | solution.py:18
  120.5 3.6 %collective-permute-start.1 = (f32[192,384]{1,0:T(8,128)S(1)}, f32[192,384]{1,0:T(8,128)S(1)}, u32[]{:S(2)}, u32[]{:S(2)}) collective-permute-start(f32[192,384]{1,0:T(8,128)S(1)} %slice.45), channel_id=1, source_target_pairs={{0,48},{16,32},{32,16},{48,0},{64,112},{80,96},{96,80},{112,64},{1... | collective-permute-start | bytes 884744 | tf_op jit(solution)/shard_map/ppermute | solution.py:18
  124.2 3.6 %collective-permute-start.3 = (f32[192,384]{1,0:T(8,128)S(1)}, f32[192,384]{1,0:T(8,128)S(1)}, u32[]{:S(2)}, u32[]{:S(2)}) collective-permute-start(f32[192,384]{1,0:T(8,128)S(1)} %slice.47), channel_id=1, source_target_pairs={{0,16},{16,0},{32,48},{48,32},{64,80},{80,64},{96,112},{112,96},{1... | collective-permute-start | bytes 884744 | tf_op jit(solution)/shard_map/ppermute | solution.py:18
  128.1 2.4 %collective-permute-start.12 = (f32[192,1152]{1,0:T(8,128)S(1)}, f32[192,1152]{1,0:T(8,128)S(1)}, u32[]{:S(2)}, u32[]{:S(2)}) collective-permute-start(f32[192,1152]{1,0:T(8,128)S(1)} %slice.55), channel_id=1, source_target_pairs={{0,512},{256,768},{512,0},{768,256},{1,513},{257,769},{513,1},{769... | collective-permute-start | bytes 2654216 | tf_op jit(solution)/shard_map/ppermute | solution.py:26
  131.0 3.4 %collective-permute-done.3 = f32[192,384]{1,0:T(8,128)S(1)} collective-permute-done((f32[192,384]{1,0:T(8,128)S(1)}, f32[192,384]{1,0:T(8,128)S(1)}, u32[]{:S(2)}, u32[]{:S(2)}) %collective-permute-start.3) | collective-permute-done | bytes 294944 | tf_op jit(solution)/shard_map/ppermute | solution.py:18
  134.5 4.3 %collective-permute-start.4 = (f32[48,768]{1,0:T(8,128)S(1)}, f32[48,768]{1,0:T(8,128)S(1)}, u32[]{:S(2)}, u32[]{:S(2)}) collective-permute-start(f32[48,768]{1,0:T(8,128)S(1)} %get-tuple-element.14), channel_id=1, source_target_pairs={{0,64},{16,80},{32,96},{48,112},{64,0},{80,16},{96,32},{112,48},{1... | collective-permute-start | bytes 442376 | tf_op jit(solution)/shard_map/ppermute | solution.py:22
  138.8 4.6 %collective-permute-start.6 = (f32[48,768]{1,0:T(8,128)S(1)}, f32[48,768]{1,0:T(8,128)S(1)}, u32[]{:S(2)}, u32[]{:S(2)}) collective-permute-start(f32[48,768]{1,0:T(8,128)S(1)} %get-tuple-element.15), channel_id=1, source_target_pairs={{0,192},{16,208},{32,224},{48,240},{64,128},{80,144},{96,160},{112... | collective-permute-start | bytes 442376 | tf_op jit(solution)/shard_map/ppermute | solution.py:22
  143.4 3.4 %collective-permute-start.5 = (f32[48,768]{1,0:T(8,128)S(1)}, f32[48,768]{1,0:T(8,128)S(1)}, u32[]{:S(2)}, u32[]{:S(2)}) collective-permute-start(f32[48,768]{1,0:T(8,128)S(1)} %get-tuple-element.16), channel_id=1, source_target_pairs={{0,128},{16,144},{32,160},{48,176},{64,192},{80,208},{96,224},{112... | collective-permute-start | bytes 442376 | tf_op jit(solution)/shard_map/ppermute | solution.py:22
  146.8 12.8 %collective-permute-done.4 = f32[48,768]{1,0:T(8,128)S(1)} collective-permute-done((f32[48,768]{1,0:T(8,128)S(1)}, f32[48,768]{1,0:T(8,128)S(1)}, u32[]{:S(2)}, u32[]{:S(2)}) %collective-permute-start.4) | collective-permute-done | bytes 147488 | tf_op jit(solution)/shard_map/ppermute | solution.py:22
  159.5 7.9 %collective-permute-done.5 = f32[48,768]{1,0:T(8,128)S(1)} collective-permute-done((f32[48,768]{1,0:T(8,128)S(1)}, f32[48,768]{1,0:T(8,128)S(1)}, u32[]{:S(2)}, u32[]{:S(2)}) %collective-permute-start.5) | collective-permute-done | bytes 147488 | tf_op jit(solution)/shard_map/ppermute | solution.py:22
  (30 shorter events, 7.6 us)
Async XLA Ops:
  7.2 87.5 %copy-start = (bf16[48,768]{1,0:T(8,128)(2,1)S(1)}, bf16[48,768]{1,0:T(8,128)(2,1)}, u32[]{:S(2)}) copy-start(bf16[48,768]{1,0:T(8,128)(2,1)} %own.1) | copy-start | bytes 221188
  7.2 87.4 %all-gather.2.cloned.1.call-start = ((), (), s32[]{:S(2)}) async-start(), calls=%async_computation | async-start | bytes 1880064 | tf_op jit(solution)/shard_map/all_gather | solution.py:81
  7.9 7.8 %collective-permute-start.7 = (bf16[48,768]{1,0:T(8,128)(2,1)}, bf16[48,768]{1,0:T(8,128)(2,1)S(1)}, u32[]{:S(2)}, u32[]{:S(2)}) collective-permute-start(bf16[48,768]{1,0:T(8,128)(2,1)} %own.1), channel_id=1, source_target_pairs={{0,64},{16,80},{32,96},{48,112},{64,0},{80,16},{96,32},{112,48},{1... | collective-permute-start | bytes 221192 | tf_op jit(solution)/shard_map/ppermute | solution.py:22
  16.6 12.5 %collective-permute-start.8 = (bf16[96,768]{1,0:T(8,128)(2,1)S(1)}, bf16[96,768]{1,0:T(8,128)(2,1)S(1)}, u32[]{:S(2)}, u32[]{:S(2)}) collective-permute-start(bf16[96,768]{1,0:T(8,128)(2,1)S(1)} %pad_maximum_fusion.3), channel_id=1, source_target_pairs={{0,192},{16,208},{32,224},{48,240},{64,128},{80,144},{96,160},{112... | collective-permute-start | bytes 442376 | tf_op jit(solution)/shard_map/ppermute | solution.py:22
  30.0 10.8 %collective-permute-start.9 = (bf16[192,768]{1,0:T(8,128)(2,1)S(1)}, bf16[192,768]{1,0:T(8,128)(2,1)S(1)}, u32[]{:S(2)}, u32[]{:S(2)}) collective-permute-start(bf16[192,768]{1,0:T(8,128)(2,1)S(1)} %pad_maximum_fusion.1), channel_id=1, source_target_pairs={{0,16},{16,0},{32,48},{48,32},{64,80},{80,64},{96,112},{112,96},{1... | collective-permute-start | bytes 884744 | tf_op jit(solution)/shard_map/ppermute | solution.py:18
  41.8 16.3 %collective-permute-start.10 = (bf16[384,768]{1,0:T(8,128)(2,1)S(1)}, bf16[384,768]{1,0:T(8,128)(2,1)S(1)}, u32[]{:S(2)}, u32[]{:S(2)}) collective-permute-start(bf16[384,768]{1,0:T(8,128)(2,1)S(1)} %pad_maximum_fusion), channel_id=1, source_target_pairs={{0,48},{16,32},{32,16},{48,0},{64,112},{80,96},{96,80},{112,64},{1... | collective-permute-start | bytes 1769480 | tf_op jit(solution)/shard_map/ppermute | solution.py:18
  45.2 55.4 %copy-start.1 = (bf16[768,1152]{1,0:T(8,128)(2,1)S(1)}, bf16[768,1152]{1,0:T(8,128)(2,1)}, u32[]{:S(2)}) copy-start(bf16[768,1152]{1,0:T(8,128)(2,1)} %weight_ref.1) | copy-start | bytes 5308420
  94.6 1.5 copy-start.2
  96.1 4.5 %copy-start.3 = (bf16[768,1152]{1,0:T(8,128)(2,1)S(1)}, bf16[768,1152]{1,0:T(8,128)(2,1)}, u32[]{:S(2)}) copy-start(bf16[768,1152]{1,0:T(8,128)(2,1)} %all-gather.2.cloned.1.call-done.grad_ref) | copy-start | bytes 5308420
  98.7 29.1 %collective-permute-start.11 = (f32[384,1152]{1,0:T(8,128)S(1)}, f32[384,1152]{1,0:T(8,128)S(1)}, u32[]{:S(2)}, u32[]{:S(2)}) collective-permute-start(f32[384,1152]{1,0:T(8,128)S(1)} %get-tuple-element.13), channel_id=1, source_target_pairs={{0,256},{256,0},{512,768},{768,512},{1,257},{257,1},{513,769},{769... | collective-permute-start | bytes 5308424 | tf_op jit(solution)/shard_map/ppermute | solution.py:26
  102.8 17.6 %collective-permute-start = (f32[384,384]{1,0:T(8,128)S(1)}, f32[384,384]{1,0:T(8,128)S(1)}, u32[]{:S(2)}, u32[]{:S(2)}) collective-permute-start(f32[384,384]{1,0:T(8,128)S(1)} %get-tuple-element.9), channel_id=1, source_target_pairs={{0,16},{16,0},{32,48},{48,32},{64,80},{80,64},{96,112},{112,96},{1... | collective-permute-start | bytes 1769480 | tf_op jit(solution)/shard_map/ppermute | solution.py:18
  105.4 18.7 %collective-permute-start.2 = (f32[384,384]{1,0:T(8,128)S(1)}, f32[384,384]{1,0:T(8,128)S(1)}, u32[]{:S(2)}, u32[]{:S(2)}) collective-permute-start(f32[384,384]{1,0:T(8,128)S(1)} %get-tuple-element.11), channel_id=1, source_target_pairs={{0,48},{16,32},{32,16},{48,0},{64,112},{80,96},{96,80},{112,64},{1... | collective-permute-start | bytes 1769480 | tf_op jit(solution)/shard_map/ppermute | solution.py:18
  120.5 10.5 %collective-permute-start.1 = (f32[192,384]{1,0:T(8,128)S(1)}, f32[192,384]{1,0:T(8,128)S(1)}, u32[]{:S(2)}, u32[]{:S(2)}) collective-permute-start(f32[192,384]{1,0:T(8,128)S(1)} %slice.45), channel_id=1, source_target_pairs={{0,48},{16,32},{32,16},{48,0},{64,112},{80,96},{96,80},{112,64},{1... | collective-permute-start | bytes 884744 | tf_op jit(solution)/shard_map/ppermute | solution.py:18
  124.2 10.2 %collective-permute-start.3 = (f32[192,384]{1,0:T(8,128)S(1)}, f32[192,384]{1,0:T(8,128)S(1)}, u32[]{:S(2)}, u32[]{:S(2)}) collective-permute-start(f32[192,384]{1,0:T(8,128)S(1)} %slice.47), channel_id=1, source_target_pairs={{0,16},{16,0},{32,48},{48,32},{64,80},{80,64},{96,112},{112,96},{1... | collective-permute-start | bytes 884744 | tf_op jit(solution)/shard_map/ppermute | solution.py:18
  128.1 40.1 %collective-permute-start.12 = (f32[192,1152]{1,0:T(8,128)S(1)}, f32[192,1152]{1,0:T(8,128)S(1)}, u32[]{:S(2)}, u32[]{:S(2)}) collective-permute-start(f32[192,1152]{1,0:T(8,128)S(1)} %slice.55), channel_id=1, source_target_pairs={{0,512},{256,768},{512,0},{768,256},{1,513},{257,769},{513,1},{769... | collective-permute-start | bytes 2654216 | tf_op jit(solution)/shard_map/ppermute | solution.py:26
  134.5 25.0 %collective-permute-start.4 = (f32[48,768]{1,0:T(8,128)S(1)}, f32[48,768]{1,0:T(8,128)S(1)}, u32[]{:S(2)}, u32[]{:S(2)}) collective-permute-start(f32[48,768]{1,0:T(8,128)S(1)} %get-tuple-element.14), channel_id=1, source_target_pairs={{0,64},{16,80},{32,96},{48,112},{64,0},{80,16},{96,32},{112,48},{1... | collective-permute-start | bytes 442376 | tf_op jit(solution)/shard_map/ppermute | solution.py:22
  138.8 20.7 %collective-permute-start.6 = (f32[48,768]{1,0:T(8,128)S(1)}, f32[48,768]{1,0:T(8,128)S(1)}, u32[]{:S(2)}, u32[]{:S(2)}) collective-permute-start(f32[48,768]{1,0:T(8,128)S(1)} %get-tuple-element.15), channel_id=1, source_target_pairs={{0,192},{16,208},{32,224},{48,240},{64,128},{80,144},{96,160},{112... | collective-permute-start | bytes 442376 | tf_op jit(solution)/shard_map/ppermute | solution.py:22
  143.4 24.1 %collective-permute-start.5 = (f32[48,768]{1,0:T(8,128)S(1)}, f32[48,768]{1,0:T(8,128)S(1)}, u32[]{:S(2)}, u32[]{:S(2)}) collective-permute-start(f32[48,768]{1,0:T(8,128)S(1)} %get-tuple-element.16), channel_id=1, source_target_pairs={{0,128},{16,144},{32,160},{48,176},{64,192},{80,208},{96,224},{112... | collective-permute-start | bytes 442376 | tf_op jit(solution)/shard_map/ppermute | solution.py:22
Sparse Core Ops, SparseCore 0:
  10.7 83.9 all-gather.1

commit v2 on v1

v2 whole, which is shorter than its diff:
```python
import jax
import jax.numpy as jnp
from jax import lax
from jax.experimental import pallas as pl
from jax.experimental.pallas import tpu as pltpu
from jax.sharding import PartitionSpec as P

F32 = jnp.float32
BF16 = jnp.bfloat16
VMEM = pl.BlockSpec(memory_space=pltpu.VMEM)
SMEM = pl.BlockSpec(memory_space=pltpu.SMEM)
ORDER = (0, 1, 3, 2)


def swap_x(value, j):
    return lax.ppermute(value, "col", [(i, i ^ j) for i in range(16)])


def swap_y(value, j):
    return lax.ppermute(value, "col", [(i, i ^ (4 * j)) for i in range(16)])


def swap_row(value, j):
    return lax.ppermute(value, "row", [(i, i ^ j) for i in range(4)])


def shift_depth(value, k):
    return lax.ppermute(value, "depth", [(i, (i + k) % 16) for i in range(16)])


def grad_inputs_kernel(place_ref, *refs):
    chunks, (weight_ref, send_a, send_b, keep_a, keep_b, rows) = refs[:16], refs[16:]
    block = chunks[0].shape[0]
    half = weight_ref.shape[0] // 2
    depth, col = place_ref[0], place_ref[1]
    for k in range(16):
        j = jnp.bitwise_xor(jnp.bitwise_and(depth + k, 15), col)
        at = jnp.bitwise_xor(j, jnp.bitwise_and(jnp.right_shift(j, 1), 5))
        at = jnp.bitwise_and(at, 3) * 4 + jnp.right_shift(at, 2)
        rows[pl.ds(pl.multiple_of(at * block, block), block), :] = chunks[k][...]
    quarter = 4 * block
    for out_half, (sent, kept, sends, keeps) in enumerate(
        ((send_a, keep_a, (1, 2), (0, 3)), (send_b, keep_b, (3, 2), (0, 1)))
    ):
        part = lax.dot_general(
            rows[...],
            weight_ref[pl.ds(out_half * half, half), :],
            (((1,), (1,)), ((), ())),
            preferred_element_type=F32,
        )
        for ref, order in ((sent, sends), (kept, keeps)):
            for slot, jx in enumerate(order):
                at = ORDER.index(jx) * quarter
                ref[pl.ds(slot * quarter, quarter), :] = part[at : at + quarter]


def grad_weight_kernel(row_ref, rows_ref, own, y1, y3, x1, x3, sent, kept, tokens, total):
    at = 0
    for ref in (own, y1, y3, x1, x3):
        tokens[pl.ds(at, ref.shape[0]), :] = ref[...]
        at += ref.shape[0]
    total[...] = lax.dot_general(
        tokens[...], rows_ref[...], (((0,), (0,)), ((), ())), preferred_element_type=F32
    )
    rows = total.shape[0] // 4
    for jy in range(2):
        for jc, ref in ((1, sent), (0, kept)):
            source = jnp.bitwise_xor(row_ref[0], jy * 2 + jc) * rows
            ref[pl.ds(jy * rows, rows), :] = total[pl.ds(pl.multiple_of(source, rows), rows), :]


def after(*values):
    return lax.optimization_barrier(values)


def per_device(inputs, weight, grad_out):
    block, width = inputs.shape
    columns = weight.shape[1]
    tokens = block * 16
    depth, col, row = (lax.axis_index(a) for a in ("depth", "col", "row"))

    chunks = [grad_out] + [None] * 15
    held, parts = inputs, [inputs]
    for k in range(1, 9):
        up, down = chunks[(17 - k) % 16], chunks[k - 1]
        if k > 2:
            up, chunks[k - 2] = after(up, chunks[k - 2])
        chunks[16 - k] = shift_depth(up, 1)
        if k < 8:
            if k > 1:
                down, chunks[17 - k] = after(down, chunks[17 - k])
            chunks[k] = shift_depth(down, -1)
        swap = {1: (swap_y, 1), 3: (swap_y, 3), 4: (swap_x, 1), 6: (swap_x, 3)}.get(k)
        if swap:
            chunks[16 - k], *parts = after(chunks[16 - k], *parts)
            held = jnp.concatenate(parts) if len(parts) > 1 else parts[0]
            parts.append(swap[0](held, swap[1]))
    y1, y3, x1, x3 = parts[1:]

    piece = jax.ShapeDtypeStruct((tokens // 2, width // 2), F32)
    send_a, send_b, keep_a, keep_b, rows_out = pl.pallas_call(
        grad_inputs_kernel,
        out_shape=[piece] * 4 + [jax.ShapeDtypeStruct((tokens, columns), BF16)],
        in_specs=[SMEM] + [VMEM] * 17,
        out_specs=[VMEM] * 5,
        compiler_params=pltpu.CompilerParams(vmem_limit_bytes=12 << 20),
        cost_estimate=pl.CostEstimate(
            flops=2 * tokens * width * columns, bytes_accessed=6 << 20, transcendentals=0
        ),
        name="grad_inputs",
    )(jnp.stack([depth, col]), *chunks, weight)
    got_a, got_b = swap_x(send_a, 1), swap_x(send_b, 3)

    half = jax.ShapeDtypeStruct((width // 2, columns), F32)
    send_w, keep_w = pl.pallas_call(
        grad_weight_kernel,
        out_shape=[half] * 2,
        in_specs=[SMEM] + [VMEM] * 6,
        out_specs=[VMEM] * 2,
        scratch_shapes=[pltpu.VMEM((tokens, width), BF16), pltpu.VMEM((width, columns), F32)],
        compiler_params=pltpu.CompilerParams(vmem_limit_bytes=20 << 20),
        cost_estimate=pl.CostEstimate(
            flops=2 * tokens * width * columns, bytes_accessed=7 << 20, transcendentals=0
        ),
        name="grad_weight",
    )(row.reshape(1), rows_out, parts[0], y1, y3, x1, x3)

    rows = width // 4
    got_w = swap_row(send_w, 1)
    sum_w = keep_w + got_w
    got_w2 = swap_row(sum_w[rows:], 2)

    quarter = tokens // 4
    got_a, got_b, sum_w = after(got_a, got_b, sum_w)
    sum_a, sum_b = keep_a + got_a, keep_b + got_b
    got_a, got_b = swap_x(sum_a[quarter:], 3), swap_x(sum_b[quarter:], 1)

    sum_a = (sum_a[:quarter] + got_a).reshape(4, block, width // 2)
    sum_b = (sum_b[:quarter] + got_b).reshape(4, block, width // 2)
    got_a = swap_y(jnp.concatenate([sum_a[1:2], sum_a[3:4]]), 1)
    got_b = swap_y(sum_b[2:4], 3)
    sum_a0, sum_a3 = sum_a[0] + got_a[0], sum_a[2] + got_a[1]
    sum_b0, sum_b1 = sum_b[0] + got_b[0], sum_b[1] + got_b[1]
    got_a, got_b = swap_y(sum_a3, 3), swap_y(sum_b1, 1)
    grad_inputs = jnp.concatenate([sum_a0 + got_a, sum_b0 + got_b], axis=1)
    grad_weight = sum_w[:rows] + got_w2
    return grad_inputs.astype(BF16), grad_weight.astype(BF16)


def solution(mesh):
    placed = (P(("row", "col"), "depth"), P("depth", "col"), P(("row", "depth"), "col"))
    return jax.shard_map(
        per_device,
        mesh=mesh,
        in_specs=placed,
        out_specs=(P(("row", "col"), "depth"), P(("depth", "row"), "col")),
        check_vma=False,
    )
```

time: 177 us -> 193 us (1.090)
  the two profiles are of different devices: /device:TPU:10 before, /device:TPU:1 now
where the time goes in v2:
time: 193 us; the launch traced here: 189 us
  starting transfers between devices  111 us (58%)
  waiting for transfers between devices  60.8 us (32%)
  other arithmetic  5.65 us (3%)
  Pallas kernels  5.24 us (3%)
  local copies, waits for them, and re-layouts  5.02 us (3%)
    ppermute x15, starting transfers between devices, shift_depth(): return lax.ppermute(value, 'depth', [(i, (i + k) % 16) for i in range(16)])  56.7 us
    ppermute x15, waiting for transfers between devices, shift_depth(): return lax.ppermute(value, 'depth', [(i, (i + k) % 16) for i in range(16)])  23.5 us
    ppermute x6, starting transfers between devices, swap_y(): return lax.ppermute(value, 'col', [(i, i ^ 4 * j) for i in range(16)])  22.6 us
    ppermute x6, waiting for transfers between devices, swap_y(): return lax.ppermute(value, 'col', [(i, i ^ 4 * j) for i in range(16)])  18.9 us
    ppermute x6, waiting for transfers between devices, swap_x(): return lax.ppermute(value, 'col', [(i, i ^ j) for i in range(16)])  18.4 us
    ppermute x6, starting transfers between devices, swap_x(): return lax.ppermute(value, 'col', [(i, i ^ j) for i in range(16)])  16.7 us
    ppermute x2, starting transfers between devices, swap_row(): return lax.ppermute(value, 'row', [(i, i ^ j) for i in range(4)])  15.1 us
    unnamed x22, local copies, waits for them, and re-layouts  4.89 us
  transfers between devices with their start and end apart: 29, of which 13 were waited for; matrix products, arithmetic and copies ran while one was open for 2% of the time, Pallas kernels for 2%

profile of v2, /device:TPU:1, one launch (start us, length us, event | category | flops | bytes accessed | tf_op | source)
XLA Modules:
  0.0 188.9 jit_solution(14986975224104394962)
XLA Ops:
  0.6 5.0 %collective-permute-start = (bf16[48,1152]{1,0:T(8,128)(2,1)}, bf16[48,1152]{1,0:T(8,128)(2,1)S(1)}, u32[]{:S(2)}, u32[]{:S(2)}) collective-permute-start(bf16[48,1152]{1,0:T(8,128)(2,1)} %refs_0_.1), channel_id=1, source_target_pairs={{0,1},{1,2},{2,3},{3,4},{4,5},{5,6},{6,7},{7,8},{8,9},{9,10},{10,1... | collective-permute-start | bytes 331784 | tf_op jit(solution)/shard_map/ppermute | solution.py:28
  5.6 15.9 %collective-permute-start.2 = (bf16[48,1152]{1,0:T(8,128)(2,1)}, bf16[48,1152]{1,0:T(8,128)(2,1)S(1)}, u32[]{:S(2)}, u32[]{:S(2)}) collective-permute-start(bf16[48,1152]{1,0:T(8,128)(2,1)} %refs_0_.1), channel_id=1, source_target_pairs={{0,15},{1,0},{2,1},{3,2},{4,3},{5,4},{6,5},{7,6},{8,7},{9,8},{10,9... | collective-permute-start | bytes 331784 | tf_op jit(solution)/shard_map/ppermute | solution.py:28
  24.5 4.8 %collective-permute-done.1.refs_14_ = bf16[48,1152]{1,0:T(8,128)(2,1)S(1)} collective-permute-done((bf16[48,1152]{1,0:T(8,128)(2,1)S(1)}, bf16[48,1152]{1,0:T(8,128)(2,1)S(1)}, u32[]{:S(2)}, u32[]{:S(2)}) %collective-permute-start.1) | collective-permute-done | bytes 110624 | tf_op jit(solution)/shard_map/ppermute | solution.py:28
  31.1 4.2 %collective-permute-start.4 = (bf16[48,768]{1,0:T(8,128)(2,1)}, bf16[48,768]{1,0:T(8,128)(2,1)S(1)}, u32[]{:S(2)}, u32[]{:S(2)}) collective-permute-start(bf16[48,768]{1,0:T(8,128)(2,1)} %own), channel_id=1, source_target_pairs={{0,64},{16,80},{32,96},{48,112},{64,0},{80,16},{96,32},{112,48},{1... | collective-permute-start | bytes 221192 | tf_op jit(solution)/shard_map/ppermute | solution.py:20
  35.4 4.6 %collective-permute-start.5 = (bf16[48,1152]{1,0:T(8,128)(2,1)S(1)}, bf16[48,1152]{1,0:T(8,128)(2,1)S(1)}, u32[]{:S(2)}, u32[]{:S(2)}) collective-permute-start(bf16[48,1152]{1,0:T(8,128)(2,1)S(1)} %collective-permute-done.2.refs_1_), channel_id=1, source_target_pairs={{0,15},{1,0},{2,1},{3,2},{4,3},{5,4},{6,5},{7,6},{8,7},{9,8},{10,9... | collective-permute-start | bytes 331784 | tf_op jit(solution)/shard_map/ppermute | solution.py:28
  40.9 5.4 %collective-permute-start.7 = (bf16[96,768]{1,0:T(8,128)(2,1)S(1)}, bf16[96,768]{1,0:T(8,128)(2,1)S(1)}, u32[]{:S(2)}, u32[]{:S(2)}) collective-permute-start(bf16[96,768]{1,0:T(8,128)(2,1)S(1)} %pad_maximum_fusion.2), channel_id=1, source_target_pairs={{0,192},{16,208},{32,224},{48,240},{64,128},{80,144},{96,160},{112... | collective-permute-start | bytes 442376 | tf_op jit(solution)/shard_map/ppermute | solution.py:20
  48.3 4.6 %collective-permute-start.8 = (bf16[48,1152]{1,0:T(8,128)(2,1)S(1)}, bf16[48,1152]{1,0:T(8,128)(2,1)S(1)}, u32[]{:S(2)}, u32[]{:S(2)}) collective-permute-start(bf16[48,1152]{1,0:T(8,128)(2,1)S(1)} %collective-permute-done.5.refs_2_), channel_id=1, source_target_pairs={{0,15},{1,0},{2,1},{3,2},{4,3},{5,4},{6,5},{7,6},{8,7},{9,8},{10,9... | collective-permute-start | bytes 331784 | tf_op jit(solution)/shard_map/ppermute | solution.py:28
  54.0 3.1 %collective-permute-start.12 = (bf16[192,768]{1,0:T(8,128)(2,1)S(1)}, bf16[192,768]{1,0:T(8,128)(2,1)S(1)}, u32[]{:S(2)}, u32[]{:S(2)}) collective-permute-start(bf16[192,768]{1,0:T(8,128)(2,1)S(1)} %pad_maximum_fusion.1), channel_id=1, source_target_pairs={{0,16},{16,0},{32,48},{48,32},{64,80},{80,64},{96,112},{112,96},{1... | collective-permute-start | bytes 884744 | tf_op jit(solution)/shard_map/ppermute | solution.py:16
  63.1 3.8 %collective-permute-done.9.refs_11_ = bf16[48,1152]{1,0:T(8,128)(2,1)S(1)} collective-permute-done((bf16[48,1152]{1,0:T(8,128)(2,1)S(1)}, bf16[48,1152]{1,0:T(8,128)(2,1)S(1)}, u32[]{:S(2)}, u32[]{:S(2)}) %collective-permute-start.9) | collective-permute-done | bytes 110624 | tf_op jit(solution)/shard_map/ppermute | solution.py:28
  69.4 4.4 %collective-permute-done.11.refs_10_ = bf16[48,1152]{1,0:T(8,128)(2,1)} collective-permute-done((bf16[48,1152]{1,0:T(8,128)(2,1)S(1)}, bf16[48,1152]{1,0:T(8,128)(2,1)}, u32[]{:S(2)}, u32[]{:S(2)}) %collective-permute-start.11) | collective-permute-done | bytes 110624 | tf_op jit(solution)/shard_map/ppermute | solution.py:28
  75.6 4.4 %collective-permute-start.20 = (bf16[384,768]{1,0:T(8,128)(2,1)}, bf16[384,768]{1,0:T(8,128)(2,1)S(1)}, u32[]{:S(2)}, u32[]{:S(2)}) collective-permute-start(bf16[384,768]{1,0:T(8,128)(2,1)} %pad_maximum_fusion), channel_id=1, source_target_pairs={{0,48},{16,32},{32,16},{48,0},{64,112},{80,96},{96,80},{112,64},{1... | collective-permute-start | bytes 1769480 | tf_op jit(solution)/shard_map/ppermute | solution.py:16
  81.9 3.7 %collective-permute-done.13.refs_5_ = bf16[48,1152]{1,0:T(8,128)(2,1)} collective-permute-done((bf16[48,1152]{1,0:T(8,128)(2,1)S(1)}, bf16[48,1152]{1,0:T(8,128)(2,1)}, u32[]{:S(2)}, u32[]{:S(2)}) %collective-permute-start.13) | collective-permute-done | bytes 110624 | tf_op jit(solution)/shard_map/ppermute | solution.py:28
  85.6 3.1 %collective-permute-start.15 = (bf16[48,1152]{1,0:T(8,128)(2,1)}, bf16[48,1152]{1,0:T(8,128)(2,1)}, u32[]{:S(2)}, u32[]{:S(2)}) collective-permute-start(bf16[48,1152]{1,0:T(8,128)(2,1)} %collective-permute-done.13.refs_5_), channel_id=1, source_target_pairs={{0,15},{1,0},{2,1},{3,2},{4,3},{5,4},{6,5},{7,6},{8,7},{9,8},{10,9... | collective-permute-start | bytes 331784 | tf_op jit(solution)/shard_map/ppermute | solution.py:28
  91.6 4.7 %collective-permute-start.16 = (bf16[48,1152]{1,0:T(8,128)(2,1)}, bf16[48,1152]{1,0:T(8,128)(2,1)S(1)}, u32[]{:S(2)}, u32[]{:S(2)}) collective-permute-start(bf16[48,1152]{1,0:T(8,128)(2,1)} %collective-permute-done.15.refs_6_), channel_id=1, source_target_pairs={{0,15},{1,0},{2,1},{3,2},{4,3},{5,4},{6,5},{7,6},{8,7},{9,8},{10,9... | collective-permute-start | bytes 331784 | tf_op jit(solution)/shard_map/ppermute | solution.py:28
  98.3 4.9 %collective-permute-done.17.refs_8_ = bf16[48,1152]{1,0:T(8,128)(2,1)S(1)} collective-permute-done((bf16[48,1152]{1,0:T(8,128)(2,1)}, bf16[48,1152]{1,0:T(8,128)(2,1)S(1)}, u32[]{:S(2)}, u32[]{:S(2)}) %collective-permute-start.17) | collective-permute-done | bytes 110624 | tf_op jit(solution)/shard_map/ppermute | solution.py:28
  106.8 3.3 %grad_inputs.1 = (f32[384,384]{1,0:T(8,128)S(1)}, f32[384,384]{1,0:T(8,128)S(1)}, f32[384,384]{1,0:T(8,128)S(1)}, f32[384,384]{1,0:T(8,128)S(1)}, bf16[768,1152]{1,0:T(8,128)(2,1)S(1)}) custom-call(s32[2]{0:T(128)S(1)} %pad_add_fusion.place_ref, bf16[48,1152]{1,0:T(8,128)(2,1)S(1)} %copy-done.2, bf16[48,1152]{1,0:T(8,128)(2,1)S(1)} %collective-permute-done.2.refs_1_, ...), custom_call_target="tpu_custom_call" | custom-call | flops 1358954496 | bytes 6291456 | tf_op jit(solution)/shard_map/grad_inputs/pallas_call | solution.py:101
  112.0 12.8 %collective-permute-start.21 = (f32[384,1152]{1,0:T(8,128)S(1)}, f32[384,1152]{1,0:T(8,128)S(1)}, u32[]{:S(2)}, u32[]{:S(2)}) collective-permute-start(f32[384,1152]{1,0:T(8,128)S(1)} %get-tuple-element.93), channel_id=1, source_target_pairs={{0,256},{256,0},{512,768},{768,512},{1,257},{257,1},{513,769},{769... | collective-permute-start | bytes 5308424 | tf_op jit(solution)/shard_map/ppermute | solution.py:24
  129.7 12.0 %collective-permute-done.18 = f32[384,384]{1,0:T(8,128)S(1)} collective-permute-done((f32[384,384]{1,0:T(8,128)S(1)}, f32[384,384]{1,0:T(8,128)S(1)}, u32[]{:S(2)}, u32[]{:S(2)}) %collective-permute-start.18) | collective-permute-done | bytes 589856 | tf_op jit(solution)/shard_map/ppermute | solution.py:16
  141.7 2.9 %collective-permute-done.19 = f32[384,384]{1,0:T(8,128)S(1)} collective-permute-done((f32[384,384]{1,0:T(8,128)S(1)}, f32[384,384]{1,0:T(8,128)S(1)}, u32[]{:S(2)}, u32[]{:S(2)}) %collective-permute-start.19) | collective-permute-done | bytes 589856 | tf_op jit(solution)/shard_map/ppermute | solution.py:16
  151.8 3.5 %collective-permute-done.22 = f32[192,384]{1,0:T(8,128)S(1)} collective-permute-done((f32[192,384]{1,0:T(8,128)S(1)}, f32[192,384]{1,0:T(8,128)S(1)}, u32[]{:S(2)}, u32[]{:S(2)}) %collective-permute-start.22) | collective-permute-done | bytes 294944 | tf_op jit(solution)/shard_map/ppermute | solution.py:16
  155.4 3.5 %collective-permute-start.23 = (f32[2,48,384]{2,1,0:T(8,128)S(1)}, f32[2,48,384]{2,1,0:T(8,128)S(1)}, u32[]{:S(2)}, u32[]{:S(2)}) collective-permute-start(f32[2,48,384]{2,1,0:T(8,128)S(1)} %pad_maximum_fusion.3), channel_id=1, source_target_pairs={{0,64},{16,80},{32,96},{48,112},{64,0},{80,16},{96,32},{112,48},{1... | collective-permute-start | bytes 442376 | tf_op jit(solution)/shard_map/ppermute | solution.py:20
  161.3 14.3 %collective-permute-done.23 = f32[2,48,384]{2,1,0:T(8,128)S(1)} collective-permute-done((f32[2,48,384]{2,1,0:T(8,128)S(1)}, f32[2,48,384]{2,1,0:T(8,128)S(1)}, u32[]{:S(2)}, u32[]{:S(2)}) %collective-permute-start.23) | collective-permute-done | bytes 147488 | tf_op jit(solution)/shard_map/ppermute | solution.py:20
  175.6 5.2 %collective-permute-start.24 = (f32[48,384]{1,0:T(8,128)S(1)}, f32[48,384]{1,0:T(8,128)S(1)}, u32[]{:S(2)}, u32[]{:S(2)}) collective-permute-start(f32[48,384]{1,0:T(8,128)S(1)} %fusion.4), channel_id=1, source_target_pairs={{0,192},{16,208},{32,224},{48,240},{64,128},{80,144},{96,160},{112... | collective-permute-start | bytes 221192 | tf_op jit(solution)/shard_map/ppermute | solution.py:20
  182.8 4.5 %collective-permute-done.27 = f32[48,384]{1,0:T(8,128)S(1)} collective-permute-done((f32[48,384]{1,0:T(8,128)S(1)}, f32[48,384]{1,0:T(8,128)S(1)}, u32[]{:S(2)}, u32[]{:S(2)}) %collective-permute-start.27) | collective-permute-done | bytes 73760 | tf_op jit(solution)/shard_map/ppermute | solution.py:20
  (79 shorter events, 49.3 us)
Async XLA Ops:
  0.6 21.9 %collective-permute-start = (bf16[48,1152]{1,0:T(8,128)(2,1)}, bf16[48,1152]{1,0:T(8,128)(2,1)S(1)}, u32[]{:S(2)}, u32[]{:S(2)}) collective-permute-start(bf16[48,1152]{1,0:T(8,128)(2,1)} %refs_0_.1), channel_id=1, source_target_pairs={{0,1},{1,2},{2,3},{3,4},{4,5},{5,6},{6,7},{7,8},{8,9},{9,10},{10,1... | collective-permute-start | bytes 331784 | tf_op jit(solution)/shard_map/ppermute | solution.py:28
  5.6 18.8 %collective-permute-start.2 = (bf16[48,1152]{1,0:T(8,128)(2,1)}, bf16[48,1152]{1,0:T(8,128)(2,1)S(1)}, u32[]{:S(2)}, u32[]{:S(2)}) collective-permute-start(bf16[48,1152]{1,0:T(8,128)(2,1)} %refs_0_.1), channel_id=1, source_target_pairs={{0,15},{1,0},{2,1},{3,2},{4,3},{5,4},{6,5},{7,6},{8,7},{9,8},{10,9... | collective-permute-start | bytes 331784 | tf_op jit(solution)/shard_map/ppermute | solution.py:28
  22.5 6.7 %collective-permute-start.1 = (bf16[48,1152]{1,0:T(8,128)(2,1)S(1)}, bf16[48,1152]{1,0:T(8,128)(2,1)S(1)}, u32[]{:S(2)}, u32[]{:S(2)}) collective-permute-start(bf16[48,1152]{1,0:T(8,128)(2,1)S(1)} %collective-permute-done.refs_15_), channel_id=1, source_target_pairs={{0,1},{1,2},{2,3},{3,4},{4,5},{5,6},{6,7},{7,8},{8,9},{9,10},{10,1... | collective-permute-start | bytes 331784 | tf_op jit(solution)/shard_map/ppermute | solution.py:28
  29.2 10.7 %collective-permute-start.3 = (bf16[48,1152]{1,0:T(8,128)(2,1)S(1)}, bf16[48,1152]{1,0:T(8,128)(2,1)S(1)}, u32[]{:S(2)}, u32[]{:S(2)}) collective-permute-start(bf16[48,1152]{1,0:T(8,128)(2,1)S(1)} %collective-permute-done.1.refs_14_), channel_id=1, source_target_pairs={{0,1},{1,2},{2,3},{3,4},{4,5},{5,6},{6,7},{7,8},{8,9},{9,10},{10,1... | collective-permute-start | bytes 331784 | tf_op jit(solution)/shard_map/ppermute | solution.py:28
  31.1 8.8 %collective-permute-start.4 = (bf16[48,768]{1,0:T(8,128)(2,1)}, bf16[48,768]{1,0:T(8,128)(2,1)S(1)}, u32[]{:S(2)}, u32[]{:S(2)}) collective-permute-start(bf16[48,768]{1,0:T(8,128)(2,1)} %own), channel_id=1, source_target_pairs={{0,64},{16,80},{32,96},{48,112},{64,0},{80,16},{96,32},{112,48},{1... | collective-permute-start | bytes 221192 | tf_op jit(solution)/shard_map/ppermute | solution.py:20
  35.4 10.9 %collective-permute-start.5 = (bf16[48,1152]{1,0:T(8,128)(2,1)S(1)}, bf16[48,1152]{1,0:T(8,128)(2,1)S(1)}, u32[]{:S(2)}, u32[]{:S(2)}) collective-permute-start(bf16[48,1152]{1,0:T(8,128)(2,1)S(1)} %collective-permute-done.2.refs_1_), channel_id=1, source_target_pairs={{0,15},{1,0},{2,1},{3,2},{4,3},{5,4},{6,5},{7,6},{8,7},{9,8},{10,9... | collective-permute-start | bytes 331784 | tf_op jit(solution)/shard_map/ppermute | solution.py:28
  40.9 12.2 %collective-permute-start.7 = (bf16[96,768]{1,0:T(8,128)(2,1)S(1)}, bf16[96,768]{1,0:T(8,128)(2,1)S(1)}, u32[]{:S(2)}, u32[]{:S(2)}) collective-permute-start(bf16[96,768]{1,0:T(8,128)(2,1)S(1)} %pad_maximum_fusion.2), channel_id=1, source_target_pairs={{0,192},{16,208},{32,224},{48,240},{64,128},{80,144},{96,160},{112... | collective-permute-start | bytes 442376 | tf_op jit(solution)/shard_map/ppermute | solution.py:20
  46.3 6.7 %collective-permute-start.6 = (bf16[48,1152]{1,0:T(8,128)(2,1)S(1)}, bf16[48,1152]{1,0:T(8,128)(2,1)S(1)}, u32[]{:S(2)}, u32[]{:S(2)}) collective-permute-start(bf16[48,1152]{1,0:T(8,128)(2,1)S(1)} %collective-permute-done.3.refs_13_), channel_id=1, source_target_pairs={{0,1},{1,2},{2,3},{3,4},{4,5},{5,6},{6,7},{7,8},{8,9},{9,10},{10,1... | collective-permute-start | bytes 331784 | tf_op jit(solution)/shard_map/ppermute | solution.py:28
  48.3 8.9 %collective-permute-start.8 = (bf16[48,1152]{1,0:T(8,128)(2,1)S(1)}, bf16[48,1152]{1,0:T(8,128)(2,1)S(1)}, u32[]{:S(2)}, u32[]{:S(2)}) collective-permute-start(bf16[48,1152]{1,0:T(8,128)(2,1)S(1)} %collective-permute-done.5.refs_2_), channel_id=1, source_target_pairs={{0,15},{1,0},{2,1},{3,2},{4,3},{5,4},{6,5},{7,6},{8,7},{9,8},{10,9... | collective-permute-start | bytes 331784 | tf_op jit(solution)/shard_map/ppermute | solution.py:28
  54.0 19.8 %collective-permute-start.12 = (bf16[192,768]{1,0:T(8,128)(2,1)S(1)}, bf16[192,768]{1,0:T(8,128)(2,1)S(1)}, u32[]{:S(2)}, u32[]{:S(2)}) collective-permute-start(bf16[192,768]{1,0:T(8,128)(2,1)S(1)} %pad_maximum_fusion.1), channel_id=1, source_target_pairs={{0,16},{16,0},{32,48},{48,32},{64,80},{80,64},{96,112},{112,96},{1... | collective-permute-start | bytes 884744 | tf_op jit(solution)/shard_map/ppermute | solution.py:16
  66.9 7.0 %collective-permute-start.11 = (bf16[48,1152]{1,0:T(8,128)(2,1)S(1)}, bf16[48,1152]{1,0:T(8,128)(2,1)}, u32[]{:S(2)}, u32[]{:S(2)}) collective-permute-start(bf16[48,1152]{1,0:T(8,128)(2,1)S(1)} %collective-permute-done.9.refs_11_), channel_id=1, source_target_pairs={{0,1},{1,2},{2,3},{3,4},{4,5},{5,6},{6,7},{7,8},{8,9},{9,10},{10,1... | collective-permute-start | bytes 331784 | tf_op jit(solution)/shard_map/ppermute | solution.py:28
  75.6 34.5 %collective-permute-start.20 = (bf16[384,768]{1,0:T(8,128)(2,1)}, bf16[384,768]{1,0:T(8,128)(2,1)S(1)}, u32[]{:S(2)}, u32[]{:S(2)}) collective-permute-start(bf16[384,768]{1,0:T(8,128)(2,1)} %pad_maximum_fusion), channel_id=1, source_target_pairs={{0,48},{16,32},{32,16},{48,0},{64,112},{80,96},{96,80},{112,64},{1... | collective-permute-start | bytes 1769480 | tf_op jit(solution)/shard_map/ppermute | solution.py:16
  88.7 7.5 %collective-permute-start.14 = (bf16[48,1152]{1,0:T(8,128)(2,1)}, bf16[48,1152]{1,0:T(8,128)(2,1)}, u32[]{:S(2)}, u32[]{:S(2)}) collective-permute-start(bf16[48,1152]{1,0:T(8,128)(2,1)} %collective-permute-done.11.refs_10_), channel_id=1, source_target_pairs={{0,1},{1,2},{2,3},{3,4},{4,5},{5,6},{6,7},{7,8},{8,9},{9,10},{10,1... | collective-permute-start | bytes 331784 | tf_op jit(solution)/shard_map/ppermute | solution.py:28
  91.6 6.7 %collective-permute-start.16 = (bf16[48,1152]{1,0:T(8,128)(2,1)}, bf16[48,1152]{1,0:T(8,128)(2,1)S(1)}, u32[]{:S(2)}, u32[]{:S(2)}) collective-permute-start(bf16[48,1152]{1,0:T(8,128)(2,1)} %collective-permute-done.15.refs_6_), channel_id=1, source_target_pairs={{0,15},{1,0},{2,1},{3,2},{4,3},{5,4},{6,5},{7,6},{8,7},{9,8},{10,9... | collective-permute-start | bytes 331784 | tf_op jit(solution)/shard_map/ppermute | solution.py:28
  96.3 6.9 %collective-permute-start.17 = (bf16[48,1152]{1,0:T(8,128)(2,1)}, bf16[48,1152]{1,0:T(8,128)(2,1)S(1)}, u32[]{:S(2)}, u32[]{:S(2)}) collective-permute-start(bf16[48,1152]{1,0:T(8,128)(2,1)} %collective-permute-done.14.refs_9_), channel_id=1, source_target_pairs={{0,1},{1,2},{2,3},{3,4},{4,5},{5,6},{6,7},{7,8},{8,9},{9,10},{10,1... | collective-permute-start | bytes 331784 | tf_op jit(solution)/shard_map/ppermute | solution.py:28
  112.0 17.5 %collective-permute-start.21 = (f32[384,1152]{1,0:T(8,128)S(1)}, f32[384,1152]{1,0:T(8,128)S(1)}, u32[]{:S(2)}, u32[]{:S(2)}) collective-permute-start(f32[384,1152]{1,0:T(8,128)S(1)} %get-tuple-element.93), channel_id=1, source_target_pairs={{0,256},{256,0},{512,768},{768,512},{1,257},{257,1},{513,769},{769... | collective-permute-start | bytes 5308424 | tf_op jit(solution)/shard_map/ppermute | solution.py:24
  124.9 16.8 %collective-permute-start.18 = (f32[384,384]{1,0:T(8,128)S(1)}, f32[384,384]{1,0:T(8,128)S(1)}, u32[]{:S(2)}, u32[]{:S(2)}) collective-permute-start(f32[384,384]{1,0:T(8,128)S(1)} %get-tuple-element.85), channel_id=1, source_target_pairs={{0,16},{16,0},{32,48},{48,32},{64,80},{80,64},{96,112},{112,96},{1... | collective-permute-start | bytes 1769480 | tf_op jit(solution)/shard_map/ppermute | solution.py:16
  126.8 17.8 %collective-permute-start.19 = (f32[384,384]{1,0:T(8,128)S(1)}, f32[384,384]{1,0:T(8,128)S(1)}, u32[]{:S(2)}, u32[]{:S(2)}) collective-permute-start(f32[384,384]{1,0:T(8,128)S(1)} %get-tuple-element.86), channel_id=1, source_target_pairs={{0,48},{16,32},{32,16},{48,0},{64,112},{80,96},{96,80},{112,64},{1... | collective-permute-start | bytes 1769480 | tf_op jit(solution)/shard_map/ppermute | solution.py:16
  144.7 10.6 %collective-permute-start.22 = (f32[192,384]{1,0:T(8,128)S(1)}, f32[192,384]{1,0:T(8,128)S(1)}, u32[]{:S(2)}, u32[]{:S(2)}) collective-permute-start(f32[192,384]{1,0:T(8,128)S(1)} %slice.85), channel_id=1, source_target_pairs={{0,48},{16,32},{32,16},{48,0},{64,112},{80,96},{96,80},{112,64},{1... | collective-permute-start | bytes 884744 | tf_op jit(solution)/shard_map/ppermute | solution.py:16
  147.5 11.4 %collective-permute-start.25 = (f32[192,384]{1,0:T(8,128)S(1)}, f32[192,384]{1,0:T(8,128)S(1)}, u32[]{:S(2)}, u32[]{:S(2)}) collective-permute-start(f32[192,384]{1,0:T(8,128)S(1)} %slice.93), channel_id=1, source_target_pairs={{0,16},{16,0},{32,48},{48,32},{64,80},{80,64},{96,112},{112,96},{1... | collective-permute-start | bytes 884744 | tf_op jit(solution)/shard_map/ppermute | solution.py:16
  149.4 38.6 %collective-permute-start.28 = (f32[192,1152]{1,0:T(8,128)S(1)}, f32[192,1152]{1,0:T(8,128)S(1)}, u32[]{:S(2)}, u32[]{:S(2)}) collective-permute-start(f32[192,1152]{1,0:T(8,128)S(1)} %slice.99), channel_id=1, source_target_pairs={{0,512},{256,768},{512,0},{768,256},{1,513},{257,769},{513,1},{769... | collective-permute-start | bytes 2654216 | tf_op jit(solution)/shard_map/ppermute | solution.py:24
  155.4 20.2 %collective-permute-start.23 = (f32[2,48,384]{2,1,0:T(8,128)S(1)}, f32[2,48,384]{2,1,0:T(8,128)S(1)}, u32[]{:S(2)}, u32[]{:S(2)}) collective-permute-start(f32[2,48,384]{2,1,0:T(8,128)S(1)} %pad_maximum_fusion.3), channel_id=1, source_target_pairs={{0,64},{16,80},{32,96},{48,112},{64,0},{80,16},{96,32},{112,48},{1... | collective-permute-start | bytes 442376 | tf_op jit(solution)/shard_map/ppermute | solution.py:20
  159.0 21.9 %collective-permute-start.26 = (f32[2,48,384]{2,1,0:T(8,128)S(1)}, f32[2,48,384]{2,1,0:T(8,128)S(1)}, u32[]{:S(2)}, u32[]{:S(2)}) collective-permute-start(f32[2,48,384]{2,1,0:T(8,128)S(1)} %bitcast.32), channel_id=1, source_target_pairs={{0,192},{16,208},{32,224},{48,240},{64,128},{80,144},{96,160},{112... | collective-permute-start | bytes 442376 | tf_op jit(solution)/shard_map/ppermute | solution.py:20
  175.6 7.2 %collective-permute-start.24 = (f32[48,384]{1,0:T(8,128)S(1)}, f32[48,384]{1,0:T(8,128)S(1)}, u32[]{:S(2)}, u32[]{:S(2)}) collective-permute-start(f32[48,384]{1,0:T(8,128)S(1)} %fusion.4), channel_id=1, source_target_pairs={{0,192},{16,208},{32,224},{48,240},{64,128},{80,144},{96,160},{112... | collective-permute-start | bytes 221192 | tf_op jit(solution)/shard_map/ppermute | solution.py:20
  (16 other events, 290.2 us)

commit v3 on v2

v3 whole, which is shorter than its diff:
```python
import jax
import jax.numpy as jnp
from jax import lax
from jax.experimental import pallas as pl
from jax.experimental.pallas import tpu as pltpu
from jax.sharding import PartitionSpec as P

F32 = jnp.float32
BF16 = jnp.bfloat16
VMEM = pl.BlockSpec(memory_space=pltpu.VMEM)
SMEM = pl.BlockSpec(memory_space=pltpu.SMEM)
ORDER = (0, 1, 3, 2)


def swap_x(value, j):
    return lax.ppermute(value, "col", [(i, i ^ j) for i in range(16)])


def swap_y(value, j):
    return lax.ppermute(value, "col", [(i, i ^ (4 * j)) for i in range(16)])


def swap_row(value, j):
    return lax.ppermute(value, "row", [(i, i ^ j) for i in range(4)])


def grad_inputs_kernel(col_ref, grad_lo, grad_hi, weight_ref, send_a, send_b, keep_a, keep_b, rows):
    block = grad_lo.shape[0] // 16
    half, cut = weight_ref.shape[0] // 2, grad_lo.shape[1]
    for at in range(16):
        j = ORDER[at % 4] * 4 + at // 4
        source = pl.multiple_of(jnp.bitwise_xor(col_ref[0], j) * block, block)
        rows[pl.ds(at * block, block), :cut] = grad_lo[pl.ds(source, block), :]
        rows[pl.ds(at * block, block), cut:] = grad_hi[pl.ds(source, block), :]
    quarter = 4 * block
    for out_half, (sent, kept, sends, keeps) in enumerate(
        ((send_a, keep_a, (1, 2), (0, 3)), (send_b, keep_b, (3, 2), (0, 1)))
    ):
        part = lax.dot_general(
            rows[...],
            weight_ref[pl.ds(out_half * half, half), :],
            (((1,), (1,)), ((), ())),
            preferred_element_type=F32,
        )
        for ref, order in ((sent, sends), (kept, keeps)):
            for slot, jx in enumerate(order):
                ref[pl.ds(slot * quarter, quarter), :] = part[jx * quarter : (jx + 1) * quarter]


def grad_weight_kernel(row_ref, grad_lo, grad_hi, in_lo, in_hi, sent, kept, total):
    height, cut = in_lo.shape[1], grad_lo.shape[1]
    for i, tokens in enumerate((in_lo, in_hi)):
        for grads, columns in ((grad_lo, slice(0, cut)), (grad_hi, slice(cut, None))):
            total[pl.ds(i * height, height), columns] = lax.dot_general(
                tokens[...], grads[...], (((0,), (0,)), ((), ())), preferred_element_type=F32
            )
    rows = total.shape[0] // 4
    for jy in range(2):
        for jc, ref in ((1, sent), (0, kept)):
            source = jnp.bitwise_xor(row_ref[0], jy * 2 + jc) * rows
            ref[pl.ds(jy * rows, rows), :] = total[pl.ds(pl.multiple_of(source, rows), rows), :]


def after(*values):
    return lax.optimization_barrier(values)


def per_device(inputs, weight, grad_out):
    block, width = inputs.shape
    columns = weight.shape[1]
    tokens = block * 16
    col, row = lax.axis_index("col"), lax.axis_index("row")
    cut = columns * 5 // 9
    grads = [
        lax.all_gather(part, "depth", axis=0, tiled=True)
        for part in (grad_out[:, :cut], grad_out[:, cut:])
    ]
    gathered = [
        lax.all_gather(part, "col", axis=0, tiled=True)
        for part in (inputs[:, : width // 2], inputs[:, width // 2 :])
    ]

    piece = jax.ShapeDtypeStruct((tokens // 2, width // 2), F32)
    send_a, send_b, keep_a, keep_b = pl.pallas_call(
        grad_inputs_kernel,
        out_shape=[piece] * 4,
        in_specs=[SMEM] + [VMEM] * 3,
        out_specs=[VMEM] * 4,
        scratch_shapes=[pltpu.VMEM((tokens, columns), BF16)],
        compiler_params=pltpu.CompilerParams(vmem_limit_bytes=12 << 20),
        cost_estimate=pl.CostEstimate(
            flops=2 * tokens * width * columns, bytes_accessed=6 << 20, transcendentals=0
        ),
        name="grad_inputs",
    )(col.reshape(1), *grads, weight)
    got_a, got_b = swap_x(send_a, 1), swap_x(send_b, 3)

    half = jax.ShapeDtypeStruct((width // 2, columns), F32)
    send_w, keep_w = pl.pallas_call(
        grad_weight_kernel,
        out_shape=[half] * 2,
        in_specs=[SMEM] + [VMEM] * 4,
        out_specs=[VMEM] * 2,
        scratch_shapes=[pltpu.VMEM((width, columns), F32)],
        compiler_params=pltpu.CompilerParams(vmem_limit_bytes=20 << 20),
        cost_estimate=pl.CostEstimate(
            flops=2 * tokens * width * columns, bytes_accessed=7 << 20, transcendentals=0
        ),
        name="grad_weight",
    )(row.reshape(1), *grads, *gathered)

    rows = width // 4
    got_w = swap_row(send_w, 1)
    sum_w = keep_w[rows:] + got_w[rows:]
    got_w2 = swap_row(sum_w, 2)

    quarter = tokens // 4
    got_a, got_b, sum_w = after(got_a, got_b, sum_w)
    sum_a, sum_b = keep_a + got_a, keep_b + got_b
    got_a, got_b = swap_x(sum_a[quarter:], 3), swap_x(sum_b[quarter:], 1)

    sum_a = (sum_a[:quarter] + got_a).reshape(4, block, width // 2)
    sum_b = (sum_b[:quarter] + got_b).reshape(4, block, width // 2)
    got_a = swap_y(jnp.concatenate([sum_a[1:2], sum_a[3:4]]), 1)
    got_b = swap_y(sum_b[2:4], 3)
    sum_a0, sum_a3 = sum_a[0] + got_a[0], sum_a[2] + got_a[1]
    sum_b0, sum_b1 = sum_b[0] + got_b[0], sum_b[1] + got_b[1]
    got_a, got_b = swap_y(sum_a3, 3), swap_y(sum_b1, 1)
    grad_inputs = jnp.concatenate([sum_a0 + got_a, sum_b0 + got_b], axis=1)
    grad_weight = keep_w[:rows] + got_w[:rows] + got_w2
    return grad_inputs.astype(BF16), grad_weight.astype(BF16)


def solution(mesh):
    placed = (P(("row", "col"), "depth"), P("depth", "col"), P(("row", "depth"), "col"))
    return jax.shard_map(
        per_device,
        mesh=mesh,
        in_specs=placed,
        out_specs=(P(("row", "col"), "depth"), P(("depth", "row"), "col")),
        check_vma=False,
    )
```

time: 193 us -> 256 us (1.33)
  blocking collectives: 0 us -> 149 us
  starting transfers between devices: 111 us -> 51.6 us
  waiting for transfers between devices: 60.8 us -> 36.8 us
    all_gather x0 -> x4, blocking collectives: none -> 149 us  [the longest x2 83.1 us: per_device(): lax.all_gather(part, 'col', axis=0, tiled=True)]
    ppermute x15 -> x0, starting transfers between devices: 56.7 us -> none  [shift_depth(): return lax.ppermute(value, 'depth', [(i, (i + k) % 16) for i in range(16)])]
    ppermute x15 -> x0, waiting for transfers between devices: 23.5 us -> none  [shift_depth(): return lax.ppermute(value, 'depth', [(i, (i + k) % 16) for i in range(16)])]
    ppermute x2, starting transfers between devices: 15.1 us -> 31 us  [swap_row(): return lax.ppermute(value, 'row', [(i, i ^ j) for i in range(4)])]
    ppermute x6 -> x4, starting transfers between devices: 22.6 us -> 11.1 us  [swap_y(): return lax.ppermute(value, 'col', [(i, i ^ 4 * j) for i in range(16)])]
    ppermute x6 -> x4, starting transfers between devices: 16.7 us -> 9.52 us  [swap_x(): return lax.ppermute(value, 'col', [(i, i ^ j) for i in range(16)])]
    concatenate x3 -> x0, other arithmetic: 3.6 us -> none  [per_device(): held = jnp.concatenate(parts) if len(parts) > 1 else parts[0]]
    ppermute x6 -> x4, waiting for transfers between devices: 18.9 us -> 16.9 us  [swap_y(): return lax.ppermute(value, 'col', [(i, i ^ 4 * j) for i in range(16)])]
  transfers between devices with their start and end apart: 29 -> 10, of which waited for: 13 -> 7; matrix products, arithmetic and copies ran while one was open for 2% -> 1% of each run, Pallas kernels for 2% -> 1%
where the time goes in v3:
time: 256 us; the launch traced here: 253 us
  blocking collectives  149 us (58%)
  starting transfers between devices  51.6 us (20%)
  waiting for transfers between devices  36.8 us (14%)
  local copies, waits for them, and re-layouts  5.35 us (2%)
  Pallas kernels  5.34 us (2%)
  other arithmetic  4.25 us (2%)
    all_gather x2, blocking collectives, per_device(): lax.all_gather(part, 'col', axis=0, tiled=True)  83.1 us
    all_gather x2, blocking collectives, per_device(): lax.all_gather(part, 'depth', axis=0, tiled=True)  65.5 us
    ppermute x2, starting transfers between devices, swap_row(): return lax.ppermute(value, 'row', [(i, i ^ j) for i in range(4)])  31 us
    ppermute x4, waiting for transfers between devices, swap_x(): return lax.ppermute(value, 'col', [(i, i ^ j) for i in range(16)])  19.9 us
    ppermute x4, waiting for transfers between devices, swap_y(): return lax.ppermute(value, 'col', [(i, i ^ 4 * j) for i in range(16)])  16.9 us
    ppermute x4, starting transfers between devices, swap_y(): return lax.ppermute(value, 'col', [(i, i ^ 4 * j) for i in range(16)])  11.1 us
    ppermute x4, starting transfers between devices, swap_x(): return lax.ppermute(value, 'col', [(i, i ^ j) for i in range(16)])  9.52 us
  transfers between devices with their start and end apart: 10, of which 7 were waited for; matrix products, arithmetic and copies ran while one was open for 1% of the time, Pallas kernels for 1%

profile of v3, /device:TPU:1, one launch (start us, length us, event | category | flops | bytes accessed | tf_op | source)
XLA Modules:
  0.0 252.8 jit_solution(12646472509773957044)
XLA Ops:
  2.3 41.9 %all_gather.12.grad_lo = bf16[768,640]{1,0:T(8,128)(2,1)S(1)} all-gather(bf16[48,640]{1,0:T(8,128)(2,1)S(1)} %slice.82), channel_id=1, replica_groups=mesh['row'=4,'col'=16,'depth'=16] {'depth'}, dimensions={0}, use_global_device_ids=true | all-gather | bytes 1044480 | tf_op jit(solution)/shard_map/all_gather | solution.py:75
  44.2 23.6 %all_gather.13.grad_hi = bf16[768,512]{1,0:T(8,128)(2,1)S(1)} all-gather(bf16[48,512]{1,0:T(8,128)(2,1)S(1)} %slice.83), channel_id=1, replica_groups=mesh['row'=4,'col'=16,'depth'=16] {'depth'}, dimensions={0}, use_global_device_ids=true | all-gather | bytes 835584 | tf_op jit(solution)/shard_map/all_gather | solution.py:75
  67.8 45.0 %all_gather.14.in_lo = bf16[768,384]{1,0:T(8,128)(2,1)} all-gather(bf16[48,384]{1,0:T(8,128)(2,1)S(1)} %get-tuple-element.21), channel_id=1, replica_groups=mesh['row'=4,'col'=16,'depth'=16] {'col'}, dimensions={0}, use_global_device_ids=true | all-gather | bytes 626688 | tf_op jit(solution)/shard_map/all_gather | solution.py:79
  112.8 38.1 %all_gather.15.in_hi = bf16[768,384]{1,0:T(8,128)(2,1)} all-gather(bf16[48,384]{1,0:T(8,128)(2,1)S(1)} %get-tuple-element.20), channel_id=1, replica_groups=mesh['row'=4,'col'=16,'depth'=16] {'col'}, dimensions={0}, use_global_device_ids=true | all-gather | bytes 626688 | tf_op jit(solution)/shard_map/all_gather | solution.py:79
  153.1 3.2 %grad_weight.1 = (f32[384,1152]{1,0:T(8,128)}, f32[384,1152]{1,0:T(8,128)S(1)}) custom-call(s32[1]{0:T(128)} %bitcast.1.row_ref, bf16[768,640]{1,0:T(8,128)(2,1)S(1)} %all_gather.12.grad_lo, bf16[768,512]{1,0:T(8,128)(2,1)S(1)} %all_gather.13.grad_hi, bf16[768,384]{1,0:T(8,128)(2,1)S(1)} %copy-done, bf16[768,384]{1,0:T(8,128)(2,1)S(1)} %copy-done.1), custom_call_target="tpu_custom_call" | custom-call | flops 1358954496 | bytes 7340032 | tf_op jit(solution)/shard_map/grad_weight/pallas_call | solution.py:99
  156.3 29.1 %collective-permute-start.2 = (f32[384,1152]{1,0:T(8,128)}, f32[384,1152]{1,0:T(8,128)}, u32[]{:S(2)}, u32[]{:S(2)}) collective-permute-start(f32[384,1152]{1,0:T(8,128)} %get-tuple-element.14), channel_id=1, source_target_pairs={{0,256},{256,0},{512,768},{768,512},{1,257},{257,1},{513,769},{769... | collective-permute-start | bytes 5308424 | tf_op jit(solution)/shard_map/ppermute | solution.py:24
  185.4 1.5 copy-done.2
  186.9 2.1 grad_inputs.1
  189.0 3.4 %collective-permute-start = (f32[384,384]{1,0:T(8,128)S(1)}, f32[384,384]{1,0:T(8,128)S(1)}, u32[]{:S(2)}, u32[]{:S(2)}) collective-permute-start(f32[384,384]{1,0:T(8,128)S(1)} %get-tuple-element.11), channel_id=1, source_target_pairs={{0,16},{16,0},{32,48},{48,32},{64,80},{80,64},{96,112},{112,96},{1... | collective-permute-start | bytes 1769480 | tf_op jit(solution)/shard_map/ppermute | solution.py:16
  192.5 1.9 collective-permute-start.1
  194.4 1.3 slice_add_fusion.1
  195.7 10.4 %collective-permute-done = f32[384,384]{1,0:T(8,128)S(1)} collective-permute-done((f32[384,384]{1,0:T(8,128)S(1)}, f32[384,384]{1,0:T(8,128)S(1)}, u32[]{:S(2)}, u32[]{:S(2)}) %collective-permute-start) | collective-permute-done | bytes 589856 | tf_op jit(solution)/shard_map/ppermute | solution.py:16
  206.0 4.2 %collective-permute-done.1 = f32[384,384]{1,0:T(8,128)S(1)} collective-permute-done((f32[384,384]{1,0:T(8,128)S(1)}, f32[384,384]{1,0:T(8,128)S(1)}, u32[]{:S(2)}, u32[]{:S(2)}) %collective-permute-start.1) | collective-permute-done | bytes 589856 | tf_op jit(solution)/shard_map/ppermute | solution.py:16
  210.3 2.2 collective-permute-start.3
  212.5 1.9 collective-permute-start.9
  214.6 1.9 collective-permute-start.6
  216.5 4.3 %collective-permute-done.3 = f32[192,384]{1,0:T(8,128)S(1)} collective-permute-done((f32[192,384]{1,0:T(8,128)S(1)}, f32[192,384]{1,0:T(8,128)S(1)}, u32[]{:S(2)}, u32[]{:S(2)}) %collective-permute-start.3) | collective-permute-done | bytes 294944 | tf_op jit(solution)/shard_map/ppermute | solution.py:16
  220.9 1.9 collective-permute-start.4
  223.9 2.2 collective-permute-start.7
  226.1 12.8 %collective-permute-done.4 = f32[2,48,384]{2,1,0:T(8,128)S(1)} collective-permute-done((f32[2,48,384]{2,1,0:T(8,128)S(1)}, f32[2,48,384]{2,1,0:T(8,128)S(1)}, u32[]{:S(2)}, u32[]{:S(2)}) %collective-permute-start.4) | collective-permute-done | bytes 147488 | tf_op jit(solution)/shard_map/ppermute | solution.py:20
  239.0 5.0 %collective-permute-start.5 = (f32[48,384]{1,0:T(8,128)S(1)}, f32[48,384]{1,0:T(8,128)S(1)}, u32[]{:S(2)}, u32[]{:S(2)}) collective-permute-start(f32[48,384]{1,0:T(8,128)S(1)} %fusion.6), channel_id=1, source_target_pairs={{0,192},{16,208},{32,224},{48,240},{64,128},{80,144},{96,160},{112... | collective-permute-start | bytes 221192 | tf_op jit(solution)/shard_map/ppermute | solution.py:20
  244.0 1.9 collective-permute-start.8
  246.3 3.8 %collective-permute-done.8 = f32[48,384]{1,0:T(8,128)S(1)} collective-permute-done((f32[48,384]{1,0:T(8,128)S(1)}, f32[48,384]{1,0:T(8,128)S(1)}, u32[]{:S(2)}, u32[]{:S(2)}) %collective-permute-start.8) | collective-permute-done | bytes 73760 | tf_op jit(solution)/shard_map/ppermute | solution.py:20
  250.7 2.1 fusion.1
  (29 shorter events, 6.2 us)
Async XLA Ops:
  0.6 67.2 %copy-start.3 = (bf16[48,768]{1,0:T(8,128)(2,1)S(1)}, bf16[48,768]{1,0:T(8,128)(2,1)}, u32[]{:S(2)}) copy-start(bf16[48,768]{1,0:T(8,128)(2,1)} %param.3) | copy-start | bytes 221188
  151.0 1.1 copy-start
  152.0 1.1 copy-start.1
  156.3 38.1 %collective-permute-start.2 = (f32[384,1152]{1,0:T(8,128)}, f32[384,1152]{1,0:T(8,128)}, u32[]{:S(2)}, u32[]{:S(2)}) collective-permute-start(f32[384,1152]{1,0:T(8,128)} %get-tuple-element.14), channel_id=1, source_target_pairs={{0,256},{256,0},{512,768},{768,512},{1,257},{257,1},{513,769},{769... | collective-permute-start | bytes 5308424 | tf_op jit(solution)/shard_map/ppermute | solution.py:24
  185.4 1.5 copy-start.2
  189.0 17.0 %collective-permute-start = (f32[384,384]{1,0:T(8,128)S(1)}, f32[384,384]{1,0:T(8,128)S(1)}, u32[]{:S(2)}, u32[]{:S(2)}) collective-permute-start(f32[384,384]{1,0:T(8,128)S(1)} %get-tuple-element.11), channel_id=1, source_target_pairs={{0,16},{16,0},{32,48},{48,32},{64,80},{80,64},{96,112},{112,96},{1... | collective-permute-start | bytes 1769480 | tf_op jit(solution)/shard_map/ppermute | solution.py:16
  192.5 17.7 %collective-permute-start.1 = (f32[384,384]{1,0:T(8,128)S(1)}, f32[384,384]{1,0:T(8,128)S(1)}, u32[]{:S(2)}, u32[]{:S(2)}) collective-permute-start(f32[384,384]{1,0:T(8,128)S(1)} %get-tuple-element.12), channel_id=1, source_target_pairs={{0,48},{16,32},{32,16},{48,0},{64,112},{80,96},{96,80},{112,64},{1... | collective-permute-start | bytes 1769480 | tf_op jit(solution)/shard_map/ppermute | solution.py:16
  210.3 10.5 %collective-permute-start.3 = (f32[192,384]{1,0:T(8,128)S(1)}, f32[192,384]{1,0:T(8,128)S(1)}, u32[]{:S(2)}, u32[]{:S(2)}) collective-permute-start(f32[192,384]{1,0:T(8,128)S(1)} %slice.110), channel_id=1, source_target_pairs={{0,48},{16,32},{32,16},{48,0},{64,112},{80,96},{96,80},{112,64},{1... | collective-permute-start | bytes 884744 | tf_op jit(solution)/shard_map/ppermute | solution.py:16
  212.5 38.2 %collective-permute-start.9 = (f32[192,1152]{1,0:T(8,128)S(1)}, f32[192,1152]{1,0:T(8,128)S(1)}, u32[]{:S(2)}, u32[]{:S(2)}) collective-permute-start(f32[192,1152]{1,0:T(8,128)S(1)} %slice_add_fusion.1), channel_id=1, source_target_pairs={{0,512},{256,768},{512,0},{768,256},{1,513},{257,769},{513,1},{769... | collective-permute-start | bytes 2654216 | tf_op jit(solution)/shard_map/ppermute | solution.py:24
  214.6 9.3 %collective-permute-start.6 = (f32[192,384]{1,0:T(8,128)S(1)}, f32[192,384]{1,0:T(8,128)S(1)}, u32[]{:S(2)}, u32[]{:S(2)}) collective-permute-start(f32[192,384]{1,0:T(8,128)S(1)} %slice.118), channel_id=1, source_target_pairs={{0,16},{16,0},{32,48},{48,32},{64,80},{80,64},{96,112},{112,96},{1... | collective-permute-start | bytes 884744 | tf_op jit(solution)/shard_map/ppermute | solution.py:16
  220.9 18.1 %collective-permute-start.4 = (f32[2,48,384]{2,1,0:T(8,128)S(1)}, f32[2,48,384]{2,1,0:T(8,128)S(1)}, u32[]{:S(2)}, u32[]{:S(2)}) collective-permute-start(f32[2,48,384]{2,1,0:T(8,128)S(1)} %pad_maximum_fusion), channel_id=1, source_target_pairs={{0,64},{16,80},{32,96},{48,112},{64,0},{80,16},{96,32},{112,48},{1... | collective-permute-start | bytes 442376 | tf_op jit(solution)/shard_map/ppermute | solution.py:20
  223.9 20.1 %collective-permute-start.7 = (f32[2,48,384]{2,1,0:T(8,128)S(1)}, f32[2,48,384]{2,1,0:T(8,128)S(1)}, u32[]{:S(2)}, u32[]{:S(2)}) collective-permute-start(f32[2,48,384]{2,1,0:T(8,128)S(1)} %bitcast.31), channel_id=1, source_target_pairs={{0,192},{16,208},{32,224},{48,240},{64,128},{80,144},{96,160},{112... | collective-permute-start | bytes 442376 | tf_op jit(solution)/shard_map/ppermute | solution.py:20
  239.0 7.3 %collective-permute-start.5 = (f32[48,384]{1,0:T(8,128)S(1)}, f32[48,384]{1,0:T(8,128)S(1)}, u32[]{:S(2)}, u32[]{:S(2)}) collective-permute-start(f32[48,384]{1,0:T(8,128)S(1)} %fusion.6), channel_id=1, source_target_pairs={{0,192},{16,208},{32,224},{48,240},{64,128},{80,144},{96,160},{112... | collective-permute-start | bytes 221192 | tf_op jit(solution)/shard_map/ppermute | solution.py:20
  244.0 6.0 %collective-permute-start.8 = (f32[48,384]{1,0:T(8,128)S(1)}, f32[48,384]{1,0:T(8,128)S(1)}, u32[]{:S(2)}, u32[]{:S(2)}) collective-permute-start(f32[48,384]{1,0:T(8,128)S(1)} %fusion.2), channel_id=1, source_target_pairs={{0,64},{16,80},{32,96},{48,112},{64,0},{80,16},{96,32},{112,48},{1... | collective-permute-start | bytes 221192 | tf_op jit(solution)/shard_map/ppermute | solution.py:20

commit v4 on v3

--- a/solution.py
+++ b/solution.py
@@ -24,7 +24,7 @@
     return lax.ppermute(value, "row", [(i, i ^ j) for i in range(4)])
 
 
-def grad_inputs_kernel(col_ref, grad_lo, grad_hi, weight_ref, send_a, send_b, keep_a, keep_b, rows):
+def grad_inputs_kernel(col_ref, grad_lo, grad_hi, weight_ref, send_a, send_b, keep_a, keep_b, first, rows):
     block = grad_lo.shape[0] // 16
     half, cut = weight_ref.shape[0] // 2, grad_lo.shape[1]
     for at in range(16):
@@ -32,6 +32,7 @@
         source = pl.multiple_of(jnp.bitwise_xor(col_ref[0], j) * block, block)
         rows[pl.ds(at * block, block), :cut] = grad_lo[pl.ds(source, block), :]
         rows[pl.ds(at * block, block), cut:] = grad_hi[pl.ds(source, block), :]
+    first[...] = jnp.zeros_like(first)
     quarter = 4 * block
     for out_half, (sent, kept, sends, keeps) in enumerate(
         ((send_a, keep_a, (1, 2), (0, 3)), (send_b, keep_b, (3, 2), (0, 1)))
@@ -47,13 +48,12 @@
                 ref[pl.ds(slot * quarter, quarter), :] = part[jx * quarter : (jx + 1) * quarter]
 
 
-def grad_weight_kernel(row_ref, grad_lo, grad_hi, in_lo, in_hi, sent, kept, total):
-    height, cut = in_lo.shape[1], grad_lo.shape[1]
-    for i, tokens in enumerate((in_lo, in_hi)):
-        for grads, columns in ((grad_lo, slice(0, cut)), (grad_hi, slice(cut, None))):
-            total[pl.ds(i * height, height), columns] = lax.dot_general(
-                tokens[...], grads[...], (((0,), (0,)), ((), ())), preferred_element_type=F32
-            )
+def grad_weight_kernel(row_ref, _, grad_lo, grad_hi, tokens, sent, kept, total):
+    cut = grad_lo.shape[1]
+    for grads, columns in ((grad_lo, slice(0, cut)), (grad_hi, slice(cut, None))):
+        total[:, columns] = lax.dot_general(
+            tokens[...], grads[...], (((0,), (0,)), ((), ())), preferred_element_type=F32
+        )
     rows = total.shape[0] // 4
     for jy in range(2):
         for jc, ref in ((1, sent), (0, kept)):
@@ -75,17 +75,14 @@
         lax.all_gather(part, "depth", axis=0, tiled=True)
         for part in (grad_out[:, :cut], grad_out[:, cut:])
     ]
-    gathered = [
-        lax.all_gather(part, "col", axis=0, tiled=True)
-        for part in (inputs[:, : width // 2], inputs[:, width // 2 :])
-    ]
+    gathered = lax.all_gather(inputs, "col", axis=0, tiled=True)
 
     piece = jax.ShapeDtypeStruct((tokens // 2, width // 2), F32)
-    send_a, send_b, keep_a, keep_b = pl.pallas_call(
+    send_a, send_b, keep_a, keep_b, first = pl.pallas_call(
         grad_inputs_kernel,
-        out_shape=[piece] * 4,
+        out_shape=[piece] * 4 + [jax.ShapeDtypeStruct((8, 128), F32)],
         in_specs=[SMEM] + [VMEM] * 3,
-        out_specs=[VMEM] * 4,
+        out_specs=[VMEM] * 5,
         scratch_shapes=[pltpu.VMEM((tokens, columns), BF16)],
         compiler_params=pltpu.CompilerParams(vmem_limit_bytes=12 << 20),
         cost_estimate=pl.CostEstimate(
@@ -102,12 +99,12 @@
         in_specs=[SMEM] + [VMEM] * 4,
         out_specs=[VMEM] * 2,
         scratch_shapes=[pltpu.VMEM((width, columns), F32)],
-        compiler_params=pltpu.CompilerParams(vmem_limit_bytes=20 << 20),
+        compiler_params=pltpu.CompilerParams(vmem_limit_bytes=14 << 20),
         cost_estimate=pl.CostEstimate(
             flops=2 * tokens * width * columns, bytes_accessed=7 << 20, transcendentals=0
         ),
         name="grad_weight",
-    )(row.reshape(1), *grads, *gathered)
+    )(row.reshape(1), first, *grads, gathered)
 
     rows = width // 4
     got_w = swap_row(send_w, 1)
@@ -119,6 +116,7 @@
     sum_a, sum_b = keep_a + got_a, keep_b + got_b
     got_a, got_b = swap_x(sum_a[quarter:], 3), swap_x(sum_b[quarter:], 1)
 
+    got_a, got_b, got_w2 = after(got_a, got_b, got_w2)
     sum_a = (sum_a[:quarter] + got_a).reshape(4, block, width // 2)
     sum_b = (sum_b[:quarter] + got_b).reshape(4, block, width // 2)
     got_a = swap_y(jnp.concatenate([sum_a[1:2], sum_a[3:4]]), 1)

time: 256 us -> 165 us (0.64)
  the two profiles are of different devices: /device:TPU:1 before, /device:TPU:8 now
where the time goes in v4:
time: 165 us; the launch traced here: 164 us
  blocking collectives  79 us (48%)
  starting transfers between devices  33.9 us (21%)
  waiting for transfers between devices  27.5 us (17%)
  between operations  14.2 us (9%)
  Pallas kernels  4.11 us (2%)
  local copies, waits for them, and re-layouts  3.81 us (2%)
  other arithmetic  1.89 us (1%)
    all_gather x2, blocking collectives, per_device(): lax.all_gather(part, 'depth', axis=0, tiled=True)  79 us
    ppermute x4, waiting for transfers between devices, swap_x(): return lax.ppermute(value, 'col', [(i, i ^ j) for i in range(16)])  19.8 us
    ppermute x4, starting transfers between devices, swap_y(): return lax.ppermute(value, 'col', [(i, i ^ 4 * j) for i in range(16)])  15.7 us
    ppermute x4, starting transfers between devices, swap_x(): return lax.ppermute(value, 'col', [(i, i ^ j) for i in range(16)])  13.7 us
    ppermute x4, waiting for transfers between devices, swap_y(): return lax.ppermute(value, 'col', [(i, i ^ 4 * j) for i in range(16)])  6.97 us
    ppermute x2, starting transfers between devices, swap_row(): return lax.ppermute(value, 'row', [(i, i ^ j) for i in range(4)])  4.43 us
  transfers between devices with their start and end apart: 11, of which 6 were waited for; matrix products, arithmetic and copies ran while one was open for 2% of the time, Pallas kernels for 1%

profile of v4, /device:TPU:8, one launch (start us, length us, event | category | flops | bytes accessed | tf_op | source)
XLA Modules:
  0.0 164.4 jit_solution(12981199147841504568)
XLA Ops:
  8.7 0.8 slice.76
  9.5 47.3 %all_gather.10.grad_hi = bf16[768,512]{1,0:T(8,128)(2,1)S(1)} all-gather(bf16[48,512]{1,0:T(8,128)(2,1)S(1)} %slice.77), channel_id=1, replica_groups=mesh['row'=4,'col'=16,'depth'=16] {'depth'}, dimensions={0}, use_global_device_ids=true | all-gather | bytes 835584 | tf_op jit(solution)/shard_map/all_gather | solution.py:75
  56.9 31.7 %all_gather.9.grad_lo = bf16[768,640]{1,0:T(8,128)(2,1)S(1)} all-gather(bf16[48,640]{1,0:T(8,128)(2,1)S(1)} %slice.76), channel_id=1, replica_groups=mesh['row'=4,'col'=16,'depth'=16] {'depth'}, dimensions={0}, use_global_device_ids=true | all-gather | bytes 1044480 | tf_op jit(solution)/shard_map/all_gather | solution.py:75
  88.6 2.1 %grad_inputs.1 = (f32[384,384]{1,0:T(8,128)S(1)}, f32[384,384]{1,0:T(8,128)S(1)}, f32[384,384]{1,0:T(8,128)S(1)}, f32[384,384]{1,0:T(8,128)S(1)}, f32[8,128]{1,0:T(8,128)S(1)}) custom-call(s32[1]{0:T(128)} %bitcast.col_ref, bf16[768,640]{1,0:T(8,128)(2,1)S(1)} %all_gather.9.grad_lo, bf16[768,512]{1,0:T(8,128)(2,1)S(1)} %all_gather.10.grad_hi, ...), custom_call_target="tpu_custom_call" | custom-call | flops 1358954496 | bytes 6291456 | tf_op jit(solution)/shard_map/grad_inputs/pallas_call | solution.py:81
  90.7 0.8 copy-done.2
  91.5 1.3 copy-done.1
  92.8 2.0 %grad_weight.1 = (f32[384,1152]{1,0:T(8,128)S(1)}, f32[384,1152]{1,0:T(8,128)S(1)}) custom-call(s32[1]{0:T(128)} %bitcast.1.row_ref, f32[8,128]{1,0:T(8,128)S(1)} %get-tuple-element.17._, bf16[768,640]{1,0:T(8,128)(2,1)S(1)} %all_gather.9.grad_lo, bf16[768,512]{1,0:T(8,128)(2,1)S(1)} %all_gather.10.grad_hi, bf16[768,768]{1,0:T(8,128)(2,1)S(1)} %copy-done.1), custom_call_target="tpu_custom_call" | custom-call | flops 1358954496 | bytes 7340032 | tf_op jit(solution)/shard_map/grad_weight/pallas_call | solution.py:96
  94.8 1.9 %collective-permute-start.2 = (f32[384,1152]{1,0:T(8,128)S(1)}, f32[384,1152]{1,0:T(8,128)S(1)}, u32[]{:S(2)}, u32[]{:S(2)}) collective-permute-start(f32[384,1152]{1,0:T(8,128)S(1)} %get-tuple-element.19), channel_id=1, source_target_pairs={{0,256},{256,0},{512,768},{768,512},{1,257},{257,1},{513,769},{769... | collective-permute-start | bytes 5308424 | tf_op jit(solution)/shard_map/ppermute | solution.py:24
  96.7 3.6 %collective-permute-start = (f32[384,384]{1,0:T(8,128)S(1)}, f32[384,384]{1,0:T(8,128)S(1)}, u32[]{:S(2)}, u32[]{:S(2)}) collective-permute-start(f32[384,384]{1,0:T(8,128)S(1)} %copy-done.3), channel_id=1, source_target_pairs={{0,16},{16,0},{32,48},{48,32},{64,80},{80,64},{96,112},{112,96},{1... | collective-permute-start | bytes 1769480 | tf_op jit(solution)/shard_map/ppermute | solution.py:16
  100.4 4.1 %collective-permute-start.1 = (f32[384,384]{1,0:T(8,128)S(1)}, f32[384,384]{1,0:T(8,128)S(1)}, u32[]{:S(2)}, u32[]{:S(2)}) collective-permute-start(f32[384,384]{1,0:T(8,128)S(1)} %get-tuple-element.16), channel_id=1, source_target_pairs={{0,48},{16,32},{32,16},{48,0},{64,112},{80,96},{96,80},{112,64},{1... | collective-permute-start | bytes 1769480 | tf_op jit(solution)/shard_map/ppermute | solution.py:16
  104.6 2.5 %collective-permute-start.5 = (f32[192,1152]{1,0:T(8,128)S(1)}, f32[192,1152]{1,0:T(8,128)S(1)}, u32[]{:S(2)}, u32[]{:S(2)}) collective-permute-start(f32[192,1152]{1,0:T(8,128)S(1)} %slice_add_fusion.1), channel_id=1, source_target_pairs={{0,512},{256,768},{512,0},{768,256},{1,513},{257,769},{513,1},{769... | collective-permute-start | bytes 2654216 | tf_op jit(solution)/shard_map/ppermute | solution.py:24
  107.1 7.3 %collective-permute-done = f32[384,384]{1,0:T(8,128)S(1)} collective-permute-done((f32[384,384]{1,0:T(8,128)S(1)}, f32[384,384]{1,0:T(8,128)S(1)}, u32[]{:S(2)}, u32[]{:S(2)}) %collective-permute-start) | collective-permute-done | bytes 589856 | tf_op jit(solution)/shard_map/ppermute | solution.py:16
  114.4 4.6 %collective-permute-done.1 = f32[384,384]{1,0:T(8,128)S(1)} collective-permute-done((f32[384,384]{1,0:T(8,128)S(1)}, f32[384,384]{1,0:T(8,128)S(1)}, u32[]{:S(2)}, u32[]{:S(2)}) %collective-permute-start.1) | collective-permute-done | bytes 589856 | tf_op jit(solution)/shard_map/ppermute | solution.py:16
  119.1 4.1 %collective-permute-start.3 = (f32[192,384]{1,0:T(8,128)S(1)}, f32[192,384]{1,0:T(8,128)S(1)}, u32[]{:S(2)}, u32[]{:S(2)}) collective-permute-start(f32[192,384]{1,0:T(8,128)S(1)} %slice.102), channel_id=1, source_target_pairs={{0,48},{16,32},{32,16},{48,0},{64,112},{80,96},{96,80},{112,64},{1... | collective-permute-start | bytes 884744 | tf_op jit(solution)/shard_map/ppermute | solution.py:16
  123.2 1.9 %collective-permute-start.4 = (f32[192,384]{1,0:T(8,128)S(1)}, f32[192,384]{1,0:T(8,128)S(1)}, u32[]{:S(2)}, u32[]{:S(2)}) collective-permute-start(f32[192,384]{1,0:T(8,128)S(1)} %slice.103), channel_id=1, source_target_pairs={{0,16},{16,0},{32,48},{48,32},{64,80},{80,64},{96,112},{112,96},{1... | collective-permute-start | bytes 884744 | tf_op jit(solution)/shard_map/ppermute | solution.py:16
  125.2 5.4 %collective-permute-done.3 = f32[192,384]{1,0:T(8,128)S(1)} collective-permute-done((f32[192,384]{1,0:T(8,128)S(1)}, f32[192,384]{1,0:T(8,128)S(1)}, u32[]{:S(2)}, u32[]{:S(2)}) %collective-permute-start.3) | collective-permute-done | bytes 294944 | tf_op jit(solution)/shard_map/ppermute | solution.py:16
  130.6 2.6 %collective-permute-done.4 = f32[192,384]{1,0:T(8,128)S(1)} collective-permute-done((f32[192,384]{1,0:T(8,128)S(1)}, f32[192,384]{1,0:T(8,128)S(1)}, u32[]{:S(2)}, u32[]{:S(2)}) %collective-permute-start.4) | collective-permute-done | bytes 294944 | tf_op jit(solution)/shard_map/ppermute | solution.py:16
  133.3 4.0 %collective-permute-start.6 = (f32[2,48,384]{2,1,0:T(8,128)S(1)}, f32[2,48,384]{2,1,0:T(8,128)S(1)}, u32[]{:S(2)}, u32[]{:S(2)}) collective-permute-start(f32[2,48,384]{2,1,0:T(8,128)S(1)} %pad_maximum_fusion), channel_id=1, source_target_pairs={{0,64},{16,80},{32,96},{48,112},{64,0},{80,16},{96,32},{112,48},{1... | collective-permute-start | bytes 442376 | tf_op jit(solution)/shard_map/ppermute | solution.py:20
  137.3 4.1 %collective-permute-start.8 = (f32[2,48,384]{2,1,0:T(8,128)S(1)}, f32[2,48,384]{2,1,0:T(8,128)S(1)}, u32[]{:S(2)}, u32[]{:S(2)}) collective-permute-start(f32[2,48,384]{2,1,0:T(8,128)S(1)} %bitcast.31), channel_id=1, source_target_pairs={{0,192},{16,208},{32,224},{48,240},{64,128},{80,144},{96,160},{112... | collective-permute-start | bytes 442376 | tf_op jit(solution)/shard_map/ppermute | solution.py:20
  141.5 0.9 fusion.1
  142.4 5.6 %collective-permute-start.7 = (f32[48,384]{1,0:T(8,128)S(1)}, f32[48,384]{1,0:T(8,128)S(1)}, u32[]{:S(2)}, u32[]{:S(2)}) collective-permute-start(f32[48,384]{1,0:T(8,128)S(1)} %fusion.6), channel_id=1, source_target_pairs={{0,192},{16,208},{32,224},{48,240},{64,128},{80,144},{96,160},{112... | collective-permute-start | bytes 221192 | tf_op jit(solution)/shard_map/ppermute | solution.py:20
  148.0 1.8 %collective-permute-done.8 = f32[2,48,384]{2,1,0:T(8,128)S(1)} collective-permute-done((f32[2,48,384]{2,1,0:T(8,128)S(1)}, f32[2,48,384]{2,1,0:T(8,128)S(1)}, u32[]{:S(2)}, u32[]{:S(2)}) %collective-permute-start.8) | collective-permute-done | bytes 147488 | tf_op jit(solution)/shard_map/ppermute | solution.py:20
  149.8 1.9 %collective-permute-start.9 = (f32[48,384]{1,0:T(8,128)S(1)}, f32[48,384]{1,0:T(8,128)S(1)}, u32[]{:S(2)}, u32[]{:S(2)}) collective-permute-start(f32[48,384]{1,0:T(8,128)S(1)} %fusion.2), channel_id=1, source_target_pairs={{0,64},{16,80},{32,96},{48,112},{64,0},{80,16},{96,32},{112,48},{1... | collective-permute-start | bytes 221192 | tf_op jit(solution)/shard_map/ppermute | solution.py:20
  151.7 5.2 %collective-permute-done.9 = f32[48,384]{1,0:T(8,128)S(1)} collective-permute-done((f32[48,384]{1,0:T(8,128)S(1)}, f32[48,384]{1,0:T(8,128)S(1)}, u32[]{:S(2)}, u32[]{:S(2)}) %collective-permute-start.9) | collective-permute-done | bytes 73760 | tf_op jit(solution)/shard_map/ppermute | solution.py:20
  (29 shorter events, 2.6 us)
Async XLA Ops:
  7.2 84.4 %all-gather.2.cloned.1.call-start = ((), (), s32[]{:S(2)}) async-start(), calls=%async_computation | async-start | bytes 1253376 | tf_op jit(solution)/shard_map/all_gather | solution.py:78
  9.5 79.0 %copy-start = (bf16[768,1152]{1,0:T(8,128)(2,1)S(1)}, bf16[768,1152]{1,0:T(8,128)(2,1)}, u32[]{:S(2)}) copy-start(bf16[768,1152]{1,0:T(8,128)(2,1)} %weight_ref.1) | copy-start | bytes 5308420
  90.7 0.8 copy-start.2
  91.5 1.3 copy-start.1
  92.8 3.9 %copy-start.3 = (f32[384,384]{1,0:T(8,128)S(1)}, f32[384,384]{1,0:T(8,128)}, u32[]{:S(2)}) copy-start(f32[384,384]{1,0:T(8,128)} %copy-done.2) | copy-start | bytes 1769476
  94.8 9.7 %collective-permute-start.2 = (f32[384,1152]{1,0:T(8,128)S(1)}, f32[384,1152]{1,0:T(8,128)S(1)}, u32[]{:S(2)}, u32[]{:S(2)}) collective-permute-start(f32[384,1152]{1,0:T(8,128)S(1)} %get-tuple-element.19), channel_id=1, source_target_pairs={{0,256},{256,0},{512,768},{768,512},{1,257},{257,1},{513,769},{769... | collective-permute-start | bytes 5308424 | tf_op jit(solution)/shard_map/ppermute | solution.py:24
  96.7 17.6 %collective-permute-start = (f32[384,384]{1,0:T(8,128)S(1)}, f32[384,384]{1,0:T(8,128)S(1)}, u32[]{:S(2)}, u32[]{:S(2)}) collective-permute-start(f32[384,384]{1,0:T(8,128)S(1)} %copy-done.3), channel_id=1, source_target_pairs={{0,16},{16,0},{32,48},{48,32},{64,80},{80,64},{96,112},{112,96},{1... | collective-permute-start | bytes 1769480 | tf_op jit(solution)/shard_map/ppermute | solution.py:16
  100.4 18.6 %collective-permute-start.1 = (f32[384,384]{1,0:T(8,128)S(1)}, f32[384,384]{1,0:T(8,128)S(1)}, u32[]{:S(2)}, u32[]{:S(2)}) collective-permute-start(f32[384,384]{1,0:T(8,128)S(1)} %get-tuple-element.16), channel_id=1, source_target_pairs={{0,48},{16,32},{32,16},{48,0},{64,112},{80,96},{96,80},{112,64},{1... | collective-permute-start | bytes 1769480 | tf_op jit(solution)/shard_map/ppermute | solution.py:16
  104.6 28.6 %collective-permute-start.5 = (f32[192,1152]{1,0:T(8,128)S(1)}, f32[192,1152]{1,0:T(8,128)S(1)}, u32[]{:S(2)}, u32[]{:S(2)}) collective-permute-start(f32[192,1152]{1,0:T(8,128)S(1)} %slice_add_fusion.1), channel_id=1, source_target_pairs={{0,512},{256,768},{512,0},{768,256},{1,513},{257,769},{513,1},{769... | collective-permute-start | bytes 2654216 | tf_op jit(solution)/shard_map/ppermute | solution.py:24
  119.1 11.4 %collective-permute-start.3 = (f32[192,384]{1,0:T(8,128)S(1)}, f32[192,384]{1,0:T(8,128)S(1)}, u32[]{:S(2)}, u32[]{:S(2)}) collective-permute-start(f32[192,384]{1,0:T(8,128)S(1)} %slice.102), channel_id=1, source_target_pairs={{0,48},{16,32},{32,16},{48,0},{64,112},{80,96},{96,80},{112,64},{1... | collective-permute-start | bytes 884744 | tf_op jit(solution)/shard_map/ppermute | solution.py:16
  123.2 9.9 %collective-permute-start.4 = (f32[192,384]{1,0:T(8,128)S(1)}, f32[192,384]{1,0:T(8,128)S(1)}, u32[]{:S(2)}, u32[]{:S(2)}) collective-permute-start(f32[192,384]{1,0:T(8,128)S(1)} %slice.103), channel_id=1, source_target_pairs={{0,16},{16,0},{32,48},{48,32},{64,80},{80,64},{96,112},{112,96},{1... | collective-permute-start | bytes 884744 | tf_op jit(solution)/shard_map/ppermute | solution.py:16
  133.3 9.0 %collective-permute-start.6 = (f32[2,48,384]{2,1,0:T(8,128)S(1)}, f32[2,48,384]{2,1,0:T(8,128)S(1)}, u32[]{:S(2)}, u32[]{:S(2)}) collective-permute-start(f32[2,48,384]{2,1,0:T(8,128)S(1)} %pad_maximum_fusion), channel_id=1, source_target_pairs={{0,64},{16,80},{32,96},{48,112},{64,0},{80,16},{96,32},{112,48},{1... | collective-permute-start | bytes 442376 | tf_op jit(solution)/shard_map/ppermute | solution.py:20
  137.3 12.4 %collective-permute-start.8 = (f32[2,48,384]{2,1,0:T(8,128)S(1)}, f32[2,48,384]{2,1,0:T(8,128)S(1)}, u32[]{:S(2)}, u32[]{:S(2)}) collective-permute-start(f32[2,48,384]{2,1,0:T(8,128)S(1)} %bitcast.31), channel_id=1, source_target_pairs={{0,192},{16,208},{32,224},{48,240},{64,128},{80,144},{96,160},{112... | collective-permute-start | bytes 442376 | tf_op jit(solution)/shard_map/ppermute | solution.py:20
  142.4 9.3 %collective-permute-start.7 = (f32[48,384]{1,0:T(8,128)S(1)}, f32[48,384]{1,0:T(8,128)S(1)}, u32[]{:S(2)}, u32[]{:S(2)}) collective-permute-start(f32[48,384]{1,0:T(8,128)S(1)} %fusion.6), channel_id=1, source_target_pairs={{0,192},{16,208},{32,224},{48,240},{64,128},{80,144},{96,160},{112... | collective-permute-start | bytes 221192 | tf_op jit(solution)/shard_map/ppermute | solution.py:20
  149.8 7.1 %collective-permute-start.9 = (f32[48,384]{1,0:T(8,128)S(1)}, f32[48,384]{1,0:T(8,128)S(1)}, u32[]{:S(2)}, u32[]{:S(2)}) collective-permute-start(f32[48,384]{1,0:T(8,128)S(1)} %fusion.2), channel_id=1, source_target_pairs={{0,64},{16,80},{32,96},{48,112},{64,0},{80,16},{96,32},{112,48},{1... | collective-permute-start | bytes 221192 | tf_op jit(solution)/shard_map/ppermute | solution.py:20
Sparse Core Ops, SparseCore 0:
  12.2 76.7 all-gather.1

commit v5 on v3

v5 whole, which is shorter than its diff:
```python
import jax
import jax.numpy as jnp
from jax import lax
from jax.experimental import pallas as pl
from jax.experimental.pallas import tpu as pltpu
from jax.sharding import PartitionSpec as P

F32 = jnp.float32
BF16 = jnp.bfloat16
VMEM = pl.BlockSpec(memory_space=pltpu.VMEM)
SMEM = pl.BlockSpec(memory_space=pltpu.SMEM)
ORDER = (0, 1, 3, 2)


def swap_x(value, j):
    return lax.ppermute(value, "col", [(i, i ^ j) for i in range(16)])


def swap_y(value, j):
    return lax.ppermute(value, "col", [(i, i ^ (4 * j)) for i in range(16)])


def swap_row(value, j):
    return lax.ppermute(value, "row", [(i, i ^ j) for i in range(4)])


def spread(depth, chunks, block, into, place):
    parity = jnp.bitwise_and(depth, 1)
    for ref, own, lead in zip(chunks, (1, 0, 0), (0, 0, ref_blocks(chunks[1], block))):
        for k in range(ref_blocks(ref, block)):
            source = 2 * (lead + k) + (parity if own else 1 - parity)
            at = pl.multiple_of(place(source) * block, block)
            into[pl.ds(at, block), :] = ref[pl.ds(k * block, block), :]


def ref_blocks(ref, block):
    return ref.shape[0] // block


def grad_inputs_kernel(place_ref, own, near, far, weight_ref, send_a, send_b, keep_a, keep_b, rows):
    block = own.shape[0] // 8
    half = weight_ref.shape[0] // 2

    def place(source):
        j = jnp.bitwise_xor(source, place_ref[1])
        jx, jy = jnp.bitwise_and(j, 3), jnp.right_shift(j, 2)
        return jx * 4 + jnp.bitwise_xor(jy, jnp.right_shift(jy, 1))

    spread(place_ref[0], (own, near, far), block, rows, place)
    quarter = 4 * block
    for out_half, (sent, kept, sends, keeps) in enumerate(
        ((send_a, keep_a, (1, 2), (0, 3)), (send_b, keep_b, (3, 2), (0, 1)))
    ):
        part = lax.dot_general(
            rows[...],
            weight_ref[pl.ds(out_half * half, half), :],
            (((1,), (1,)), ((), ())),
            preferred_element_type=F32,
        )
        for ref, order in ((sent, sends), (kept, keeps)):
            for slot, jx in enumerate(order):
                ref[pl.ds(slot * quarter, quarter), :] = part[jx * quarter : (jx + 1) * quarter]


def grad_weight_kernel(place_ref, _a, _b, own, near, far, tokens, sent, kept, grads, total):
    spread(place_ref[0], (own, near, far), own.shape[0] // 8, grads, lambda source: source)
    total[...] = lax.dot_general(
        tokens[...], grads[...], (((0,), (0,)), ((), ())), preferred_element_type=F32
    )
    rows = total.shape[0] // 4
    for jy in range(2):
        for jc, ref in ((1, sent), (0, kept)):
            source = jnp.bitwise_xor(place_ref[1], jy * 2 + jc) * rows
            ref[pl.ds(jy * rows, rows), :] = total[pl.ds(pl.multiple_of(source, rows), rows), :]


def after(*values):
    return lax.optimization_barrier(values)


def per_device(inputs, weight, grad_out):
    block, width = inputs.shape
    columns = weight.shape[1]
    tokens = block * 16
    depth, col, row = (lax.axis_index(a) for a in ("depth", "col", "row"))
    own = lax.all_gather(
        grad_out,
        "depth",
        axis=0,
        tiled=True,
        axis_index_groups=[list(range(parity, 16, 2)) for parity in range(2)],
    )
    near = lax.ppermute(own[: tokens // 4], "depth", [(i, i ^ 1) for i in range(16)])
    far = lax.ppermute(own[tokens // 4 :], "depth", [(i, ((i + 1) ^ 1) - 1 & 15) for i in range(16)])
    grads = (own, near, far)
    gathered = lax.all_gather(inputs, "col", axis=0, tiled=True)

    piece = jax.ShapeDtypeStruct((tokens // 2, width // 2), F32)
    send_a, send_b, keep_a, keep_b = pl.pallas_call(
        grad_inputs_kernel,
        out_shape=[piece] * 4,
        in_specs=[SMEM] + [VMEM] * 4,
        out_specs=[VMEM] * 4,
        scratch_shapes=[pltpu.VMEM((tokens, columns), BF16)],
        compiler_params=pltpu.CompilerParams(vmem_limit_bytes=12 << 20),
        cost_estimate=pl.CostEstimate(
            flops=2 * tokens * width * columns, bytes_accessed=6 << 20, transcendentals=0
        ),
        name="grad_inputs",
    )(jnp.stack([depth, col]), *grads, weight)
    got_a, got_b = swap_x(send_a, 1), swap_x(send_b, 3)

    quarter = tokens // 4
    sum_a, sum_b = keep_a + got_a, keep_b + got_b
    got_a, got_b = swap_x(sum_a[quarter:], 3), swap_x(sum_b[quarter:], 1)

    half = jax.ShapeDtypeStruct((width // 2, columns), F32)
    send_w, keep_w = pl.pallas_call(
        grad_weight_kernel,
        out_shape=[half] * 2,
        in_specs=[SMEM] + [pl.BlockSpec(memory_space=pl.ANY)] * 2 + [VMEM] * 4,
        out_specs=[VMEM] * 2,
        scratch_shapes=[pltpu.VMEM((tokens, columns), BF16), pltpu.VMEM((width, columns), F32)],
        compiler_params=pltpu.CompilerParams(vmem_limit_bytes=16 << 20),
        cost_estimate=pl.CostEstimate(
            flops=2 * tokens * width * columns, bytes_accessed=7 << 20, transcendentals=0
        ),
        name="grad_weight",
    )(jnp.stack([depth, row]), got_a, got_b, *grads, gathered)

    rows = width // 4
    got_w = swap_row(send_w, 1)
    sum_w = keep_w[rows:] + got_w[rows:]
    got_w2 = swap_row(sum_w, 2)

    sum_a = (sum_a[:quarter] + got_a).reshape(4, block, width // 2)
    sum_b = (sum_b[:quarter] + got_b).reshape(4, block, width // 2)
    got_a = swap_y(jnp.concatenate([sum_a[1:2], sum_a[3:4]]), 1)
    got_b = swap_y(sum_b[2:4], 3)
    sum_a0, sum_a3 = sum_a[0] + got_a[0], sum_a[2] + got_a[1]
    sum_b0, sum_b1 = sum_b[0] + got_b[0], sum_b[1] + got_b[1]
    got_a, got_b = swap_y(sum_a3, 3), swap_y(sum_b1, 1)
    grad_inputs = jnp.concatenate([sum_a0 + got_a, sum_b0 + got_b], axis=1)
    grad_weight = keep_w[:rows] + got_w[:rows] + got_w2
    return grad_inputs.astype(BF16), grad_weight.astype(BF16)


def solution(mesh):
    placed = (P(("row", "col"), "depth"), P("depth", "col"), P(("row", "depth"), "col"))
    return jax.shard_map(
        per_device,
        mesh=mesh,
        in_specs=placed,
        out_specs=(P(("row", "col"), "depth"), P(("depth", "row"), "col")),
        check_vma=False,
    )
```

time: 256 us -> 160 us (0.62)
  blocking collectives: 149 us -> 42 us
  between operations: 0.84 us -> 14.2 us
  waiting for transfers between devices: 36.8 us -> 42.2 us
    all_gather x4 -> x1, blocking collectives: 149 us -> 42 us  [per_device(): lax.all_gather(grad_out, 'depth', axis=0, tiled=True, axis_index_groups=[...]
    ppermute x2, starting transfers between devices: 31 us -> 15.4 us  [swap_row(): return lax.ppermute(value, 'row', [(i, i ^ j) for i in range(4)])]
    ppermute x0 -> x2, waiting for transfers between devices: none -> 7.38 us  [the longest x1 4.15 us: per_device(): lax.ppermute(own[tokens // 4:], 'depth', [(i, (i + 1 ^ 1) - 1 & 15) for i...]
    ppermute x4, starting transfers between devices: 11.1 us -> 17.3 us  [swap_y(): return lax.ppermute(value, 'col', [(i, i ^ 4 * j) for i in range(16)])]
    ppermute x0 -> x2, starting transfers between devices: none -> 5.92 us  [the longest x1 3 us: per_device(): lax.ppermute(own[tokens // 4:], 'depth', [(i, (i + 1 ^ 1) - 1 & 15) for i...]
    ppermute x4, waiting for transfers between devices: 19.9 us -> 16.5 us  [swap_x(): return lax.ppermute(value, 'col', [(i, i ^ j) for i in range(16)])]
  transfers between devices with their start and end apart: 10 -> 13, of which waited for: 7 -> 9; matrix products, arithmetic and copies ran while one was open for 1% -> 2% of each run, Pallas kernels for 1% -> 2%
where the time goes in v5:
time: 160 us; the launch traced here: 159 us
  starting transfers between devices  49.5 us (31%)
  waiting for transfers between devices  42.2 us (26%)
  blocking collectives  42 us (26%)
  between operations  14.2 us (9%)
  Pallas kernels  5.35 us (3%)
  local copies, waits for them, and re-layouts  3.85 us (2%)
  other arithmetic  2.15 us (1%)
    all_gather x1, blocking collectives, per_device(): lax.all_gather(grad_out, 'depth', axis=0, tiled=True, axis_index_groups=[...  42 us
    ppermute x4, waiting for transfers between devices, swap_y(): return lax.ppermute(value, 'col', [(i, i ^ 4 * j) for i in range(16)])  17.6 us
    ppermute x4, starting transfers between devices, swap_y(): return lax.ppermute(value, 'col', [(i, i ^ 4 * j) for i in range(16)])  17.3 us
    ppermute x4, waiting for transfers between devices, swap_x(): return lax.ppermute(value, 'col', [(i, i ^ j) for i in range(16)])  16.5 us
    ppermute x2, starting transfers between devices, swap_row(): return lax.ppermute(value, 'row', [(i, i ^ j) for i in range(4)])  15.4 us
    ppermute x4, starting transfers between devices, swap_x(): return lax.ppermute(value, 'col', [(i, i ^ j) for i in range(16)])  10.8 us
    ppermute x1, waiting for transfers between devices, per_device(): lax.ppermute(own[tokens // 4:], 'depth', [(i, (i + 1 ^ 1) - 1 & 15) for i...  4.15 us
    ppermute x1, waiting for transfers between devices, per_device(): lax.ppermute(own[:tokens // 4], 'depth', [(i, i ^ 1) for i in range(16)])  3.23 us
  transfers between devices with their start and end apart: 13, of which 9 were waited for; matrix products, arithmetic and copies ran while one was open for 2% of the time, Pallas kernels for 2%

profile of v5, /device:TPU:1, one launch (start us, length us, event | category | flops | bytes accessed | tf_op | source)
XLA Modules:
  0.0 159.2 jit_solution(1880052984166460174)
XLA Ops:
  7.9 42.0 %all_gather.6.own = bf16[384,1152]{1,0:T(8,128)(2,1)S(1)} all-gather(bf16[48,1152]{1,0:T(8,128)(2,1)} %param.5), channel_id=1, replica_groups={{0,2,4,6,8,10,12,14},{1,3,5,7,9,11,13,15},{16,18,20,22,24,26,28,30},{17..., dimensions={0}, use_global_device_ids=true | all-gather | bytes 995328 | tf_op jit(solution)/shard_map/all_gather | solution.py:86
  49.9 1.0 fusion.10
  50.9 2.9 %collective-permute-start = (bf16[192,1152]{1,0:T(8,128)(2,1)}, bf16[192,1152]{1,0:T(8,128)(2,1)S(1)}, u32[]{:S(2)}, u32[]{:S(2)}) collective-permute-start(bf16[192,1152]{1,0:T(8,128)(2,1)} %get-tuple-element.15), channel_id=1, source_target_pairs={{0,1},{1,0},{2,3},{3,2},{4,5},{5,4},{6,7},{7,6},{8,9},{9,8},{10,11... | collective-permute-start | bytes 1327112 | tf_op jit(solution)/shard_map/ppermute | solution.py:93
  53.8 3.0 %collective-permute-start.1 = (bf16[192,1152]{1,0:T(8,128)(2,1)}, bf16[192,1152]{1,0:T(8,128)(2,1)S(1)}, u32[]{:S(2)}, u32[]{:S(2)}) collective-permute-start(bf16[192,1152]{1,0:T(8,128)(2,1)} %get-tuple-element.14), channel_id=1, source_target_pairs={{0,15},{1,2},{2,1},{3,4},{4,3},{5,6},{6,5},{7,8},{8,7},{9,10},{10,... | collective-permute-start | bytes 1327112 | tf_op jit(solution)/shard_map/ppermute | solution.py:94
  56.9 3.2 %collective-permute-done.near = bf16[192,1152]{1,0:T(8,128)(2,1)S(1)} collective-permute-done((bf16[192,1152]{1,0:T(8,128)(2,1)}, bf16[192,1152]{1,0:T(8,128)(2,1)S(1)}, u32[]{:S(2)}, u32[]{:S(2)}) %collective-permute-start) | collective-permute-done | bytes 442400 | tf_op jit(solution)/shard_map/ppermute | solution.py:93
  60.1 4.1 %collective-permute-done.1.far = bf16[192,1152]{1,0:T(8,128)(2,1)S(1)} collective-permute-done((bf16[192,1152]{1,0:T(8,128)(2,1)}, bf16[192,1152]{1,0:T(8,128)(2,1)S(1)}, u32[]{:S(2)}, u32[]{:S(2)}) %collective-permute-start.1) | collective-permute-done | bytes 442400 | tf_op jit(solution)/shard_map/ppermute | solution.py:94
  64.3 2.7 %grad_inputs.1 = (f32[384,384]{1,0:T(8,128)S(1)}, f32[384,384]{1,0:T(8,128)S(1)}, f32[384,384]{1,0:T(8,128)S(1)}, f32[384,384]{1,0:T(8,128)S(1)}) custom-call(s32[2]{0:T(128)S(1)} %pad_add_fusion.place_ref, bf16[384,1152]{1,0:T(8,128)(2,1)S(1)} %all_gather.6.own, bf16[192,1152]{1,0:T(8,128)(2,1)S(1)} %collective-permute-done.near, ...), custom_call_target="tpu_custom_call" | custom-call | flops 1358954496 | bytes 6291456 | tf_op jit(solution)/shard_map/grad_inputs/pallas_call | solution.py:99
  67.0 3.3 %collective-permute-start.6 = (f32[384,384]{1,0:T(8,128)S(1)}, f32[384,384]{1,0:T(8,128)S(1)}, u32[]{:S(2)}, u32[]{:S(2)}) collective-permute-start(f32[384,384]{1,0:T(8,128)S(1)} %get-tuple-element.11), channel_id=1, source_target_pairs={{0,48},{16,32},{32,16},{48,0},{64,112},{80,96},{96,80},{112,64},{1... | collective-permute-start | bytes 1769480 | tf_op jit(solution)/shard_map/ppermute | solution.py:16
  70.3 1.9 %collective-permute-start.2 = (f32[384,384]{1,0:T(8,128)S(1)}, f32[384,384]{1,0:T(8,128)S(1)}, u32[]{:S(2)}, u32[]{:S(2)}) collective-permute-start(f32[384,384]{1,0:T(8,128)S(1)} %get-tuple-element.9), channel_id=1, source_target_pairs={{0,16},{16,0},{32,48},{48,32},{64,80},{80,64},{96,112},{112,96},{1... | collective-permute-start | bytes 1769480 | tf_op jit(solution)/shard_map/ppermute | solution.py:16
  72.2 9.3 %collective-permute-done.6 = f32[384,384]{1,0:T(8,128)S(1)} collective-permute-done((f32[384,384]{1,0:T(8,128)S(1)}, f32[384,384]{1,0:T(8,128)S(1)}, u32[]{:S(2)}, u32[]{:S(2)}) %collective-permute-start.6) | collective-permute-done | bytes 589856 | tf_op jit(solution)/shard_map/ppermute | solution.py:16
  81.6 1.9 %collective-permute-start.7 = (f32[192,384]{1,0:T(8,128)S(1)}, f32[192,384]{1,0:T(8,128)S(1)}, u32[]{:S(2)}, u32[]{:S(2)}) collective-permute-start(f32[192,384]{1,0:T(8,128)S(1)} %slice.111), channel_id=1, source_target_pairs={{0,16},{16,0},{32,48},{48,32},{64,80},{80,64},{96,112},{112,96},{1... | collective-permute-start | bytes 884744 | tf_op jit(solution)/shard_map/ppermute | solution.py:16
  83.5 2.1 %collective-permute-done.2 = f32[384,384]{1,0:T(8,128)S(1)} collective-permute-done((f32[384,384]{1,0:T(8,128)S(1)}, f32[384,384]{1,0:T(8,128)S(1)}, u32[]{:S(2)}, u32[]{:S(2)}) %collective-permute-start.2) | collective-permute-done | bytes 589856 | tf_op jit(solution)/shard_map/ppermute | solution.py:16
  87.2 3.7 %collective-permute-start.3 = (f32[192,384]{1,0:T(8,128)}, f32[192,384]{1,0:T(8,128)S(1)}, u32[]{:S(2)}, u32[]{:S(2)}) collective-permute-start(f32[192,384]{1,0:T(8,128)} %slice.103), channel_id=1, source_target_pairs={{0,48},{16,32},{32,16},{48,0},{64,112},{80,96},{96,80},{112,64},{1... | collective-permute-start | bytes 884744 | tf_op jit(solution)/shard_map/ppermute | solution.py:16
  91.0 2.6 %collective-permute-done.7._b = f32[192,384]{1,0:T(8,128)S(1)} collective-permute-done((f32[192,384]{1,0:T(8,128)S(1)}, f32[192,384]{1,0:T(8,128)S(1)}, u32[]{:S(2)}, u32[]{:S(2)}) %collective-permute-start.7) | collective-permute-done | bytes 294944 | tf_op jit(solution)/shard_map/ppermute | solution.py:16
  93.6 2.5 %collective-permute-done.3._a = f32[192,384]{1,0:T(8,128)S(1)} collective-permute-done((f32[192,384]{1,0:T(8,128)}, f32[192,384]{1,0:T(8,128)S(1)}, u32[]{:S(2)}, u32[]{:S(2)}) %collective-permute-start.3) | collective-permute-done | bytes 294944 | tf_op jit(solution)/shard_map/ppermute | solution.py:16
  96.1 1.3 copy-done.1
  97.4 2.6 %grad_weight.1 = (f32[384,1152]{1,0:T(8,128)S(1)}, f32[384,1152]{1,0:T(8,128)S(1)}) custom-call(s32[2]{0:T(128)S(1)} %pad_add_fusion.1.place_ref, f32[192,384]{1,0:T(8,128)S(1)} %collective-permute-done.3._a, f32[192,384]{1,0:T(8,128)S(1)} %collective-permute-done.7._b, bf16[384,1152]{1,0:T(8,128)(2,1)S(1)} %all_gather.6.own, ...), custom_call_target="tpu_custom_call" | custom-call | flops 1358954496 | bytes 7340032 | tf_op jit(solution)/shard_map/grad_weight/pallas_call | solution.py:118
  100.0 13.3 %collective-permute-start.10 = (f32[384,1152]{1,0:T(8,128)S(1)}, f32[384,1152]{1,0:T(8,128)S(1)}, u32[]{:S(2)}, u32[]{:S(2)}) collective-permute-start(f32[384,1152]{1,0:T(8,128)S(1)} %get-tuple-element.13), channel_id=1, source_target_pairs={{0,256},{256,0},{512,768},{768,512},{1,257},{257,1},{513,769},{769... | collective-permute-start | bytes 5308424 | tf_op jit(solution)/shard_map/ppermute | solution.py:24
  113.4 5.8 %collective-permute-start.8 = (f32[2,48,384]{2,1,0:T(8,128)S(1)}, f32[2,48,384]{2,1,0:T(8,128)S(1)}, u32[]{:S(2)}, u32[]{:S(2)}) collective-permute-start(f32[2,48,384]{2,1,0:T(8,128)S(1)} %bitcast.32), channel_id=1, source_target_pairs={{0,192},{16,208},{32,224},{48,240},{64,128},{80,144},{96,160},{112... | collective-permute-start | bytes 442376 | tf_op jit(solution)/shard_map/ppermute | solution.py:20
  119.2 4.0 %collective-permute-start.4 = (f32[2,48,384]{2,1,0:T(8,128)S(1)}, f32[2,48,384]{2,1,0:T(8,128)S(1)}, u32[]{:S(2)}, u32[]{:S(2)}) collective-permute-start(f32[2,48,384]{2,1,0:T(8,128)S(1)} %pad_maximum_fusion), channel_id=1, source_target_pairs={{0,64},{16,80},{32,96},{48,112},{64,0},{80,16},{96,32},{112,48},{1... | collective-permute-start | bytes 442376 | tf_op jit(solution)/shard_map/ppermute | solution.py:20
  123.3 2.2 %collective-permute-start.11 = (f32[192,1152]{1,0:T(8,128)S(1)}, f32[192,1152]{1,0:T(8,128)S(1)}, u32[]{:S(2)}, u32[]{:S(2)}) collective-permute-start(f32[192,1152]{1,0:T(8,128)S(1)} %slice_add_fusion), channel_id=1, source_target_pairs={{0,512},{256,768},{512,0},{768,256},{1,513},{257,769},{513,1},{769... | collective-permute-start | bytes 2654216 | tf_op jit(solution)/shard_map/ppermute | solution.py:24
  125.8 4.5 %collective-permute-start.9 = (f32[48,384]{1,0:T(8,128)S(1)}, f32[48,384]{1,0:T(8,128)S(1)}, u32[]{:S(2)}, u32[]{:S(2)}) collective-permute-start(f32[48,384]{1,0:T(8,128)S(1)} %fusion.2), channel_id=1, source_target_pairs={{0,64},{16,80},{32,96},{48,112},{64,0},{80,16},{96,32},{112,48},{1... | collective-permute-start | bytes 221192 | tf_op jit(solution)/shard_map/ppermute | solution.py:20
  130.9 3.1 %collective-permute-start.5 = (f32[48,384]{1,0:T(8,128)S(1)}, f32[48,384]{1,0:T(8,128)S(1)}, u32[]{:S(2)}, u32[]{:S(2)}) collective-permute-start(f32[48,384]{1,0:T(8,128)S(1)} %fusion.6), channel_id=1, source_target_pairs={{0,192},{16,208},{32,224},{48,240},{64,128},{80,144},{96,160},{112... | collective-permute-start | bytes 221192 | tf_op jit(solution)/shard_map/ppermute | solution.py:20
  134.0 16.7 %collective-permute-done.9 = f32[48,384]{1,0:T(8,128)S(1)} collective-permute-done((f32[48,384]{1,0:T(8,128)S(1)}, f32[48,384]{1,0:T(8,128)S(1)}, u32[]{:S(2)}, u32[]{:S(2)}) %collective-permute-start.9) | collective-permute-done | bytes 73760 | tf_op jit(solution)/shard_map/ppermute | solution.py:20
  (33 shorter events, 5.4 us)
Async XLA Ops:
  7.2 57.1 %copy-start = (bf16[768,1152]{1,0:T(8,128)(2,1)S(1)}, bf16[768,1152]{1,0:T(8,128)(2,1)}, u32[]{:S(2)}) copy-start(bf16[768,1152]{1,0:T(8,128)(2,1)} %weight_ref.1) | copy-start | bytes 5308420
  7.2 88.9 %all-gather.2.cloned.1.call-start = ((), (), s32[]{:S(2)}) async-start(), calls=%async_computation | async-start | bytes 1253376 | tf_op jit(solution)/shard_map/all_gather | solution.py:96
  50.9 9.2 %collective-permute-start = (bf16[192,1152]{1,0:T(8,128)(2,1)}, bf16[192,1152]{1,0:T(8,128)(2,1)S(1)}, u32[]{:S(2)}, u32[]{:S(2)}) collective-permute-start(bf16[192,1152]{1,0:T(8,128)(2,1)} %get-tuple-element.15), channel_id=1, source_target_pairs={{0,1},{1,0},{2,3},{3,2},{4,5},{5,4},{6,7},{7,6},{8,9},{9,8},{10,11... | collective-permute-start | bytes 1327112 | tf_op jit(solution)/shard_map/ppermute | solution.py:93
  53.8 10.5 %collective-permute-start.1 = (bf16[192,1152]{1,0:T(8,128)(2,1)}, bf16[192,1152]{1,0:T(8,128)(2,1)S(1)}, u32[]{:S(2)}, u32[]{:S(2)}) collective-permute-start(bf16[192,1152]{1,0:T(8,128)(2,1)} %get-tuple-element.14), channel_id=1, source_target_pairs={{0,15},{1,2},{2,1},{3,4},{4,3},{5,6},{6,5},{7,8},{8,7},{9,10},{10,... | collective-permute-start | bytes 1327112 | tf_op jit(solution)/shard_map/ppermute | solution.py:94
  67.0 14.5 %collective-permute-start.6 = (f32[384,384]{1,0:T(8,128)S(1)}, f32[384,384]{1,0:T(8,128)S(1)}, u32[]{:S(2)}, u32[]{:S(2)}) collective-permute-start(f32[384,384]{1,0:T(8,128)S(1)} %get-tuple-element.11), channel_id=1, source_target_pairs={{0,48},{16,32},{32,16},{48,0},{64,112},{80,96},{96,80},{112,64},{1... | collective-permute-start | bytes 1769480 | tf_op jit(solution)/shard_map/ppermute | solution.py:16
  70.3 15.3 %collective-permute-start.2 = (f32[384,384]{1,0:T(8,128)S(1)}, f32[384,384]{1,0:T(8,128)S(1)}, u32[]{:S(2)}, u32[]{:S(2)}) collective-permute-start(f32[384,384]{1,0:T(8,128)S(1)} %get-tuple-element.9), channel_id=1, source_target_pairs={{0,16},{16,0},{32,48},{48,32},{64,80},{80,64},{96,112},{112,96},{1... | collective-permute-start | bytes 1769480 | tf_op jit(solution)/shard_map/ppermute | solution.py:16
  81.6 12.0 %collective-permute-start.7 = (f32[192,384]{1,0:T(8,128)S(1)}, f32[192,384]{1,0:T(8,128)S(1)}, u32[]{:S(2)}, u32[]{:S(2)}) collective-permute-start(f32[192,384]{1,0:T(8,128)S(1)} %slice.111), channel_id=1, source_target_pairs={{0,16},{16,0},{32,48},{48,32},{64,80},{80,64},{96,112},{112,96},{1... | collective-permute-start | bytes 884744 | tf_op jit(solution)/shard_map/ppermute | solution.py:16
  85.7 0.8 copy-start.2
  87.2 8.9 %collective-permute-start.3 = (f32[192,384]{1,0:T(8,128)}, f32[192,384]{1,0:T(8,128)S(1)}, u32[]{:S(2)}, u32[]{:S(2)}) collective-permute-start(f32[192,384]{1,0:T(8,128)} %slice.103), channel_id=1, source_target_pairs={{0,48},{16,32},{32,16},{48,0},{64,112},{80,96},{96,80},{112,64},{1... | collective-permute-start | bytes 884744 | tf_op jit(solution)/shard_map/ppermute | solution.py:16
  96.1 1.3 copy-start.1
  97.4 21.7 %copy-start.3 = (f32[384,384]{1,0:T(8,128)S(1)}, f32[384,384]{1,0:T(8,128)}, u32[]{:S(2)}) copy-start(f32[384,384]{1,0:T(8,128)} %copy-done.2) | copy-start | bytes 1769476
  100.0 23.2 %collective-permute-start.10 = (f32[384,1152]{1,0:T(8,128)S(1)}, f32[384,1152]{1,0:T(8,128)S(1)}, u32[]{:S(2)}, u32[]{:S(2)}) collective-permute-start(f32[384,1152]{1,0:T(8,128)S(1)} %get-tuple-element.13), channel_id=1, source_target_pairs={{0,256},{256,0},{512,768},{768,512},{1,257},{257,1},{513,769},{769... | collective-permute-start | bytes 5308424 | tf_op jit(solution)/shard_map/ppermute | solution.py:24
  113.4 12.5 %collective-permute-start.8 = (f32[2,48,384]{2,1,0:T(8,128)S(1)}, f32[2,48,384]{2,1,0:T(8,128)S(1)}, u32[]{:S(2)}, u32[]{:S(2)}) collective-permute-start(f32[2,48,384]{2,1,0:T(8,128)S(1)} %bitcast.32), channel_id=1, source_target_pairs={{0,192},{16,208},{32,224},{48,240},{64,128},{80,144},{96,160},{112... | collective-permute-start | bytes 442376 | tf_op jit(solution)/shard_map/ppermute | solution.py:20
  119.2 11.7 %collective-permute-start.4 = (f32[2,48,384]{2,1,0:T(8,128)S(1)}, f32[2,48,384]{2,1,0:T(8,128)S(1)}, u32[]{:S(2)}, u32[]{:S(2)}) collective-permute-start(f32[2,48,384]{2,1,0:T(8,128)S(1)} %pad_maximum_fusion), channel_id=1, source_target_pairs={{0,64},{16,80},{32,96},{48,112},{64,0},{80,16},{96,32},{112,48},{1... | collective-permute-start | bytes 442376 | tf_op jit(solution)/shard_map/ppermute | solution.py:20
  123.3 28.1 %collective-permute-start.11 = (f32[192,1152]{1,0:T(8,128)S(1)}, f32[192,1152]{1,0:T(8,128)S(1)}, u32[]{:S(2)}, u32[]{:S(2)}) collective-permute-start(f32[192,1152]{1,0:T(8,128)S(1)} %slice_add_fusion), channel_id=1, source_target_pairs={{0,512},{256,768},{512,0},{768,256},{1,513},{257,769},{513,1},{769... | collective-permute-start | bytes 2654216 | tf_op jit(solution)/shard_map/ppermute | solution.py:24
  125.8 24.9 %collective-permute-start.9 = (f32[48,384]{1,0:T(8,128)S(1)}, f32[48,384]{1,0:T(8,128)S(1)}, u32[]{:S(2)}, u32[]{:S(2)}) collective-permute-start(f32[48,384]{1,0:T(8,128)S(1)} %fusion.2), channel_id=1, source_target_pairs={{0,64},{16,80},{32,96},{48,112},{64,0},{80,16},{96,32},{112,48},{1... | collective-permute-start | bytes 221192 | tf_op jit(solution)/shard_map/ppermute | solution.py:20
  130.9 19.8 %collective-permute-start.5 = (f32[48,384]{1,0:T(8,128)S(1)}, f32[48,384]{1,0:T(8,128)S(1)}, u32[]{:S(2)}, u32[]{:S(2)}) collective-permute-start(f32[48,384]{1,0:T(8,128)S(1)} %fusion.6), channel_id=1, source_target_pairs={{0,192},{16,208},{32,224},{48,240},{64,128},{80,144},{96,160},{112... | collective-permute-start | bytes 221192 | tf_op jit(solution)/shard_map/ppermute | solution.py:20
Sparse Core Ops, SparseCore 0:
  12.2 77.8 all-gather.1

commit v6 on v5

--- a/solution.py
+++ b/solution.py
@@ -102,17 +102,13 @@
         in_specs=[SMEM] + [VMEM] * 4,
         out_specs=[VMEM] * 4,
         scratch_shapes=[pltpu.VMEM((tokens, columns), BF16)],
-        compiler_params=pltpu.CompilerParams(vmem_limit_bytes=12 << 20),
+        compiler_params=pltpu.CompilerParams(vmem_limit_bytes=7 << 20),
         cost_estimate=pl.CostEstimate(
             flops=2 * tokens * width * columns, bytes_accessed=6 << 20, transcendentals=0
         ),
         name="grad_inputs",
     )(jnp.stack([depth, col]), *grads, weight)
     got_a, got_b = swap_x(send_a, 1), swap_x(send_b, 3)
-
-    quarter = tokens // 4
-    sum_a, sum_b = keep_a + got_a, keep_b + got_b
-    got_a, got_b = swap_x(sum_a[quarter:], 3), swap_x(sum_b[quarter:], 1)
 
     half = jax.ShapeDtypeStruct((width // 2, columns), F32)
     send_w, keep_w = pl.pallas_call(
@@ -121,7 +117,7 @@
         in_specs=[SMEM] + [pl.BlockSpec(memory_space=pl.ANY)] * 2 + [VMEM] * 4,
         out_specs=[VMEM] * 2,
         scratch_shapes=[pltpu.VMEM((tokens, columns), BF16), pltpu.VMEM((width, columns), F32)],
-        compiler_params=pltpu.CompilerParams(vmem_limit_bytes=16 << 20),
+        compiler_params=pltpu.CompilerParams(vmem_limit_bytes=9 << 20),
         cost_estimate=pl.CostEstimate(
             flops=2 * tokens * width * columns, bytes_accessed=7 << 20, transcendentals=0
         ),
@@ -133,12 +129,18 @@
     sum_w = keep_w[rows:] + got_w[rows:]
     got_w2 = swap_row(sum_w, 2)
 
+    quarter = tokens // 4
+    sum_a, sum_b = keep_a + got_a, keep_b + got_b
+    got_a, got_b = swap_x(sum_a[quarter:], 3), swap_x(sum_b[quarter:], 1)
+
+    got_a, got_b, sum_w = after(got_a, got_b, sum_w)
     sum_a = (sum_a[:quarter] + got_a).reshape(4, block, width // 2)
     sum_b = (sum_b[:quarter] + got_b).reshape(4, block, width // 2)
     got_a = swap_y(jnp.concatenate([sum_a[1:2], sum_a[3:4]]), 1)
     got_b = swap_y(sum_b[2:4], 3)
     sum_a0, sum_a3 = sum_a[0] + got_a[0], sum_a[2] + got_a[1]
     sum_b0, sum_b1 = sum_b[0] + got_b[0], sum_b[1] + got_b[1]
+    sum_a3, sum_b1, got_w2 = after(sum_a3, sum_b1, got_w2)
     got_a, got_b = swap_y(sum_a3, 3), swap_y(sum_b1, 1)
     grad_inputs = jnp.concatenate([sum_a0 + got_a, sum_b0 + got_b], axis=1)
     grad_weight = keep_w[:rows] + got_w[:rows] + got_w2

time: 160 us -> 157 us (0.981)
  starting transfers between devices: 49.5 us -> 41.4 us
  waiting for transfers between devices: 42.2 us -> 45.2 us
    ppermute x2, starting transfers between devices: 15.4 us -> 8.38 us  [swap_row(): return lax.ppermute(value, 'row', [(i, i ^ j) for i in range(4)])]
    all_gather x1, waiting for transfers between devices: 0.01 us -> 3.59 us  [per_device(): gathered = lax.all_gather(inputs, 'col', axis=0, tiled=True)]
    unnamed x8 -> x12, local copies, waits for them, and re-layouts: 2.09 us -> 4.78 us
    ppermute x4, waiting for transfers between devices: 17.6 us -> 15.4 us  [swap_y(): return lax.ppermute(value, 'col', [(i, i ^ 4 * j) for i in range(16)])]
    ppermute x4, waiting for transfers between devices: 16.5 us -> 18.4 us  [swap_x(): return lax.ppermute(value, 'col', [(i, i ^ j) for i in range(16)])]
  transfers between devices with their start and end apart: 13 -> 13, of which waited for: 9 -> 9; matrix products, arithmetic and copies ran while one was open for 2% -> 1% of each run, Pallas kernels for 2% -> 2%
where the time goes in v6:
time: 157 us; the launch traced here: 156 us
  waiting for transfers between devices  45.2 us (29%)
  blocking collectives  42 us (27%)
  starting transfers between devices  41.4 us (26%)
  between operations  14.3 us (9%)
  Pallas kernels  6.18 us (4%)
  local copies, waits for them, and re-layouts  4.91 us (3%)
  other arithmetic  2.04 us (1%)
    all_gather x1, blocking collectives, per_device(): lax.all_gather(grad_out, 'depth', axis=0, tiled=True, axis_index_groups=[...  42 us
    ppermute x4, waiting for transfers between devices, swap_x(): return lax.ppermute(value, 'col', [(i, i ^ j) for i in range(16)])  18.4 us
    ppermute x4, starting transfers between devices, swap_y(): return lax.ppermute(value, 'col', [(i, i ^ 4 * j) for i in range(16)])  16.4 us
    ppermute x4, waiting for transfers between devices, swap_y(): return lax.ppermute(value, 'col', [(i, i ^ 4 * j) for i in range(16)])  15.4 us
    ppermute x4, starting transfers between devices, swap_x(): return lax.ppermute(value, 'col', [(i, i ^ j) for i in range(16)])  10.6 us
    ppermute x2, starting transfers between devices, swap_row(): return lax.ppermute(value, 'row', [(i, i ^ j) for i in range(4)])  8.38 us
    unnamed x12, local copies, waits for them, and re-layouts  4.78 us
    ppermute x1, waiting for transfers between devices, per_device(): lax.ppermute(own[tokens // 4:], 'depth', [(i, (i + 1 ^ 1) - 1 & 15) for i...  4.15 us
  transfers between devices with their start and end apart: 13, of which 9 were waited for; matrix products, arithmetic and copies ran while one was open for 1% of the time, Pallas kernels for 2%

profile of v6, /device:TPU:1, one launch (start us, length us, event | category | flops | bytes accessed | tf_op | source)
XLA Modules:
  0.0 156.0 jit_solution(5950201748683776380)
XLA Ops:
  7.9 42.0 %all_gather.6.own = bf16[384,1152]{1,0:T(8,128)(2,1)S(1)} all-gather(bf16[48,1152]{1,0:T(8,128)(2,1)} %param.5), channel_id=1, replica_groups={{0,2,4,6,8,10,12,14},{1,3,5,7,9,11,13,15},{16,18,20,22,24,26,28,30},{17..., dimensions={0}, use_global_device_ids=true | all-gather | bytes 995328 | tf_op jit(solution)/shard_map/all_gather | solution.py:86
  50.0 2.9 %collective-permute-start = (bf16[192,1152]{1,0:T(8,128)(2,1)S(1)}, bf16[192,1152]{1,0:T(8,128)(2,1)S(1)}, u32[]{:S(2)}, u32[]{:S(2)}) collective-permute-start(bf16[192,1152]{1,0:T(8,128)(2,1)S(1)} %get-tuple-element.25), channel_id=1, source_target_pairs={{0,1},{1,0},{2,3},{3,2},{4,5},{5,4},{6,7},{7,6},{8,9},{9,8},{10,11... | collective-permute-start | bytes 1327112 | tf_op jit(solution)/shard_map/ppermute | solution.py:93
  52.9 3.0 %collective-permute-start.1 = (bf16[192,1152]{1,0:T(8,128)(2,1)S(1)}, bf16[192,1152]{1,0:T(8,128)(2,1)S(1)}, u32[]{:S(2)}, u32[]{:S(2)}) collective-permute-start(bf16[192,1152]{1,0:T(8,128)(2,1)S(1)} %get-tuple-element.24), channel_id=1, source_target_pairs={{0,15},{1,2},{2,1},{3,4},{4,3},{5,6},{6,5},{7,8},{8,7},{9,10},{10,... | collective-permute-start | bytes 1327112 | tf_op jit(solution)/shard_map/ppermute | solution.py:94
  56.0 3.0 %collective-permute-done.near = bf16[192,1152]{1,0:T(8,128)(2,1)S(1)} collective-permute-done((bf16[192,1152]{1,0:T(8,128)(2,1)S(1)}, bf16[192,1152]{1,0:T(8,128)(2,1)S(1)}, u32[]{:S(2)}, u32[]{:S(2)}) %collective-permute-start) | collective-permute-done | bytes 442400 | tf_op jit(solution)/shard_map/ppermute | solution.py:93
  59.0 4.1 %collective-permute-done.1.far = bf16[192,1152]{1,0:T(8,128)(2,1)S(1)} collective-permute-done((bf16[192,1152]{1,0:T(8,128)(2,1)S(1)}, bf16[192,1152]{1,0:T(8,128)(2,1)S(1)}, u32[]{:S(2)}, u32[]{:S(2)}) %collective-permute-start.1) | collective-permute-done | bytes 442400 | tf_op jit(solution)/shard_map/ppermute | solution.py:94
  64.6 3.6 %grad_inputs.1 = (f32[384,384]{1,0:T(8,128)}, f32[384,384]{1,0:T(8,128)}, f32[384,384]{1,0:T(8,128)S(1)}, f32[384,384]{1,0:T(8,128)S(1)}) custom-call(s32[2]{0:T(128)S(1)} %pad_add_fusion.place_ref, bf16[384,1152]{1,0:T(8,128)(2,1)S(1)} %all_gather.6.own, bf16[192,1152]{1,0:T(8,128)(2,1)S(1)} %collective-permute-done.near, ...), custom_call_target="tpu_custom_call" | custom-call | flops 1358954496 | bytes 6291456 | tf_op jit(solution)/shard_map/grad_inputs/pallas_call | solution.py:99
  68.2 1.9 %collective-permute-start.2 = (f32[384,384]{1,0:T(8,128)}, f32[384,384]{1,0:T(8,128)S(1)}, u32[]{:S(2)}, u32[]{:S(2)}) collective-permute-start(f32[384,384]{1,0:T(8,128)} %get-tuple-element.14), channel_id=1, source_target_pairs={{0,16},{16,0},{32,48},{48,32},{64,80},{80,64},{96,112},{112,96},{1... | collective-permute-start | bytes 1769480 | tf_op jit(solution)/shard_map/ppermute | solution.py:16
  70.2 3.7 %collective-permute-start.4 = (f32[384,384]{1,0:T(8,128)}, f32[384,384]{1,0:T(8,128)S(1)}, u32[]{:S(2)}, u32[]{:S(2)}) collective-permute-start(f32[384,384]{1,0:T(8,128)} %get-tuple-element.16), channel_id=1, source_target_pairs={{0,48},{16,32},{32,16},{48,0},{64,112},{80,96},{96,80},{112,64},{1... | collective-permute-start | bytes 1769480 | tf_op jit(solution)/shard_map/ppermute | solution.py:16
  73.9 8.7 %collective-permute-done.2._a = f32[384,384]{1,0:T(8,128)S(1)} collective-permute-done((f32[384,384]{1,0:T(8,128)}, f32[384,384]{1,0:T(8,128)S(1)}, u32[]{:S(2)}, u32[]{:S(2)}) %collective-permute-start.2) | collective-permute-done | bytes 589856 | tf_op jit(solution)/shard_map/ppermute | solution.py:16
  82.6 4.4 %collective-permute-done.4._b = f32[384,384]{1,0:T(8,128)S(1)} collective-permute-done((f32[384,384]{1,0:T(8,128)}, f32[384,384]{1,0:T(8,128)S(1)}, u32[]{:S(2)}, u32[]{:S(2)}) %collective-permute-start.4) | collective-permute-done | bytes 589856 | tf_op jit(solution)/shard_map/ppermute | solution.py:16
  87.0 3.6 %all-gather.2.cloned.1.call-done.tokens = bf16[768,768]{1,0:T(8,128)(2,1)} async-done(((bf16[48,768]{1,0:T(8,128)(2,1)}), bf16[768,768]{1,0:T(8,128)(2,1)}) %all-gather.2.cloned.1.call-update) | async-done | bytes 1179664 | tf_op jit(solution)/shard_map/all_gather | solution.py:96
  93.9 2.6 %grad_weight.1 = (f32[384,1152]{1,0:T(8,128)S(1)}, f32[384,1152]{1,0:T(8,128)S(1)}) custom-call(s32[2]{0:T(128)S(1)} %pad_add_fusion.1.place_ref, f32[384,384]{1,0:T(8,128)S(1)} %collective-permute-done.2._a, f32[384,384]{1,0:T(8,128)S(1)} %collective-permute-done.4._b, bf16[384,1152]{1,0:T(8,128)(2,1)S(1)} %all_gather.6.own, ...), custom_call_target="tpu_custom_call" | custom-call | flops 1358954496 | bytes 7340032 | tf_op jit(solution)/shard_map/grad_weight/pallas_call | solution.py:114
  96.5 5.3 %collective-permute-start.6 = (f32[384,1152]{1,0:T(8,128)S(1)}, f32[384,1152]{1,0:T(8,128)S(1)}, u32[]{:S(2)}, u32[]{:S(2)}) collective-permute-start(f32[384,1152]{1,0:T(8,128)S(1)} %get-tuple-element.18), channel_id=1, source_target_pairs={{0,256},{256,0},{512,768},{768,512},{1,257},{257,1},{513,769},{769... | collective-permute-start | bytes 5308424 | tf_op jit(solution)/shard_map/ppermute | solution.py:24
  101.9 2.1 %collective-permute-start.5 = (f32[192,384]{1,0:T(8,128)S(1)}, f32[192,384]{1,0:T(8,128)S(1)}, u32[]{:S(2)}, u32[]{:S(2)}) collective-permute-start(f32[192,384]{1,0:T(8,128)S(1)} %slice.104), channel_id=1, source_target_pairs={{0,16},{16,0},{32,48},{48,32},{64,80},{80,64},{96,112},{112,96},{1... | collective-permute-start | bytes 884744 | tf_op jit(solution)/shard_map/ppermute | solution.py:16
  104.1 2.9 %collective-permute-start.3 = (f32[192,384]{1,0:T(8,128)S(1)}, f32[192,384]{1,0:T(8,128)S(1)}, u32[]{:S(2)}, u32[]{:S(2)}) collective-permute-start(f32[192,384]{1,0:T(8,128)S(1)} %slice.103), channel_id=1, source_target_pairs={{0,48},{16,32},{32,16},{48,0},{64,112},{80,96},{96,80},{112,64},{1... | collective-permute-start | bytes 884744 | tf_op jit(solution)/shard_map/ppermute | solution.py:16
  107.1 3.1 %collective-permute-start.9 = (f32[192,1152]{1,0:T(8,128)S(1)}, f32[192,1152]{1,0:T(8,128)S(1)}, u32[]{:S(2)}, u32[]{:S(2)}) collective-permute-start(f32[192,1152]{1,0:T(8,128)S(1)} %slice_add_fusion.1), channel_id=1, source_target_pairs={{0,512},{256,768},{512,0},{768,256},{1,513},{257,769},{513,1},{769... | collective-permute-start | bytes 2654216 | tf_op jit(solution)/shard_map/ppermute | solution.py:24
  110.2 2.1 %collective-permute-done.5 = f32[192,384]{1,0:T(8,128)S(1)} collective-permute-done((f32[192,384]{1,0:T(8,128)S(1)}, f32[192,384]{1,0:T(8,128)S(1)}, u32[]{:S(2)}, u32[]{:S(2)}) %collective-permute-start.5) | collective-permute-done | bytes 294944 | tf_op jit(solution)/shard_map/ppermute | solution.py:16
  112.4 3.1 %collective-permute-done.3 = f32[192,384]{1,0:T(8,128)S(1)} collective-permute-done((f32[192,384]{1,0:T(8,128)S(1)}, f32[192,384]{1,0:T(8,128)S(1)}, u32[]{:S(2)}, u32[]{:S(2)}) %collective-permute-start.3) | collective-permute-done | bytes 294944 | tf_op jit(solution)/shard_map/ppermute | solution.py:16
  115.6 5.8 %collective-permute-start.8 = (f32[2,48,384]{2,1,0:T(8,128)S(1)}, f32[2,48,384]{2,1,0:T(8,128)S(1)}, u32[]{:S(2)}, u32[]{:S(2)}) collective-permute-start(f32[2,48,384]{2,1,0:T(8,128)S(1)} %bitcast.32), channel_id=1, source_target_pairs={{0,192},{16,208},{32,224},{48,240},{64,128},{80,144},{96,160},{112... | collective-permute-start | bytes 442376 | tf_op jit(solution)/shard_map/ppermute | solution.py:20
  121.5 3.7 %collective-permute-start.7 = (f32[2,48,384]{2,1,0:T(8,128)S(1)}, f32[2,48,384]{2,1,0:T(8,128)S(1)}, u32[]{:S(2)}, u32[]{:S(2)}) collective-permute-start(f32[2,48,384]{2,1,0:T(8,128)S(1)} %pad_maximum_fusion), channel_id=1, source_target_pairs={{0,64},{16,80},{32,96},{48,112},{64,0},{80,16},{96,32},{112,48},{1... | collective-permute-start | bytes 442376 | tf_op jit(solution)/shard_map/ppermute | solution.py:20
  125.2 13.1 %collective-permute-done.8 = f32[2,48,384]{2,1,0:T(8,128)S(1)} collective-permute-done((f32[2,48,384]{2,1,0:T(8,128)S(1)}, f32[2,48,384]{2,1,0:T(8,128)S(1)}, u32[]{:S(2)}, u32[]{:S(2)}) %collective-permute-start.8) | collective-permute-done | bytes 147488 | tf_op jit(solution)/shard_map/ppermute | solution.py:20
  138.3 3.9 %collective-permute-start.10 = (f32[48,384]{1,0:T(8,128)S(1)}, f32[48,384]{1,0:T(8,128)S(1)}, u32[]{:S(2)}, u32[]{:S(2)}) collective-permute-start(f32[48,384]{1,0:T(8,128)S(1)} %fusion.6), channel_id=1, source_target_pairs={{0,192},{16,208},{32,224},{48,240},{64,128},{80,144},{96,160},{112... | collective-permute-start | bytes 221192 | tf_op jit(solution)/shard_map/ppermute | solution.py:20
  142.2 3.1 %collective-permute-start.11 = (f32[48,384]{1,0:T(8,128)S(1)}, f32[48,384]{1,0:T(8,128)S(1)}, u32[]{:S(2)}, u32[]{:S(2)}) collective-permute-start(f32[48,384]{1,0:T(8,128)S(1)} %fusion.5), channel_id=1, source_target_pairs={{0,64},{16,80},{32,96},{48,112},{64,0},{80,16},{96,32},{112,48},{1... | collective-permute-start | bytes 221192 | tf_op jit(solution)/shard_map/ppermute | solution.py:20
  146.2 2.3 %collective-permute-done.11 = f32[48,384]{1,0:T(8,128)S(1)} collective-permute-done((f32[48,384]{1,0:T(8,128)S(1)}, f32[48,384]{1,0:T(8,128)S(1)}, u32[]{:S(2)}, u32[]{:S(2)}) %collective-permute-start.11) | collective-permute-done | bytes 73760 | tf_op jit(solution)/shard_map/ppermute | solution.py:20
  (37 shorter events, 7.7 us)
Async XLA Ops:
  7.2 83.4 %all-gather.2.cloned.1.call-start = ((), (), s32[]{:S(2)}) async-start(), calls=%async_computation | async-start | bytes 1253376 | tf_op jit(solution)/shard_map/all_gather | solution.py:96
  50.0 9.0 %collective-permute-start = (bf16[192,1152]{1,0:T(8,128)(2,1)S(1)}, bf16[192,1152]{1,0:T(8,128)(2,1)S(1)}, u32[]{:S(2)}, u32[]{:S(2)}) collective-permute-start(bf16[192,1152]{1,0:T(8,128)(2,1)S(1)} %get-tuple-element.25), channel_id=1, source_target_pairs={{0,1},{1,0},{2,3},{3,2},{4,5},{5,4},{6,7},{7,6},{8,9},{9,8},{10,11... | collective-permute-start | bytes 1327112 | tf_op jit(solution)/shard_map/ppermute | solution.py:93
  52.9 10.3 %collective-permute-start.1 = (bf16[192,1152]{1,0:T(8,128)(2,1)S(1)}, bf16[192,1152]{1,0:T(8,128)(2,1)S(1)}, u32[]{:S(2)}, u32[]{:S(2)}) collective-permute-start(bf16[192,1152]{1,0:T(8,128)(2,1)S(1)} %get-tuple-element.24), channel_id=1, source_target_pairs={{0,15},{1,2},{2,1},{3,4},{4,3},{5,6},{6,5},{7,8},{8,7},{9,10},{10,... | collective-permute-start | bytes 1327112 | tf_op jit(solution)/shard_map/ppermute | solution.py:94
  59.0 9.2 %copy-start.2 = (bf16[192,1152]{1,0:T(8,128)(2,1)}, bf16[192,1152]{1,0:T(8,128)(2,1)S(1)}, u32[]{:S(2)}) copy-start(bf16[192,1152]{1,0:T(8,128)(2,1)S(1)} %collective-permute-done.near) | copy-start | bytes 1327108
  63.2 1.5 copy-start
  64.6 3.6 %copy-start.4 = (bf16[192,1152]{1,0:T(8,128)(2,1)}, bf16[192,1152]{1,0:T(8,128)(2,1)S(1)}, u32[]{:S(2)}) copy-start(bf16[192,1152]{1,0:T(8,128)(2,1)S(1)} %collective-permute-done.1.far) | copy-start | bytes 1327108
  68.2 14.4 %collective-permute-start.2 = (f32[384,384]{1,0:T(8,128)}, f32[384,384]{1,0:T(8,128)S(1)}, u32[]{:S(2)}, u32[]{:S(2)}) collective-permute-start(f32[384,384]{1,0:T(8,128)} %get-tuple-element.14), channel_id=1, source_target_pairs={{0,16},{16,0},{32,48},{48,32},{64,80},{80,64},{96,112},{112,96},{1... | collective-permute-start | bytes 1769480 | tf_op jit(solution)/shard_map/ppermute | solution.py:16
  70.2 16.9 %collective-permute-start.4 = (f32[384,384]{1,0:T(8,128)}, f32[384,384]{1,0:T(8,128)S(1)}, u32[]{:S(2)}, u32[]{:S(2)}) collective-permute-start(f32[384,384]{1,0:T(8,128)} %get-tuple-element.16), channel_id=1, source_target_pairs={{0,48},{16,32},{32,16},{48,0},{64,112},{80,96},{96,80},{112,64},{1... | collective-permute-start | bytes 1769480 | tf_op jit(solution)/shard_map/ppermute | solution.py:16
  90.6 1.3 copy-start.1
  91.9 1.0 copy-start.3
  92.9 1.0 copy-start.5
  96.5 10.5 %collective-permute-start.6 = (f32[384,1152]{1,0:T(8,128)S(1)}, f32[384,1152]{1,0:T(8,128)S(1)}, u32[]{:S(2)}, u32[]{:S(2)}) collective-permute-start(f32[384,1152]{1,0:T(8,128)S(1)} %get-tuple-element.18), channel_id=1, source_target_pairs={{0,256},{256,0},{512,768},{768,512},{1,257},{257,1},{513,769},{769... | collective-permute-start | bytes 5308424 | tf_op jit(solution)/shard_map/ppermute | solution.py:24
  101.9 10.5 %collective-permute-start.5 = (f32[192,384]{1,0:T(8,128)S(1)}, f32[192,384]{1,0:T(8,128)S(1)}, u32[]{:S(2)}, u32[]{:S(2)}) collective-permute-start(f32[192,384]{1,0:T(8,128)S(1)} %slice.104), channel_id=1, source_target_pairs={{0,16},{16,0},{32,48},{48,32},{64,80},{80,64},{96,112},{112,96},{1... | collective-permute-start | bytes 884744 | tf_op jit(solution)/shard_map/ppermute | solution.py:16
  104.1 11.4 %collective-permute-start.3 = (f32[192,384]{1,0:T(8,128)S(1)}, f32[192,384]{1,0:T(8,128)S(1)}, u32[]{:S(2)}, u32[]{:S(2)}) collective-permute-start(f32[192,384]{1,0:T(8,128)S(1)} %slice.103), channel_id=1, source_target_pairs={{0,48},{16,32},{32,16},{48,0},{64,112},{80,96},{96,80},{112,64},{1... | collective-permute-start | bytes 884744 | tf_op jit(solution)/shard_map/ppermute | solution.py:16
  107.1 31.2 %collective-permute-start.9 = (f32[192,1152]{1,0:T(8,128)S(1)}, f32[192,1152]{1,0:T(8,128)S(1)}, u32[]{:S(2)}, u32[]{:S(2)}) collective-permute-start(f32[192,1152]{1,0:T(8,128)S(1)} %slice_add_fusion.1), channel_id=1, source_target_pairs={{0,512},{256,768},{512,0},{768,256},{1,513},{257,769},{513,1},{769... | collective-permute-start | bytes 2654216 | tf_op jit(solution)/shard_map/ppermute | solution.py:24
  115.6 22.6 %collective-permute-start.8 = (f32[2,48,384]{2,1,0:T(8,128)S(1)}, f32[2,48,384]{2,1,0:T(8,128)S(1)}, u32[]{:S(2)}, u32[]{:S(2)}) collective-permute-start(f32[2,48,384]{2,1,0:T(8,128)S(1)} %bitcast.32), channel_id=1, source_target_pairs={{0,192},{16,208},{32,224},{48,240},{64,128},{80,144},{96,160},{112... | collective-permute-start | bytes 442376 | tf_op jit(solution)/shard_map/ppermute | solution.py:20
  121.5 16.8 %collective-permute-start.7 = (f32[2,48,384]{2,1,0:T(8,128)S(1)}, f32[2,48,384]{2,1,0:T(8,128)S(1)}, u32[]{:S(2)}, u32[]{:S(2)}) collective-permute-start(f32[2,48,384]{2,1,0:T(8,128)S(1)} %pad_maximum_fusion), channel_id=1, source_target_pairs={{0,64},{16,80},{32,96},{48,112},{64,0},{80,16},{96,32},{112,48},{1... | collective-permute-start | bytes 442376 | tf_op jit(solution)/shard_map/ppermute | solution.py:20
  138.3 7.9 %collective-permute-start.10 = (f32[48,384]{1,0:T(8,128)S(1)}, f32[48,384]{1,0:T(8,128)S(1)}, u32[]{:S(2)}, u32[]{:S(2)}) collective-permute-start(f32[48,384]{1,0:T(8,128)S(1)} %fusion.6), channel_id=1, source_target_pairs={{0,192},{16,208},{32,224},{48,240},{64,128},{80,144},{96,160},{112... | collective-permute-start | bytes 221192 | tf_op jit(solution)/shard_map/ppermute | solution.py:20
  142.2 6.3 %collective-permute-start.11 = (f32[48,384]{1,0:T(8,128)S(1)}, f32[48,384]{1,0:T(8,128)S(1)}, u32[]{:S(2)}, u32[]{:S(2)}) collective-permute-start(f32[48,384]{1,0:T(8,128)S(1)} %fusion.5), channel_id=1, source_target_pairs={{0,64},{16,80},{32,96},{48,112},{64,0},{80,16},{96,32},{112,48},{1... | collective-permute-start | bytes 221192 | tf_op jit(solution)/shard_map/ppermute | solution.py:20
Sparse Core Ops, SparseCore 0:
  12.2 78.3 all-gather.1

commit v7 on v6

--- a/solution.py
+++ b/solution.py
@@ -24,29 +24,17 @@
     return lax.ppermute(value, "row", [(i, i ^ j) for i in range(4)])
 
 
-def spread(depth, chunks, block, into, place):
-    parity = jnp.bitwise_and(depth, 1)
-    for ref, own, lead in zip(chunks, (1, 0, 0), (0, 0, ref_blocks(chunks[1], block))):
-        for k in range(ref_blocks(ref, block)):
-            source = 2 * (lead + k) + (parity if own else 1 - parity)
-            at = pl.multiple_of(place(source) * block, block)
-            into[pl.ds(at, block), :] = ref[pl.ds(k * block, block), :]
-
-
-def ref_blocks(ref, block):
-    return ref.shape[0] // block
-
-
 def grad_inputs_kernel(place_ref, own, near, far, weight_ref, send_a, send_b, keep_a, keep_b, rows):
     block = own.shape[0] // 8
     half = weight_ref.shape[0] // 2
 
-    def place(source):
-        j = jnp.bitwise_xor(source, place_ref[1])
-        jx, jy = jnp.bitwise_and(j, 3), jnp.right_shift(j, 2)
-        return jx * 4 + jnp.bitwise_xor(jy, jnp.right_shift(jy, 1))
-
-    spread(place_ref[0], (own, near, far), block, rows, place)
+    parity = jnp.bitwise_and(place_ref[0], 1)
+    for ref, first, odd in ((own, 0, parity), (near, 0, 1 - parity), (far, 8, 1 - parity)):
+        for k in range(ref.shape[0] // block):
+            j = jnp.bitwise_xor(first + 2 * k + odd, place_ref[1])
+            jx, jy = jnp.bitwise_and(j, 3), jnp.right_shift(j, 2)
+            at = jx * 4 + jnp.bitwise_xor(jy, jnp.right_shift(jy, 1))
+            rows[pl.ds(pl.multiple_of(at * block, block), block), :] = ref[pl.ds(k * block, block), :]
     quarter = 4 * block
     for out_half, (sent, kept, sends, keeps) in enumerate(
         ((send_a, keep_a, (1, 2), (0, 3)), (send_b, keep_b, (3, 2), (0, 1)))
@@ -62,15 +50,16 @@
                 ref[pl.ds(slot * quarter, quarter), :] = part[jx * quarter : (jx + 1) * quarter]
 
 
-def grad_weight_kernel(place_ref, _a, _b, own, near, far, tokens, sent, kept, grads, total):
-    spread(place_ref[0], (own, near, far), own.shape[0] // 8, grads, lambda source: source)
+def grad_weight_kernel(row_ref, grads, x0, x1, x2, x3, sent, kept, tokens, total):
+    for jx, ref in enumerate((x0, x1, x2, x3)):
+        tokens[pl.ds(jx * ref.shape[0], ref.shape[0]), :] = ref[...]
     total[...] = lax.dot_general(
         tokens[...], grads[...], (((0,), (0,)), ((), ())), preferred_element_type=F32
     )
     rows = total.shape[0] // 4
     for jy in range(2):
         for jc, ref in ((1, sent), (0, kept)):
-            source = jnp.bitwise_xor(place_ref[1], jy * 2 + jc) * rows
+            source = jnp.bitwise_xor(row_ref[0], jy * 2 + jc) * rows
             ref[pl.ds(jy * rows, rows), :] = total[pl.ds(pl.multiple_of(source, rows), rows), :]
 
 
@@ -83,6 +72,7 @@
     columns = weight.shape[1]
     tokens = block * 16
     depth, col, row = (lax.axis_index(a) for a in ("depth", "col", "row"))
+    ring = [inputs] + [swap_y(inputs, j) for j in ORDER[1:]]
     own = lax.all_gather(
         grad_out,
         "depth",
@@ -92,37 +82,37 @@
     )
     near = lax.ppermute(own[: tokens // 4], "depth", [(i, i ^ 1) for i in range(16)])
     far = lax.ppermute(own[tokens // 4 :], "depth", [(i, ((i + 1) ^ 1) - 1 & 15) for i in range(16)])
-    grads = (own, near, far)
-    gathered = lax.all_gather(inputs, "col", axis=0, tiled=True)
+    x0 = jnp.concatenate(ring)
+    x1, x3 = swap_x(x0, 1), swap_x(x0, 3)
+    x2 = swap_x(x1, 3)
 
     piece = jax.ShapeDtypeStruct((tokens // 2, width // 2), F32)
-    send_a, send_b, keep_a, keep_b = pl.pallas_call(
+    send_a, send_b, keep_a, keep_b, grads = pl.pallas_call(
         grad_inputs_kernel,
-        out_shape=[piece] * 4,
+        out_shape=[piece] * 4 + [jax.ShapeDtypeStruct((tokens, columns), BF16)],
         in_specs=[SMEM] + [VMEM] * 4,
-        out_specs=[VMEM] * 4,
-        scratch_shapes=[pltpu.VMEM((tokens, columns), BF16)],
+        out_specs=[VMEM] * 5,
         compiler_params=pltpu.CompilerParams(vmem_limit_bytes=7 << 20),
         cost_estimate=pl.CostEstimate(
             flops=2 * tokens * width * columns, bytes_accessed=6 << 20, transcendentals=0
         ),
         name="grad_inputs",
-    )(jnp.stack([depth, col]), *grads, weight)
+    )(jnp.stack([depth, col]), own, near, far, weight)
     got_a, got_b = swap_x(send_a, 1), swap_x(send_b, 3)
 
     half = jax.ShapeDtypeStruct((width // 2, columns), F32)
     send_w, keep_w = pl.pallas_call(
         grad_weight_kernel,
         out_shape=[half] * 2,
-        in_specs=[SMEM] + [pl.BlockSpec(memory_space=pl.ANY)] * 2 + [VMEM] * 4,
+        in_specs=[SMEM] + [VMEM] * 5,
         out_specs=[VMEM] * 2,
-        scratch_shapes=[pltpu.VMEM((tokens, columns), BF16), pltpu.VMEM((width, columns), F32)],
+        scratch_shapes=[pltpu.VMEM((tokens, width), BF16), pltpu.VMEM((width, columns), F32)],
         compiler_params=pltpu.CompilerParams(vmem_limit_bytes=9 << 20),
         cost_estimate=pl.CostEstimate(
             flops=2 * tokens * width * columns, bytes_accessed=7 << 20, transcendentals=0
         ),
         name="grad_weight",
-    )(jnp.stack([depth, row]), got_a, got_b, *grads, gathered)
+    )(row.reshape(1), grads, x0, x1, x2, x3)
 
     rows = width // 4
     got_w = swap_row(send_w, 1)

time: 157 us -> 157 us (level); the launches traced: 156 us -> 154 us
  starting transfers between devices: 41.4 us -> 66.7 us
  between operations: 14.3 us -> 0.95 us
  waiting for transfers between devices: 45.2 us -> 36.8 us
  local copies, waits for them, and re-layouts: 4.91 us -> 1.95 us
  blocking collectives: 42 us -> 39.6 us
    ppermute x4 -> x7, starting transfers between devices: 16.4 us -> 27.9 us  [swap_y(): return lax.ppermute(value, 'col', [(i, i ^ 4 * j) for i in range(16)])]
    ppermute x4 -> x7, starting transfers between devices: 10.6 us -> 19.1 us  [swap_x(): return lax.ppermute(value, 'col', [(i, i ^ j) for i in range(16)])]
    ppermute x2, starting transfers between devices: 8.38 us -> 12.9 us  [swap_row(): return lax.ppermute(value, 'row', [(i, i ^ j) for i in range(4)])]
    ppermute x1, waiting for transfers between devices: 4.15 us -> 0.01 us  [per_device(): lax.ppermute(own[tokens // 4:], 'depth', [(i, (i + 1 ^ 1) - 1 & 15) for i...]
    unnamed x12 -> x5, local copies, waits for them, and re-layouts: 4.78 us -> 0.91 us
    all_gather x1 -> x0, waiting for transfers between devices: 3.59 us -> none  [per_device(): gathered = lax.all_gather(inputs, 'col', axis=0, tiled=True)]
    all_gather x1, blocking collectives: 42 us -> 39.6 us  [per_device(): lax.all_gather(grad_out, 'depth', axis=0, tiled=True, axis_index_groups=[...]
    ppermute x1, waiting for transfers between devices: 3.02 us -> 1.02 us  [per_device(): lax.ppermute(own[:tokens // 4], 'depth', [(i, i ^ 1) for i in range(16)])]
  transfers between devices with their start and end apart: 13 -> 18, of which waited for: 9 -> 9; matrix products, arithmetic and copies ran while one was open for 1% -> 2% of each run, Pallas kernels for 2% -> 2%
where the time goes in v7:
time: 157 us; the launch traced here: 154 us
  starting transfers between devices  66.7 us (42%)
  blocking collectives  39.6 us (25%)
  waiting for transfers between devices  36.8 us (23%)
  Pallas kernels  6.34 us (4%)
  other arithmetic  1.99 us (1%)
  local copies, waits for them, and re-layouts  1.95 us (1%)
    all_gather x1, blocking collectives, per_device(): lax.all_gather(grad_out, 'depth', axis=0, tiled=True, axis_index_groups=[...  39.6 us
    ppermute x7, starting transfers between devices, swap_y(): return lax.ppermute(value, 'col', [(i, i ^ 4 * j) for i in range(16)])  27.9 us
    ppermute x7, waiting for transfers between devices, swap_x(): return lax.ppermute(value, 'col', [(i, i ^ j) for i in range(16)])  19.3 us
    ppermute x7, starting transfers between devices, swap_x(): return lax.ppermute(value, 'col', [(i, i ^ j) for i in range(16)])  19.1 us
    ppermute x7, waiting for transfers between devices, swap_y(): return lax.ppermute(value, 'col', [(i, i ^ 4 * j) for i in range(16)])  16.5 us
    ppermute x2, starting transfers between devices, swap_row(): return lax.ppermute(value, 'row', [(i, i ^ j) for i in range(4)])  12.9 us
    ppermute x1, starting transfers between devices, per_device(): lax.ppermute(own[tokens // 4:], 'depth', [(i, (i + 1 ^ 1) - 1 & 15) for i...  4.97 us
    pallas_call x1, Pallas kernels, per_device(): pl.pallas_call(grad_inputs_kernel, out_shape=[piece] * 4 + [jax.ShapeDtyp...  3.23 us
  transfers between devices with their start and end apart: 18, of which 9 were waited for; matrix products, arithmetic and copies ran while one was open for 2% of the time, Pallas kernels for 2%

profile of v7, /device:TPU:1, one launch (start us, length us, event | category | flops | bytes accessed | tf_op | source)
XLA Modules:
  0.0 154.3 jit_solution(4965098119393486117)
XLA Ops:
  0.6 6.8 %collective-permute-start.7 = (bf16[48,768]{1,0:T(8,128)(2,1)}, bf16[48,768]{1,0:T(8,128)(2,1)S(1)}, u32[]{:S(2)}, u32[]{:S(2)}) collective-permute-start(bf16[48,768]{1,0:T(8,128)(2,1)} %param.3), channel_id=1, source_target_pairs={{0,192},{16,208},{32,224},{48,240},{64,128},{80,144},{96,160},{112... | collective-permute-start | bytes 221192 | tf_op jit(solution)/shard_map/ppermute | solution.py:20
  7.5 3.8 %collective-permute-start.6 = (bf16[48,768]{1,0:T(8,128)(2,1)}, bf16[48,768]{1,0:T(8,128)(2,1)S(1)}, u32[]{:S(2)}, u32[]{:S(2)}) collective-permute-start(bf16[48,768]{1,0:T(8,128)(2,1)} %param.3), channel_id=1, source_target_pairs={{0,64},{16,80},{32,96},{48,112},{64,0},{80,16},{96,32},{112,48},{1... | collective-permute-start | bytes 221192 | tf_op jit(solution)/shard_map/ppermute | solution.py:20
  11.3 2.1 %collective-permute-start.8 = (bf16[48,768]{1,0:T(8,128)(2,1)}, bf16[48,768]{1,0:T(8,128)(2,1)S(1)}, u32[]{:S(2)}, u32[]{:S(2)}) collective-permute-start(bf16[48,768]{1,0:T(8,128)(2,1)} %param.3), channel_id=1, source_target_pairs={{0,128},{16,144},{32,160},{48,176},{64,192},{80,208},{96,224},{112... | collective-permute-start | bytes 221192 | tf_op jit(solution)/shard_map/ppermute | solution.py:20
  13.4 39.6 %all_gather.3.own = bf16[384,1152]{1,0:T(8,128)(2,1)S(1)} all-gather(bf16[48,1152]{1,0:T(8,128)(2,1)} %param.5), channel_id=1, replica_groups={{0,2,4,6,8,10,12,14},{1,3,5,7,9,11,13,15},{16,18,20,22,24,26,28,30},{17..., dimensions={0}, use_global_device_ids=true | all-gather | bytes 995328 | tf_op jit(solution)/shard_map/all_gather | solution.py:76
  53.9 3.2 %collective-permute-start.9 = (bf16[192,768]{1,0:T(8,128)(2,1)S(1)}, bf16[192,768]{1,0:T(8,128)(2,1)}, u32[]{:S(2)}, u32[]{:S(2)}) collective-permute-start(bf16[192,768]{1,0:T(8,128)(2,1)S(1)} %constant_dynamic-update-slice_fusion.x0), channel_id=1, source_target_pairs={{0,16},{16,0},{32,48},{48,32},{64,80},{80,64},{96,112},{112,96},{1... | collective-permute-start | bytes 884744 | tf_op jit(solution)/shard_map/ppermute | solution.py:16
  58.1 5.0 %collective-permute-start.1 = (bf16[192,1152]{1,0:T(8,128)(2,1)}, bf16[192,1152]{1,0:T(8,128)(2,1)S(1)}, u32[]{:S(2)}, u32[]{:S(2)}) collective-permute-start(bf16[192,1152]{1,0:T(8,128)(2,1)} %get-tuple-element.26), channel_id=1, source_target_pairs={{0,15},{1,2},{2,1},{3,4},{4,3},{5,6},{6,5},{7,8},{8,7},{9,10},{10,... | collective-permute-start | bytes 1327112 | tf_op jit(solution)/shard_map/ppermute | solution.py:84
  63.1 1.9 %collective-permute-start = (bf16[192,1152]{1,0:T(8,128)(2,1)}, bf16[192,1152]{1,0:T(8,128)(2,1)}, u32[]{:S(2)}, u32[]{:S(2)}) collective-permute-start(bf16[192,1152]{1,0:T(8,128)(2,1)} %get-tuple-element.27), channel_id=1, source_target_pairs={{0,1},{1,0},{2,3},{3,2},{4,5},{5,4},{6,7},{7,6},{8,9},{9,8},{10,11... | collective-permute-start | bytes 1327112 | tf_op jit(solution)/shard_map/ppermute | solution.py:83
  65.0 3.7 %collective-permute-start.11 = (bf16[192,768]{1,0:T(8,128)(2,1)S(1)}, bf16[192,768]{1,0:T(8,128)(2,1)}, u32[]{:S(2)}, u32[]{:S(2)}) collective-permute-start(bf16[192,768]{1,0:T(8,128)(2,1)S(1)} %constant_dynamic-update-slice_fusion.x0), channel_id=1, source_target_pairs={{0,48},{16,32},{32,16},{48,0},{64,112},{80,96},{96,80},{112,64},{1... | collective-permute-start | bytes 884744 | tf_op jit(solution)/shard_map/ppermute | solution.py:16
  68.8 2.8 %collective-permute-start.10 = (bf16[192,768]{1,0:T(8,128)(2,1)}, bf16[192,768]{1,0:T(8,128)(2,1)}, u32[]{:S(2)}, u32[]{:S(2)}) collective-permute-start(bf16[192,768]{1,0:T(8,128)(2,1)} %collective-permute-done.9.x1), channel_id=1, source_target_pairs={{0,48},{16,32},{32,16},{48,0},{64,112},{80,96},{96,80},{112,64},{1... | collective-permute-start | bytes 884744 | tf_op jit(solution)/shard_map/ppermute | solution.py:16
  72.6 3.2 %grad_inputs.1 = (f32[384,384]{1,0:T(8,128)S(1)}, f32[384,384]{1,0:T(8,128)S(1)}, f32[384,384]{1,0:T(8,128)S(1)}, f32[384,384]{1,0:T(8,128)S(1)}, bf16[768,1152]{1,0:T(8,128)(2,1)S(1)}) custom-call(s32[2]{0:T(128)S(1)} %pad_add_fusion.place_ref, bf16[384,1152]{1,0:T(8,128)(2,1)S(1)} %all_gather.3.own, bf16[192,1152]{1,0:T(8,128)(2,1)} %collective-permute-done.near, ...), custom_call_target="tpu_custom_call" | custom-call | flops 1358954496 | bytes 6291456 | tf_op jit(solution)/shard_map/grad_inputs/pallas_call | solution.py:90
  77.7 3.1 %grad_weight.1 = (f32[384,1152]{1,0:T(8,128)S(1)}, f32[384,1152]{1,0:T(8,128)S(1)}) custom-call(s32[1]{0:T(128)} %bitcast.2.row_ref, bf16[768,1152]{1,0:T(8,128)(2,1)S(1)} %get-tuple-element.18.grads, bf16[192,768]{1,0:T(8,128)(2,1)S(1)} %constant_dynamic-update-slice_fusion.x0, bf16[192,768]{1,0:T(8,128)(2,1)} %collective-permute-done.9.x1, ...), custom_call_target="tpu_custom_call" | custom-call | flops 1358954496 | bytes 7340032 | tf_op jit(solution)/shard_map/grad_weight/pallas_call | solution.py:104
  80.9 10.4 %collective-permute-start.12 = (f32[384,1152]{1,0:T(8,128)S(1)}, f32[384,1152]{1,0:T(8,128)S(1)}, u32[]{:S(2)}, u32[]{:S(2)}) collective-permute-start(f32[384,1152]{1,0:T(8,128)S(1)} %get-tuple-element.20), channel_id=1, source_target_pairs={{0,256},{256,0},{512,768},{768,512},{1,257},{257,1},{513,769},{769... | collective-permute-start | bytes 5308424 | tf_op jit(solution)/shard_map/ppermute | solution.py:24
  93.2 2.8 %collective-permute-start.4 = (f32[384,384]{1,0:T(8,128)S(1)}, f32[384,384]{1,0:T(8,128)S(1)}, u32[]{:S(2)}, u32[]{:S(2)}) collective-permute-start(f32[384,384]{1,0:T(8,128)S(1)} %get-tuple-element.17), channel_id=1, source_target_pairs={{0,48},{16,32},{32,16},{48,0},{64,112},{80,96},{96,80},{112,64},{1... | collective-permute-start | bytes 1769480 | tf_op jit(solution)/shard_map/ppermute | solution.py:16
  96.0 12.1 %collective-permute-done.2 = f32[384,384]{1,0:T(8,128)S(1)} collective-permute-done((f32[384,384]{1,0:T(8,128)S(1)}, f32[384,384]{1,0:T(8,128)S(1)}, u32[]{:S(2)}, u32[]{:S(2)}) %collective-permute-start.2) | collective-permute-done | bytes 589856 | tf_op jit(solution)/shard_map/ppermute | solution.py:16
  108.2 2.8 %collective-permute-start.3 = (f32[192,384]{1,0:T(8,128)S(1)}, f32[192,384]{1,0:T(8,128)S(1)}, u32[]{:S(2)}, u32[]{:S(2)}) collective-permute-start(f32[192,384]{1,0:T(8,128)S(1)} %slice.103), channel_id=1, source_target_pairs={{0,48},{16,32},{32,16},{48,0},{64,112},{80,96},{96,80},{112,64},{1... | collective-permute-start | bytes 884744 | tf_op jit(solution)/shard_map/ppermute | solution.py:16
  113.4 2.5 %collective-permute-start.15 = (f32[192,1152]{1,0:T(8,128)S(1)}, f32[192,1152]{1,0:T(8,128)S(1)}, u32[]{:S(2)}, u32[]{:S(2)}) collective-permute-start(f32[192,1152]{1,0:T(8,128)S(1)} %slice_add_fusion.1), channel_id=1, source_target_pairs={{0,512},{256,768},{512,0},{768,256},{1,513},{257,769},{513,1},{769... | collective-permute-start | bytes 2654216 | tf_op jit(solution)/shard_map/ppermute | solution.py:24
  115.9 3.2 %collective-permute-done.3 = f32[192,384]{1,0:T(8,128)S(1)} collective-permute-done((f32[192,384]{1,0:T(8,128)S(1)}, f32[192,384]{1,0:T(8,128)S(1)}, u32[]{:S(2)}, u32[]{:S(2)}) %collective-permute-start.3) | collective-permute-done | bytes 294944 | tf_op jit(solution)/shard_map/ppermute | solution.py:16
  121.0 3.3 %collective-permute-start.13 = (f32[2,48,384]{2,1,0:T(8,128)S(1)}, f32[2,48,384]{2,1,0:T(8,128)S(1)}, u32[]{:S(2)}, u32[]{:S(2)}) collective-permute-start(f32[2,48,384]{2,1,0:T(8,128)S(1)} %pad_maximum_fusion), channel_id=1, source_target_pairs={{0,64},{16,80},{32,96},{48,112},{64,0},{80,16},{96,32},{112,48},{1... | collective-permute-start | bytes 442376 | tf_op jit(solution)/shard_map/ppermute | solution.py:20
  124.4 5.4 %collective-permute-start.14 = (f32[2,48,384]{2,1,0:T(8,128)S(1)}, f32[2,48,384]{2,1,0:T(8,128)S(1)}, u32[]{:S(2)}, u32[]{:S(2)}) collective-permute-start(f32[2,48,384]{2,1,0:T(8,128)S(1)} %bitcast.32), channel_id=1, source_target_pairs={{0,192},{16,208},{32,224},{48,240},{64,128},{80,144},{96,160},{112... | collective-permute-start | bytes 442376 | tf_op jit(solution)/shard_map/ppermute | solution.py:20
  129.8 10.0 %collective-permute-done.13 = f32[2,48,384]{2,1,0:T(8,128)S(1)} collective-permute-done((f32[2,48,384]{2,1,0:T(8,128)S(1)}, f32[2,48,384]{2,1,0:T(8,128)S(1)}, u32[]{:S(2)}, u32[]{:S(2)}) %collective-permute-start.13) | collective-permute-done | bytes 147488 | tf_op jit(solution)/shard_map/ppermute | solution.py:20
  139.8 3.4 %collective-permute-done.14 = f32[2,48,384]{2,1,0:T(8,128)S(1)} collective-permute-done((f32[2,48,384]{2,1,0:T(8,128)S(1)}, f32[2,48,384]{2,1,0:T(8,128)S(1)}, u32[]{:S(2)}, u32[]{:S(2)}) %collective-permute-start.14) | collective-permute-done | bytes 147488 | tf_op jit(solution)/shard_map/ppermute | solution.py:20
  143.3 3.6 %collective-permute-start.16 = (f32[48,384]{1,0:T(8,128)S(1)}, f32[48,384]{1,0:T(8,128)S(1)}, u32[]{:S(2)}, u32[]{:S(2)}) collective-permute-start(f32[48,384]{1,0:T(8,128)S(1)} %fusion.6), channel_id=1, source_target_pairs={{0,192},{16,208},{32,224},{48,240},{64,128},{80,144},{96,160},{112... | collective-permute-start | bytes 221192 | tf_op jit(solution)/shard_map/ppermute | solution.py:20
  146.9 2.8 %collective-permute-start.17 = (f32[48,384]{1,0:T(8,128)S(1)}, f32[48,384]{1,0:T(8,128)S(1)}, u32[]{:S(2)}, u32[]{:S(2)}) collective-permute-start(f32[48,384]{1,0:T(8,128)S(1)} %fusion.5), channel_id=1, source_target_pairs={{0,64},{16,80},{32,96},{48,112},{64,0},{80,16},{96,32},{112,48},{1... | collective-permute-start | bytes 221192 | tf_op jit(solution)/shard_map/ppermute | solution.py:20
  150.7 3.0 %collective-permute-done.17 = f32[48,384]{1,0:T(8,128)S(1)} collective-permute-done((f32[48,384]{1,0:T(8,128)S(1)}, f32[48,384]{1,0:T(8,128)S(1)}, u32[]{:S(2)}, u32[]{:S(2)}) %collective-permute-start.17) | collective-permute-done | bytes 73760 | tf_op jit(solution)/shard_map/ppermute | solution.py:20
  (39 shorter events, 12.8 us)
Async XLA Ops:
  0.6 72.0 %copy-start = (bf16[768,1152]{1,0:T(8,128)(2,1)S(1)}, bf16[768,1152]{1,0:T(8,128)(2,1)}, u32[]{:S(2)}) copy-start(bf16[768,1152]{1,0:T(8,128)(2,1)} %weight_ref.1) | copy-start | bytes 5308420
  0.6 53.2 %collective-permute-start.7 = (bf16[48,768]{1,0:T(8,128)(2,1)}, bf16[48,768]{1,0:T(8,128)(2,1)S(1)}, u32[]{:S(2)}, u32[]{:S(2)}) collective-permute-start(bf16[48,768]{1,0:T(8,128)(2,1)} %param.3), channel_id=1, source_target_pairs={{0,192},{16,208},{32,224},{48,240},{64,128},{80,144},{96,160},{112... | collective-permute-start | bytes 221192 | tf_op jit(solution)/shard_map/ppermute | solution.py:20
  7.5 46.4 %collective-permute-start.6 = (bf16[48,768]{1,0:T(8,128)(2,1)}, bf16[48,768]{1,0:T(8,128)(2,1)S(1)}, u32[]{:S(2)}, u32[]{:S(2)}) collective-permute-start(bf16[48,768]{1,0:T(8,128)(2,1)} %param.3), channel_id=1, source_target_pairs={{0,64},{16,80},{32,96},{48,112},{64,0},{80,16},{96,32},{112,48},{1... | collective-permute-start | bytes 221192 | tf_op jit(solution)/shard_map/ppermute | solution.py:20
  11.3 42.6 %collective-permute-start.8 = (bf16[48,768]{1,0:T(8,128)(2,1)}, bf16[48,768]{1,0:T(8,128)(2,1)S(1)}, u32[]{:S(2)}, u32[]{:S(2)}) collective-permute-start(bf16[48,768]{1,0:T(8,128)(2,1)} %param.3), channel_id=1, source_target_pairs={{0,128},{16,144},{32,160},{48,176},{64,192},{80,208},{96,224},{112... | collective-permute-start | bytes 221192 | tf_op jit(solution)/shard_map/ppermute | solution.py:20
  53.9 14.8 %collective-permute-start.9 = (bf16[192,768]{1,0:T(8,128)(2,1)S(1)}, bf16[192,768]{1,0:T(8,128)(2,1)}, u32[]{:S(2)}, u32[]{:S(2)}) collective-permute-start(bf16[192,768]{1,0:T(8,128)(2,1)S(1)} %constant_dynamic-update-slice_fusion.x0), channel_id=1, source_target_pairs={{0,16},{16,0},{32,48},{48,32},{64,80},{80,64},{96,112},{112,96},{1... | collective-permute-start | bytes 884744 | tf_op jit(solution)/shard_map/ppermute | solution.py:16
  58.1 13.5 %collective-permute-start.1 = (bf16[192,1152]{1,0:T(8,128)(2,1)}, bf16[192,1152]{1,0:T(8,128)(2,1)S(1)}, u32[]{:S(2)}, u32[]{:S(2)}) collective-permute-start(bf16[192,1152]{1,0:T(8,128)(2,1)} %get-tuple-element.26), channel_id=1, source_target_pairs={{0,15},{1,2},{2,1},{3,4},{4,3},{5,6},{6,5},{7,8},{8,7},{9,10},{10,... | collective-permute-start | bytes 1327112 | tf_op jit(solution)/shard_map/ppermute | solution.py:84
  63.1 9.6 %collective-permute-start = (bf16[192,1152]{1,0:T(8,128)(2,1)}, bf16[192,1152]{1,0:T(8,128)(2,1)}, u32[]{:S(2)}, u32[]{:S(2)}) collective-permute-start(bf16[192,1152]{1,0:T(8,128)(2,1)} %get-tuple-element.27), channel_id=1, source_target_pairs={{0,1},{1,0},{2,3},{3,2},{4,5},{5,4},{6,7},{7,6},{8,9},{9,8},{10,11... | collective-permute-start | bytes 1327112 | tf_op jit(solution)/shard_map/ppermute | solution.py:83
  65.0 10.9 %collective-permute-start.11 = (bf16[192,768]{1,0:T(8,128)(2,1)S(1)}, bf16[192,768]{1,0:T(8,128)(2,1)}, u32[]{:S(2)}, u32[]{:S(2)}) collective-permute-start(bf16[192,768]{1,0:T(8,128)(2,1)S(1)} %constant_dynamic-update-slice_fusion.x0), channel_id=1, source_target_pairs={{0,48},{16,32},{32,16},{48,0},{64,112},{80,96},{96,80},{112,64},{1... | collective-permute-start | bytes 884744 | tf_op jit(solution)/shard_map/ppermute | solution.py:16
  68.8 9.0 %collective-permute-start.10 = (bf16[192,768]{1,0:T(8,128)(2,1)}, bf16[192,768]{1,0:T(8,128)(2,1)}, u32[]{:S(2)}, u32[]{:S(2)}) collective-permute-start(bf16[192,768]{1,0:T(8,128)(2,1)} %collective-permute-done.9.x1), channel_id=1, source_target_pairs={{0,48},{16,32},{32,16},{48,0},{64,112},{80,96},{96,80},{112,64},{1... | collective-permute-start | bytes 884744 | tf_op jit(solution)/shard_map/ppermute | solution.py:16
  80.9 32.4 %collective-permute-start.12 = (f32[384,1152]{1,0:T(8,128)S(1)}, f32[384,1152]{1,0:T(8,128)S(1)}, u32[]{:S(2)}, u32[]{:S(2)}) collective-permute-start(f32[384,1152]{1,0:T(8,128)S(1)} %get-tuple-element.20), channel_id=1, source_target_pairs={{0,256},{256,0},{512,768},{768,512},{1,257},{257,1},{513,769},{769... | collective-permute-start | bytes 5308424 | tf_op jit(solution)/shard_map/ppermute | solution.py:24
  91.3 16.8 %collective-permute-start.2 = (f32[384,384]{1,0:T(8,128)S(1)}, f32[384,384]{1,0:T(8,128)S(1)}, u32[]{:S(2)}, u32[]{:S(2)}) collective-permute-start(f32[384,384]{1,0:T(8,128)S(1)} %get-tuple-element.15), channel_id=1, source_target_pairs={{0,16},{16,0},{32,48},{48,32},{64,80},{80,64},{96,112},{112,96},{1... | collective-permute-start | bytes 1769480 | tf_op jit(solution)/shard_map/ppermute | solution.py:16
  93.2 18.1 %collective-permute-start.4 = (f32[384,384]{1,0:T(8,128)S(1)}, f32[384,384]{1,0:T(8,128)S(1)}, u32[]{:S(2)}, u32[]{:S(2)}) collective-permute-start(f32[384,384]{1,0:T(8,128)S(1)} %get-tuple-element.17), channel_id=1, source_target_pairs={{0,48},{16,32},{32,16},{48,0},{64,112},{80,96},{96,80},{112,64},{1... | collective-permute-start | bytes 1769480 | tf_op jit(solution)/shard_map/ppermute | solution.py:16
  108.2 10.8 %collective-permute-start.3 = (f32[192,384]{1,0:T(8,128)S(1)}, f32[192,384]{1,0:T(8,128)S(1)}, u32[]{:S(2)}, u32[]{:S(2)}) collective-permute-start(f32[192,384]{1,0:T(8,128)S(1)} %slice.103), channel_id=1, source_target_pairs={{0,48},{16,32},{32,16},{48,0},{64,112},{80,96},{96,80},{112,64},{1... | collective-permute-start | bytes 884744 | tf_op jit(solution)/shard_map/ppermute | solution.py:16
  111.4 9.6 %collective-permute-start.5 = (f32[192,384]{1,0:T(8,128)S(1)}, f32[192,384]{1,0:T(8,128)S(1)}, u32[]{:S(2)}, u32[]{:S(2)}) collective-permute-start(f32[192,384]{1,0:T(8,128)S(1)} %slice.104), channel_id=1, source_target_pairs={{0,16},{16,0},{32,48},{48,32},{64,80},{80,64},{96,112},{112,96},{1... | collective-permute-start | bytes 884744 | tf_op jit(solution)/shard_map/ppermute | solution.py:16
  113.4 29.9 %collective-permute-start.15 = (f32[192,1152]{1,0:T(8,128)S(1)}, f32[192,1152]{1,0:T(8,128)S(1)}, u32[]{:S(2)}, u32[]{:S(2)}) collective-permute-start(f32[192,1152]{1,0:T(8,128)S(1)} %slice_add_fusion.1), channel_id=1, source_target_pairs={{0,512},{256,768},{512,0},{768,256},{1,513},{257,769},{513,1},{769... | collective-permute-start | bytes 2654216 | tf_op jit(solution)/shard_map/ppermute | solution.py:24
  121.0 18.8 %collective-permute-start.13 = (f32[2,48,384]{2,1,0:T(8,128)S(1)}, f32[2,48,384]{2,1,0:T(8,128)S(1)}, u32[]{:S(2)}, u32[]{:S(2)}) collective-permute-start(f32[2,48,384]{2,1,0:T(8,128)S(1)} %pad_maximum_fusion), channel_id=1, source_target_pairs={{0,64},{16,80},{32,96},{48,112},{64,0},{80,16},{96,32},{112,48},{1... | collective-permute-start | bytes 442376 | tf_op jit(solution)/shard_map/ppermute | solution.py:20
  124.4 18.9 %collective-permute-start.14 = (f32[2,48,384]{2,1,0:T(8,128)S(1)}, f32[2,48,384]{2,1,0:T(8,128)S(1)}, u32[]{:S(2)}, u32[]{:S(2)}) collective-permute-start(f32[2,48,384]{2,1,0:T(8,128)S(1)} %bitcast.32), channel_id=1, source_target_pairs={{0,192},{16,208},{32,224},{48,240},{64,128},{80,144},{96,160},{112... | collective-permute-start | bytes 442376 | tf_op jit(solution)/shard_map/ppermute | solution.py:20
  143.3 7.4 %collective-permute-start.16 = (f32[48,384]{1,0:T(8,128)S(1)}, f32[48,384]{1,0:T(8,128)S(1)}, u32[]{:S(2)}, u32[]{:S(2)}) collective-permute-start(f32[48,384]{1,0:T(8,128)S(1)} %fusion.6), channel_id=1, source_target_pairs={{0,192},{16,208},{32,224},{48,240},{64,128},{80,144},{96,160},{112... | collective-permute-start | bytes 221192 | tf_op jit(solution)/shard_map/ppermute | solution.py:20
  146.9 6.8 %collective-permute-start.17 = (f32[48,384]{1,0:T(8,128)S(1)}, f32[48,384]{1,0:T(8,128)S(1)}, u32[]{:S(2)}, u32[]{:S(2)}) collective-permute-start(f32[48,384]{1,0:T(8,128)S(1)} %fusion.5), channel_id=1, source_target_pairs={{0,64},{16,80},{32,96},{48,112},{64,0},{80,16},{96,32},{112,48},{1... | collective-permute-start | bytes 221192 | tf_op jit(solution)/shard_map/ppermute | solution.py:20

commit v8 on v6

v8 whole, which is shorter than its diff:
```python
import jax
import jax.numpy as jnp
from jax import lax
from jax.experimental import pallas as pl
from jax.experimental.pallas import tpu as pltpu
from jax.sharding import PartitionSpec as P

F32 = jnp.float32
BF16 = jnp.bfloat16
VMEM = pl.BlockSpec(memory_space=pltpu.VMEM)
SMEM = pl.BlockSpec(memory_space=pltpu.SMEM)
ORDER = (0, 1, 3, 2)


def swap_x(value, j):
    return lax.ppermute(value, "col", [(i, i ^ j) for i in range(16)])


def swap_y(value, j):
    return lax.ppermute(value, "col", [(i, i ^ (4 * j)) for i in range(16)])


def swap_row(value, j):
    return lax.ppermute(value, "row", [(i, i ^ j) for i in range(4)])


def encode(value):
    largest = jnp.max(jnp.max(jnp.abs(value), axis=1, keepdims=True), axis=0, keepdims=True)
    power = jnp.clip(jnp.ceil(jnp.log2(jnp.maximum(largest, 1e-30))), -100.0, 100.0)
    scaled = jnp.abs(value) * jnp.exp2(7.5 - power)
    for _ in range(4):
        scaled = scaled * scaled
    rows = jnp.broadcast_to(power, (16, value.shape[1]))
    return jnp.where(value < 0, -scaled, scaled).astype(BF16), rows.astype(BF16)


def decode(ref, start, size):
    tail = ref.shape[0] - 16
    power = ref[tail:, :].astype(F32)[:1, :1]
    code = ref[pl.ds(start, size), :].astype(F32)
    root = jnp.abs(code)
    for _ in range(4):
        root = jnp.sqrt(root)
    root = root * jnp.exp2(power - 7.5)
    return jnp.where(code < 0, -root, root)


def put(ref, value):
    coded, power = encode(value)
    ref[: value.shape[0], :] = coded
    ref[value.shape[0] :, :] = power


def spread(depth, chunks, block, into, place):
    parity = jnp.bitwise_and(depth, 1)
    for ref, own, lead in zip(chunks, (1, 0, 0), (0, 0, 4)):
        for k in range(ref.shape[0] // block):
            source = 2 * (lead + k) + (parity if own else 1 - parity)
            at = pl.multiple_of(place(source) * block, block)
            into[pl.ds(at, block), :] = ref[pl.ds(k * block, block), :]


def grad_inputs_kernel(place_ref, own, near, far, weight_ref, sent, kept, rows):
    block = own.shape[0] // 8

    def place(source):
        j = jnp.bitwise_xor(source, place_ref[1])
        jx, jy = jnp.bitwise_and(j, 3), jnp.right_shift(j, 2)
        slot = jnp.where(jx == 0, 2, jnp.where(jx == 3, 3, jx - 1))
        return slot * 4 + jnp.bitwise_xor(jy, jnp.right_shift(jy, 1))

    spread(place_ref[0], (own, near, far), block, rows, place)
    half = 8 * block
    for at, ref in ((0, sent), (half, kept)):
        part = lax.dot_general(
            rows[pl.ds(at, half), :],
            weight_ref[...],
            (((1,), (1,)), ((), ())),
            preferred_element_type=F32,
        )
        if at:
            ref[...] = part
        else:
            put(ref, part)


def x_stage_kernel(mine, got, sent, kept):
    size = mine.shape[0] // 2
    put(sent, mine[size:, :] + decode(got, size, size))
    kept[...] = mine[:size, :] + decode(got, 0, size)


def y_stage_kernel(mine, got, sent, kept):
    block = mine.shape[0] // 4
    total = mine[...] + decode(got, 0, mine.shape[0])
    put(sent, jnp.concatenate([total[block : 2 * block], total[3 * block :]]))
    kept[:block, :] = total[:block]
    kept[block:, :] = total[2 * block : 3 * block]


def last_stage_kernel(mine, got, sent, kept):
    block = mine.shape[0] // 2
    kept[...] = mine[:block, :] + decode(got, 0, block)
    sent[...] = mine[block:, :] + decode(got, block, block)


def finish_weight_kernel(mine, got, out):
    out[...] = (mine[...] + decode(got, 0, mine.shape[0])).astype(BF16)


def stage(kernel, sent, kept, *operands):
    return pl.pallas_call(
        kernel,
        out_shape=[sent, kept],
        in_specs=[VMEM] * len(operands),
        out_specs=[VMEM] * 2,
        compiler_params=pltpu.CompilerParams(vmem_limit_bytes=10 << 20),
    )(*operands)


def grad_weight_kernel(place_ref, _, own, near, far, tokens, sent, kept, grads, total):
    spread(place_ref[0], (own, near, far), own.shape[0] // 8, grads, lambda source: source)
    total[...] = lax.dot_general(
        tokens[...], grads[...], (((0,), (0,)), ((), ())), preferred_element_type=F32
    )
    rows = total.shape[0] // 4
    for jy in range(2):
        for jc, ref in ((1, sent), (0, kept)):
            source = jnp.bitwise_xor(place_ref[1], jy * 2 + jc) * rows
            ref[pl.ds((1 - jy) * rows, rows), :] = total[pl.ds(pl.multiple_of(source, rows), rows), :]


def sum_weight_kernel(mine, got, sent, kept):
    rows = kept.shape[0]
    put(sent, mine[:rows, :] + got[:rows, :])
    kept[...] = mine[rows:, :] + got[rows:, :]


def per_device(inputs, weight, grad_out):
    block, width = inputs.shape
    columns = weight.shape[1]
    tokens = block * 16
    depth, col, row = (lax.axis_index(a) for a in ("depth", "col", "row"))
    own = lax.all_gather(
        grad_out,
        "depth",
        axis=0,
        tiled=True,
        axis_index_groups=[list(range(parity, 16, 2)) for parity in range(2)],
    )
    near = lax.ppermute(own[: tokens // 4], "depth", [(i, i ^ 1) for i in range(16)])
    far = lax.ppermute(own[tokens // 4 :], "depth", [(i, ((i + 1) ^ 1) - 1 & 15) for i in range(16)])
    grads = (own, near, far)
    gathered = lax.all_gather(inputs, "col", axis=0, tiled=True)

    def plain(rows, cols=width):
        return jax.ShapeDtypeStruct((rows, cols), F32)

    def coded(rows, cols=width):
        return jax.ShapeDtypeStruct((rows + 16, cols), BF16)

    sent, kept = pl.pallas_call(
        grad_inputs_kernel,
        out_shape=[coded(tokens // 2), plain(tokens // 2)],
        in_specs=[SMEM] + [VMEM] * 4,
        out_specs=[VMEM] * 2,
        scratch_shapes=[pltpu.VMEM((tokens, columns), BF16)],
        compiler_params=pltpu.CompilerParams(vmem_limit_bytes=10 << 20),
        cost_estimate=pl.CostEstimate(
            flops=2 * tokens * width * columns, bytes_accessed=6 << 20, transcendentals=0
        ),
        name="grad_inputs",
    )(jnp.stack([depth, col]), *grads, weight)
    got = swap_x(sent, 1)
    sent, kept = stage(x_stage_kernel, coded(tokens // 4), plain(tokens // 4), kept, got)
    got = swap_x(sent, 3)

    send_w, keep_w = pl.pallas_call(
        grad_weight_kernel,
        out_shape=[plain(width // 2, columns)] * 2,
        in_specs=[SMEM, pl.BlockSpec(memory_space=pl.ANY)] + [VMEM] * 4,
        out_specs=[VMEM] * 2,
        scratch_shapes=[pltpu.VMEM((tokens, columns), BF16), pltpu.VMEM((width, columns), F32)],
        compiler_params=pltpu.CompilerParams(vmem_limit_bytes=9 << 20),
        cost_estimate=pl.CostEstimate(
            flops=2 * tokens * width * columns, bytes_accessed=7 << 20, transcendentals=0
        ),
        name="grad_weight",
    )(jnp.stack([depth, row]), got, *grads, gathered)
    rows = width // 4
    got_w = swap_row(send_w, 1)
    sent_w, kept_w = stage(sum_weight_kernel, coded(rows, columns), plain(rows, columns), keep_w, got_w)
    got_w = swap_row(sent_w, 2)

    sent, kept = stage(y_stage_kernel, coded(tokens // 8), plain(tokens // 8), kept, got)
    got = swap_y(sent, 1)
    sent, kept = stage(last_stage_kernel, plain(block), plain(block), kept, got)
    grad_inputs = (kept + swap_y(sent, 3)).astype(BF16)
    grad_weight = pl.pallas_call(
        finish_weight_kernel,
        out_shape=jax.ShapeDtypeStruct((rows, columns), BF16),
        in_specs=[VMEM] * 2,
        out_specs=VMEM,
        compiler_params=pltpu.CompilerParams(vmem_limit_bytes=10 << 20),
    )(kept_w, got_w)
    return grad_inputs, grad_weight


def solution(mesh):
    placed = (P(("row", "col"), "depth"), P("depth", "col"), P(("row", "depth"), "col"))
    return jax.shard_map(
        per_device,
        mesh=mesh,
        in_specs=placed,
        out_specs=(P(("row", "col"), "depth"), P(("depth", "row"), "col")),
        check_vma=False,
    )
```

time: 157 us -> 147 us (0.936)
  waiting for transfers between devices: 45.2 us -> 38.1 us
  Pallas kernels: 6.18 us -> 11.6 us
  starting transfers between devices: 41.4 us -> 37.3 us
  local copies, waits for them, and re-layouts: 4.91 us -> 2.26 us
    ppermute x4 -> x2, starting transfers between devices: 16.4 us -> 8.39 us  [swap_y(): return lax.ppermute(value, 'col', [(i, i ^ 4 * j) for i in range(16)])]
    ppermute x2, starting transfers between devices: 8.38 us -> 15.9 us  [swap_row(): return lax.ppermute(value, 'row', [(i, i ^ j) for i in range(4)])]
    pallas_call x2 -> x7, Pallas kernels: 6.18 us -> 11.6 us  [the longest x4 4.01 us: stage(): pl.pallas_call(kernel, out_shape=[sent, kept], in_specs=[VMEM] * len(oper...]
    all_gather x1, waiting for transfers between devices: 3.59 us -> 0.01 us  [per_device(): gathered = lax.all_gather(inputs, 'col', axis=0, tiled=True)]
    ppermute x4 -> x2, starting transfers between devices: 10.6 us -> 7.12 us  [swap_x(): return lax.ppermute(value, 'col', [(i, i ^ j) for i in range(16)])]
    unnamed x12 -> x4, local copies, waits for them, and re-layouts: 4.78 us -> 1.28 us
    ppermute x4 -> x2, waiting for transfers between devices: 18.4 us -> 15.4 us  [swap_x(): return lax.ppermute(value, 'col', [(i, i ^ j) for i in range(16)])]
    ppermute x4 -> x2, waiting for transfers between devices: 15.4 us -> 14.5 us  [swap_y(): return lax.ppermute(value, 'col', [(i, i ^ 4 * j) for i in range(16)])]
  transfers between devices with their start and end apart: 13 -> 9, of which waited for: 9 -> 6; matrix products, arithmetic and copies ran while one was open for 1% -> 1% of each run, Pallas kernels for 2% -> 5%
where the time goes in v8:
time: 147 us; the launch traced here: 146 us
  blocking collectives  42 us (29%)
  waiting for transfers between devices  38.1 us (26%)
  starting transfers between devices  37.3 us (25%)
  between operations  14.2 us (10%)
  Pallas kernels  11.6 us (8%)
  local copies, waits for them, and re-layouts  2.26 us (2%)
    all_gather x1, blocking collectives, per_device(): lax.all_gather(grad_out, 'depth', axis=0, tiled=True, axis_index_groups=[...  42 us
    ppermute x2, starting transfers between devices, swap_row(): return lax.ppermute(value, 'row', [(i, i ^ j) for i in range(4)])  15.9 us
    ppermute x2, waiting for transfers between devices, swap_x(): return lax.ppermute(value, 'col', [(i, i ^ j) for i in range(16)])  15.4 us
    ppermute x2, waiting for transfers between devices, swap_y(): return lax.ppermute(value, 'col', [(i, i ^ 4 * j) for i in range(16)])  14.5 us
    ppermute x2, starting transfers between devices, swap_y(): return lax.ppermute(value, 'col', [(i, i ^ 4 * j) for i in range(16)])  8.39 us
    ppermute x2, starting transfers between devices, swap_x(): return lax.ppermute(value, 'col', [(i, i ^ j) for i in range(16)])  7.12 us
    ppermute x1, waiting for transfers between devices, per_device(): lax.ppermute(own[tokens // 4:], 'depth', [(i, (i + 1 ^ 1) - 1 & 15) for i...  4.44 us
    pallas_call x4, Pallas kernels, stage(): pl.pallas_call(kernel, out_shape=[sent, kept], in_specs=[VMEM] * len(oper...  4.01 us
  transfers between devices with their start and end apart: 9, of which 6 were waited for; matrix products, arithmetic and copies ran while one was open for 1% of the time, Pallas kernels for 5%

profile of v8, /device:TPU:1, one launch (start us, length us, event | category | flops | bytes accessed | tf_op | source)
XLA Modules:
  0.0 146.2 jit_solution(12673377658411545279)
XLA Ops:
  7.2 0.7 all-gather.2.cloned.1.call-update
  7.9 42.0 %all_gather.6.own = bf16[384,1152]{1,0:T(8,128)(2,1)S(1)} all-gather(bf16[48,1152]{1,0:T(8,128)(2,1)} %param.5), channel_id=1, replica_groups={{0,2,4,6,8,10,12,14},{1,3,5,7,9,11,13,15},{16,18,20,22,24,26,28,30},{17..., dimensions={0}, use_global_device_ids=true | all-gather | bytes 995328 | tf_op jit(solution)/shard_map/all_gather | solution.py:144
  49.9 1.0 fusion
  50.9 4.0 %collective-permute-start.1 = (bf16[192,1152]{1,0:T(8,128)(2,1)}, bf16[192,1152]{1,0:T(8,128)(2,1)S(1)}, u32[]{:S(2)}, u32[]{:S(2)}) collective-permute-start(bf16[192,1152]{1,0:T(8,128)(2,1)} %get-tuple-element.26), channel_id=1, source_target_pairs={{0,15},{1,2},{2,1},{3,4},{4,3},{5,6},{6,5},{7,8},{8,7},{9,10},{10,... | collective-permute-start | bytes 1327112 | tf_op jit(solution)/shard_map/ppermute | solution.py:152
  54.9 1.9 %collective-permute-start = (bf16[192,1152]{1,0:T(8,128)(2,1)}, bf16[192,1152]{1,0:T(8,128)(2,1)S(1)}, u32[]{:S(2)}, u32[]{:S(2)}) collective-permute-start(bf16[192,1152]{1,0:T(8,128)(2,1)} %get-tuple-element.27), channel_id=1, source_target_pairs={{0,1},{1,0},{2,3},{3,2},{4,5},{5,4},{6,7},{7,6},{8,9},{9,8},{10,11... | collective-permute-start | bytes 1327112 | tf_op jit(solution)/shard_map/ppermute | solution.py:151
  56.9 4.4 %collective-permute-done.1.far = bf16[192,1152]{1,0:T(8,128)(2,1)S(1)} collective-permute-done((bf16[192,1152]{1,0:T(8,128)(2,1)}, bf16[192,1152]{1,0:T(8,128)(2,1)S(1)}, u32[]{:S(2)}, u32[]{:S(2)}) %collective-permute-start.1) | collective-permute-done | bytes 442400 | tf_op jit(solution)/shard_map/ppermute | solution.py:152
  61.3 3.1 %collective-permute-done.near = bf16[192,1152]{1,0:T(8,128)(2,1)S(1)} collective-permute-done((bf16[192,1152]{1,0:T(8,128)(2,1)}, bf16[192,1152]{1,0:T(8,128)(2,1)S(1)}, u32[]{:S(2)}, u32[]{:S(2)}) %collective-permute-start) | collective-permute-done | bytes 442400 | tf_op jit(solution)/shard_map/ppermute | solution.py:151
  64.4 2.9 %grad_inputs.1 = (bf16[400,768]{1,0:T(8,128)(2,1)S(1)}, f32[384,768]{1,0:T(8,128)S(1)}) custom-call(s32[2]{0:T(128)S(1)} %pad_add_fusion.place_ref, bf16[384,1152]{1,0:T(8,128)(2,1)S(1)} %all_gather.6.own, bf16[192,1152]{1,0:T(8,128)(2,1)S(1)} %collective-permute-done.near, bf16[192,1152]{1,0:T(8,128)(2,1)S(1)} %collective-permute-done.1.far, ...), custom_call_target="tpu_custom_call" | custom-call | flops 1358954496 | bytes 6291456 | tf_op jit(solution)/shard_map/grad_inputs/pallas_call | solution.py:162
  67.4 2.9 %collective-permute-start.2 = (bf16[400,768]{1,0:T(8,128)(2,1)S(1)}, bf16[400,768]{1,0:T(8,128)(2,1)S(1)}, u32[]{:S(2)}, u32[]{:S(2)}) collective-permute-start(bf16[400,768]{1,0:T(8,128)(2,1)S(1)} %get-tuple-element.15), channel_id=1, source_target_pairs={{0,16},{16,0},{32,48},{48,32},{64,80},{80,64},{96,112},{112,96},{1... | collective-permute-start | bytes 1843208 | tf_op jit(solution)/shard_map/ppermute | solution.py:16
  70.3 10.0 %collective-permute-done.2.got = bf16[400,768]{1,0:T(8,128)(2,1)S(1)} collective-permute-done((bf16[400,768]{1,0:T(8,128)(2,1)S(1)}, bf16[400,768]{1,0:T(8,128)(2,1)S(1)}, u32[]{:S(2)}, u32[]{:S(2)}) %collective-permute-start.2) | collective-permute-done | bytes 614432 | tf_op jit(solution)/shard_map/ppermute | solution.py:16
  80.3 2.0 %shard_map.50 = (bf16[208,768]{1,0:T(8,128)(2,1)S(1)}, f32[192,768]{1,0:T(8,128)S(1)}) custom-call(f32[384,768]{1,0:T(8,128)S(1)} %get-tuple-element.14.mine, bf16[400,768]{1,0:T(8,128)(2,1)S(1)} %collective-permute-done.2.got), custom_call_target="tpu_custom_call" | custom-call | tf_op jit(solution)/shard_map/pallas_call | solution.py:112
  82.2 4.3 %collective-permute-start.3 = (bf16[208,768]{1,0:T(8,128)(2,1)S(1)}, bf16[208,768]{1,0:T(8,128)(2,1)S(1)}, u32[]{:S(2)}, u32[]{:S(2)}) collective-permute-start(bf16[208,768]{1,0:T(8,128)(2,1)S(1)} %get-tuple-element.17), channel_id=1, source_target_pairs={{0,48},{16,32},{32,16},{48,0},{64,112},{80,96},{96,80},{112,64},{1... | collective-permute-start | bytes 958472 | tf_op jit(solution)/shard_map/ppermute | solution.py:16
  86.6 5.4 %collective-permute-done.3.got._ = bf16[208,768]{1,0:T(8,128)(2,1)S(1)} collective-permute-done((bf16[208,768]{1,0:T(8,128)(2,1)S(1)}, bf16[208,768]{1,0:T(8,128)(2,1)S(1)}, u32[]{:S(2)}, u32[]{:S(2)}) %collective-permute-start.3) | collective-permute-done | bytes 319520 | tf_op jit(solution)/shard_map/ppermute | solution.py:16
  91.9 1.3 copy-done.1
  93.2 2.6 %grad_weight.1 = (f32[384,1152]{1,0:T(8,128)S(1)}, f32[384,1152]{1,0:T(8,128)S(1)}) custom-call(s32[2]{0:T(128)S(1)} %pad_add_fusion.1.place_ref, bf16[208,768]{1,0:T(8,128)(2,1)S(1)} %collective-permute-done.3.got._, bf16[384,1152]{1,0:T(8,128)(2,1)S(1)} %all_gather.6.own, bf16[192,1152]{1,0:T(8,128)(2,1)S(1)} %collective-permute-done.near, ...), custom_call_target="tpu_custom_call" | custom-call | flops 1358954496 | bytes 7340032 | tf_op jit(solution)/shard_map/grad_weight/pallas_call | solution.py:178
  95.8 12.7 %collective-permute-start.6 = (f32[384,1152]{1,0:T(8,128)S(1)}, f32[384,1152]{1,0:T(8,128)S(1)}, u32[]{:S(2)}, u32[]{:S(2)}) collective-permute-start(f32[384,1152]{1,0:T(8,128)S(1)} %get-tuple-element.23), channel_id=1, source_target_pairs={{0,256},{256,0},{512,768},{768,512},{1,257},{257,1},{513,769},{769... | collective-permute-start | bytes 5308424 | tf_op jit(solution)/shard_map/ppermute | solution.py:24
  108.5 0.9 shard_map.51
  109.4 4.4 %collective-permute-start.4 = (bf16[112,768]{1,0:T(8,128)(2,1)S(1)}, bf16[112,768]{1,0:T(8,128)(2,1)S(1)}, u32[]{:S(2)}, u32[]{:S(2)}) collective-permute-start(bf16[112,768]{1,0:T(8,128)(2,1)S(1)} %get-tuple-element.19), channel_id=1, source_target_pairs={{0,64},{16,80},{32,96},{48,112},{64,0},{80,16},{96,32},{112,48},{1... | collective-permute-start | bytes 516104 | tf_op jit(solution)/shard_map/ppermute | solution.py:20
  113.8 0.8 shard_map.53
  114.6 3.2 %collective-permute-start.7 = (bf16[208,1152]{1,0:T(8,128)(2,1)S(1)}, bf16[208,1152]{1,0:T(8,128)(2,1)S(1)}, u32[]{:S(2)}, u32[]{:S(2)}) collective-permute-start(bf16[208,1152]{1,0:T(8,128)(2,1)S(1)} %get-tuple-element.25), channel_id=1, source_target_pairs={{0,512},{256,768},{512,0},{768,256},{1,513},{257,769},{513,1},{769... | collective-permute-start | bytes 1437704 | tf_op jit(solution)/shard_map/ppermute | solution.py:24
  117.8 4.3 %collective-permute-done.4.got = bf16[112,768]{1,0:T(8,128)(2,1)S(1)} collective-permute-done((bf16[112,768]{1,0:T(8,128)(2,1)S(1)}, bf16[112,768]{1,0:T(8,128)(2,1)S(1)}, u32[]{:S(2)}, u32[]{:S(2)}) %collective-permute-start.4) | collective-permute-done | bytes 172064 | tf_op jit(solution)/shard_map/ppermute | solution.py:20
  122.6 4.0 %collective-permute-start.5 = (f32[48,768]{1,0:T(8,128)S(1)}, f32[48,768]{1,0:T(8,128)S(1)}, u32[]{:S(2)}, u32[]{:S(2)}) collective-permute-start(f32[48,768]{1,0:T(8,128)S(1)} %get-tuple-element.21), channel_id=1, source_target_pairs={{0,192},{16,208},{32,224},{48,240},{64,128},{80,144},{96,160},{112... | collective-permute-start | bytes 442376 | tf_op jit(solution)/shard_map/ppermute | solution.py:20
  126.5 10.1 %collective-permute-done.5 = f32[48,768]{1,0:T(8,128)S(1)} collective-permute-done((f32[48,768]{1,0:T(8,128)S(1)}, f32[48,768]{1,0:T(8,128)S(1)}, u32[]{:S(2)}, u32[]{:S(2)}) %collective-permute-start.5) | collective-permute-done | bytes 147488 | tf_op jit(solution)/shard_map/ppermute | solution.py:20
  137.3 2.1 %shard_map.54 = bf16[192,1152]{1,0:T(8,128)(2,1)} custom-call(f32[192,1152]{1,0:T(8,128)S(1)} %get-tuple-element.24.mine, bf16[208,1152]{1,0:T(8,128)(2,1)S(1)} %collective-permute-done.7.got), custom_call_target="tpu_custom_call" | custom-call | tf_op jit(solution)/shard_map/pallas_call | solution.py:199
  (11 shorter events, 1.2 us)
Async XLA Ops:
  7.2 57.3 %copy-start = (bf16[768,1152]{1,0:T(8,128)(2,1)S(1)}, bf16[768,1152]{1,0:T(8,128)(2,1)}, u32[]{:S(2)}) copy-start(bf16[768,1152]{1,0:T(8,128)(2,1)} %weight_ref.1) | copy-start | bytes 5308420
  7.2 84.8 %all-gather.2.cloned.1.call-start = ((), (), s32[]{:S(2)}) async-start(), calls=%async_computation | async-start | bytes 1253376 | tf_op jit(solution)/shard_map/all_gather | solution.py:154
  50.9 10.5 %collective-permute-start.1 = (bf16[192,1152]{1,0:T(8,128)(2,1)}, bf16[192,1152]{1,0:T(8,128)(2,1)S(1)}, u32[]{:S(2)}, u32[]{:S(2)}) collective-permute-start(bf16[192,1152]{1,0:T(8,128)(2,1)} %get-tuple-element.26), channel_id=1, source_target_pairs={{0,15},{1,2},{2,1},{3,4},{4,3},{5,6},{6,5},{7,8},{8,7},{9,10},{10,... | collective-permute-start | bytes 1327112 | tf_op jit(solution)/shard_map/ppermute | solution.py:152
  54.9 9.6 %collective-permute-start = (bf16[192,1152]{1,0:T(8,128)(2,1)}, bf16[192,1152]{1,0:T(8,128)(2,1)S(1)}, u32[]{:S(2)}, u32[]{:S(2)}) collective-permute-start(bf16[192,1152]{1,0:T(8,128)(2,1)} %get-tuple-element.27), channel_id=1, source_target_pairs={{0,1},{1,0},{2,3},{3,2},{4,5},{5,4},{6,7},{7,6},{8,9},{9,8},{10,11... | collective-permute-start | bytes 1327112 | tf_op jit(solution)/shard_map/ppermute | solution.py:151
  67.4 12.9 %collective-permute-start.2 = (bf16[400,768]{1,0:T(8,128)(2,1)S(1)}, bf16[400,768]{1,0:T(8,128)(2,1)S(1)}, u32[]{:S(2)}, u32[]{:S(2)}) collective-permute-start(bf16[400,768]{1,0:T(8,128)(2,1)S(1)} %get-tuple-element.15), channel_id=1, source_target_pairs={{0,16},{16,0},{32,48},{48,32},{64,80},{80,64},{96,112},{112,96},{1... | collective-permute-start | bytes 1843208 | tf_op jit(solution)/shard_map/ppermute | solution.py:16
  82.2 9.7 %collective-permute-start.3 = (bf16[208,768]{1,0:T(8,128)(2,1)S(1)}, bf16[208,768]{1,0:T(8,128)(2,1)S(1)}, u32[]{:S(2)}, u32[]{:S(2)}) collective-permute-start(bf16[208,768]{1,0:T(8,128)(2,1)S(1)} %get-tuple-element.17), channel_id=1, source_target_pairs={{0,48},{16,32},{32,16},{48,0},{64,112},{80,96},{96,80},{112,64},{1... | collective-permute-start | bytes 958472 | tf_op jit(solution)/shard_map/ppermute | solution.py:16
  91.9 1.3 copy-start.1
  95.8 18.0 %collective-permute-start.6 = (f32[384,1152]{1,0:T(8,128)S(1)}, f32[384,1152]{1,0:T(8,128)S(1)}, u32[]{:S(2)}, u32[]{:S(2)}) collective-permute-start(f32[384,1152]{1,0:T(8,128)S(1)} %get-tuple-element.23), channel_id=1, source_target_pairs={{0,256},{256,0},{512,768},{768,512},{1,257},{257,1},{513,769},{769... | collective-permute-start | bytes 5308424 | tf_op jit(solution)/shard_map/ppermute | solution.py:24
  109.4 12.7 %collective-permute-start.4 = (bf16[112,768]{1,0:T(8,128)(2,1)S(1)}, bf16[112,768]{1,0:T(8,128)(2,1)S(1)}, u32[]{:S(2)}, u32[]{:S(2)}) collective-permute-start(bf16[112,768]{1,0:T(8,128)(2,1)S(1)} %get-tuple-element.19), channel_id=1, source_target_pairs={{0,64},{16,80},{32,96},{48,112},{64,0},{80,16},{96,32},{112,48},{1... | collective-permute-start | bytes 516104 | tf_op jit(solution)/shard_map/ppermute | solution.py:20
  114.6 22.7 %collective-permute-start.7 = (bf16[208,1152]{1,0:T(8,128)(2,1)S(1)}, bf16[208,1152]{1,0:T(8,128)(2,1)S(1)}, u32[]{:S(2)}, u32[]{:S(2)}) collective-permute-start(bf16[208,1152]{1,0:T(8,128)(2,1)S(1)} %get-tuple-element.25), channel_id=1, source_target_pairs={{0,512},{256,768},{512,0},{768,256},{1,513},{257,769},{513,1},{769... | collective-permute-start | bytes 1437704 | tf_op jit(solution)/shard_map/ppermute | solution.py:24
  122.6 14.1 %collective-permute-start.5 = (f32[48,768]{1,0:T(8,128)S(1)}, f32[48,768]{1,0:T(8,128)S(1)}, u32[]{:S(2)}, u32[]{:S(2)}) collective-permute-start(f32[48,768]{1,0:T(8,128)S(1)} %get-tuple-element.21), channel_id=1, source_target_pairs={{0,192},{16,208},{32,224},{48,240},{64,128},{80,144},{96,160},{112... | collective-permute-start | bytes 442376 | tf_op jit(solution)/shard_map/ppermute | solution.py:20
Sparse Core Ops, SparseCore 0:
  12.2 78.4 all-gather.1

commit v9 on v8

--- a/solution.py
+++ b/solution.py
@@ -118,15 +118,17 @@
     )(*operands)
 
 
-def grad_weight_kernel(place_ref, _, own, near, far, tokens, sent, kept, grads, total):
-    spread(place_ref[0], (own, near, far), own.shape[0] // 8, grads, lambda source: source)
+def grad_weight_kernel(row_ref, _, grads, near, far, sent, kept, tokens, total):
+    quarter = near.shape[0] // 2
+    for slot, (ref, at) in enumerate(((near, quarter), (far, quarter), (near, 0), (far, 0))):
+        tokens[pl.ds(slot * quarter, quarter), :] = ref[pl.ds(at, quarter), :]
     total[...] = lax.dot_general(
         tokens[...], grads[...], (((0,), (0,)), ((), ())), preferred_element_type=F32
     )
     rows = total.shape[0] // 4
     for jy in range(2):
         for jc, ref in ((1, sent), (0, kept)):
-            source = jnp.bitwise_xor(place_ref[1], jy * 2 + jc) * rows
+            source = jnp.bitwise_xor(row_ref[0], jy * 2 + jc) * rows
             ref[pl.ds((1 - jy) * rows, rows), :] = total[pl.ds(pl.multiple_of(source, rows), rows), :]
 
 
@@ -141,6 +143,7 @@
     columns = weight.shape[1]
     tokens = block * 16
     depth, col, row = (lax.axis_index(a) for a in ("depth", "col", "row"))
+    ring = [inputs] + [swap_y(inputs, j) for j in ORDER[1:]]
     own = lax.all_gather(
         grad_out,
         "depth",
@@ -151,7 +154,9 @@
     near = lax.ppermute(own[: tokens // 4], "depth", [(i, i ^ 1) for i in range(16)])
     far = lax.ppermute(own[tokens // 4 :], "depth", [(i, ((i + 1) ^ 1) - 1 & 15) for i in range(16)])
     grads = (own, near, far)
-    gathered = lax.all_gather(inputs, "col", axis=0, tiled=True)
+    along_y = jnp.concatenate(ring)
+    near_in = jnp.concatenate([along_y, swap_x(along_y, 1)])
+    far_in = swap_x(near_in, 3)
 
     def plain(rows, cols=width):
         return jax.ShapeDtypeStruct((rows, cols), F32)
@@ -159,12 +164,11 @@
     def coded(rows, cols=width):
         return jax.ShapeDtypeStruct((rows + 16, cols), BF16)
 
-    sent, kept = pl.pallas_call(
+    sent, kept, ordered = pl.pallas_call(
         grad_inputs_kernel,
-        out_shape=[coded(tokens // 2), plain(tokens // 2)],
+        out_shape=[coded(tokens // 2), plain(tokens // 2), jax.ShapeDtypeStruct((tokens, columns), BF16)],
         in_specs=[SMEM] + [VMEM] * 4,
-        out_specs=[VMEM] * 2,
-        scratch_shapes=[pltpu.VMEM((tokens, columns), BF16)],
+        out_specs=[VMEM] * 3,
         compiler_params=pltpu.CompilerParams(vmem_limit_bytes=10 << 20),
         cost_estimate=pl.CostEstimate(
             flops=2 * tokens * width * columns, bytes_accessed=6 << 20, transcendentals=0
@@ -178,15 +182,15 @@
     send_w, keep_w = pl.pallas_call(
         grad_weight_kernel,
         out_shape=[plain(width // 2, columns)] * 2,
-        in_specs=[SMEM, pl.BlockSpec(memory_space=pl.ANY)] + [VMEM] * 4,
+        in_specs=[SMEM, pl.BlockSpec(memory_space=pl.ANY)] + [VMEM] * 3,
         out_specs=[VMEM] * 2,
-        scratch_shapes=[pltpu.VMEM((tokens, columns), BF16), pltpu.VMEM((width, columns), F32)],
+        scratch_shapes=[pltpu.VMEM((tokens, width), BF16), pltpu.VMEM((width, columns), F32)],
         compiler_params=pltpu.CompilerParams(vmem_limit_bytes=9 << 20),
         cost_estimate=pl.CostEstimate(
             flops=2 * tokens * width * columns, bytes_accessed=7 << 20, transcendentals=0
         ),
         name="grad_weight",
-    )(jnp.stack([depth, row]), got, *grads, gathered)
+    )(row.reshape(1), got, ordered, near_in, far_in)
     rows = width // 4
     got_w = swap_row(send_w, 1)
     sent_w, kept_w = stage(sum_weight_kernel, coded(rows, columns), plain(rows, columns), keep_w, got_w)

time: 147 us -> 140 us (0.952)
  starting transfers between devices: 37.3 us -> 52.2 us
  between operations: 14.2 us -> 0.89 us
  waiting for transfers between devices: 38.1 us -> 31.1 us
  blocking collectives: 42 us -> 38.8 us
    ppermute x2 -> x5, starting transfers between devices: 8.39 us -> 21.3 us  [swap_y(): return lax.ppermute(value, 'col', [(i, i ^ 4 * j) for i in range(16)])]
    ppermute x2 -> x4, starting transfers between devices: 7.12 us -> 12.6 us  [swap_x(): return lax.ppermute(value, 'col', [(i, i ^ j) for i in range(16)])]
    ppermute x2, starting transfers between devices: 15.9 us -> 10.4 us  [swap_row(): return lax.ppermute(value, 'row', [(i, i ^ j) for i in range(4)])]
    ppermute x1, waiting for transfers between devices: 4.44 us -> 0.01 us  [per_device(): lax.ppermute(own[tokens // 4:], 'depth', [(i, (i + 1 ^ 1) - 1 & 15) for i...]
    all_gather x1, blocking collectives: 42 us -> 38.8 us  [per_device(): lax.all_gather(grad_out, 'depth', axis=0, tiled=True, axis_index_groups=[...]
    ppermute x2 -> x4, waiting for transfers between devices: 15.4 us -> 13.3 us  [swap_x(): return lax.ppermute(value, 'col', [(i, i ^ j) for i in range(16)])]
    ppermute x1, starting transfers between devices: 4 us -> 5.89 us  [per_device(): lax.ppermute(own[tokens // 4:], 'depth', [(i, (i + 1 ^ 1) - 1 & 15) for i...]
    ppermute x2 -> x5, waiting for transfers between devices: 14.5 us -> 14.4 us  [swap_y(): return lax.ppermute(value, 'col', [(i, i ^ 4 * j) for i in range(16)])]
  transfers between devices with their start and end apart: 9 -> 13, of which waited for: 6 -> 5; matrix products, arithmetic and copies ran while one was open for 1% -> 3% of each run, Pallas kernels for 5% -> 5%
where the time goes in v9:
time: 140 us
  starting transfers between devices  52.2 us (37%)
  blocking collectives  38.8 us (28%)
  waiting for transfers between devices  31.1 us (22%)
  Pallas kernels  11.7 us (8%)
  local copies, waits for them, and re-layouts  3.41 us (2%)
  other arithmetic  1.63 us (1%)
    all_gather x1, blocking collectives, per_device(): lax.all_gather(grad_out, 'depth', axis=0, tiled=True, axis_index_groups=[...  38.8 us
    ppermute x5, starting transfers between devices, swap_y(): return lax.ppermute(value, 'col', [(i, i ^ 4 * j) for i in range(16)])  21.3 us
    ppermute x5, waiting for transfers between devices, swap_y(): return lax.ppermute(value, 'col', [(i, i ^ 4 * j) for i in range(16)])  14.4 us
    ppermute x4, waiting for transfers between devices, swap_x(): return lax.ppermute(value, 'col', [(i, i ^ j) for i in range(16)])  13.3 us
    ppermute x4, starting transfers between devices, swap_x(): return lax.ppermute(value, 'col', [(i, i ^ j) for i in range(16)])  12.6 us
    ppermute x2, starting transfers between devices, swap_row(): return lax.ppermute(value, 'row', [(i, i ^ j) for i in range(4)])  10.4 us
    ppermute x1, starting transfers between devices, per_device(): lax.ppermute(own[tokens // 4:], 'depth', [(i, (i + 1 ^ 1) - 1 & 15) for i...  5.89 us
    pallas_call x4, Pallas kernels, stage(): pl.pallas_call(kernel, out_shape=[sent, kept], in_specs=[VMEM] * len(oper...  4.01 us
  transfers between devices with their start and end apart: 13, of which 5 were waited for; matrix products, arithmetic and copies ran while one was open for 3% of the time, Pallas kernels for 5%

profile of v9, /device:TPU:1, one launch (start us, length us, event | category | flops | bytes accessed | tf_op | source)
XLA Modules:
  0.0 139.7 jit_solution(17698842022812845237)
XLA Ops:
  0.6 8.4 %collective-permute-start.8 = (bf16[48,768]{1,0:T(8,128)(2,1)}, bf16[48,768]{1,0:T(8,128)(2,1)S(1)}, u32[]{:S(2)}, u32[]{:S(2)}) collective-permute-start(bf16[48,768]{1,0:T(8,128)(2,1)} %param.3), channel_id=1, source_target_pairs={{0,128},{16,144},{32,160},{48,176},{64,192},{80,208},{96,224},{112... | collective-permute-start | bytes 221192 | tf_op jit(solution)/shard_map/ppermute | solution.py:20
  9.1 2.0 %collective-permute-start.7 = (bf16[48,768]{1,0:T(8,128)(2,1)}, bf16[48,768]{1,0:T(8,128)(2,1)S(1)}, u32[]{:S(2)}, u32[]{:S(2)}) collective-permute-start(bf16[48,768]{1,0:T(8,128)(2,1)} %param.3), channel_id=1, source_target_pairs={{0,192},{16,208},{32,224},{48,240},{64,128},{80,144},{96,160},{112... | collective-permute-start | bytes 221192 | tf_op jit(solution)/shard_map/ppermute | solution.py:20
  11.0 2.4 %collective-permute-start.6 = (bf16[48,768]{1,0:T(8,128)(2,1)}, bf16[48,768]{1,0:T(8,128)(2,1)}, u32[]{:S(2)}, u32[]{:S(2)}) collective-permute-start(bf16[48,768]{1,0:T(8,128)(2,1)} %param.3), channel_id=1, source_target_pairs={{0,64},{16,80},{32,96},{48,112},{64,0},{80,16},{96,32},{112,48},{1... | collective-permute-start | bytes 221192 | tf_op jit(solution)/shard_map/ppermute | solution.py:20
  13.4 38.8 %all_gather.3.own = bf16[384,1152]{1,0:T(8,128)(2,1)S(1)} all-gather(bf16[48,1152]{1,0:T(8,128)(2,1)} %param.5), channel_id=1, replica_groups={{0,2,4,6,8,10,12,14},{1,3,5,7,9,11,13,15},{16,18,20,22,24,26,28,30},{17..., dimensions={0}, use_global_device_ids=true | all-gather | bytes 995328 | tf_op jit(solution)/shard_map/all_gather | solution.py:147
  53.3 5.9 %collective-permute-start.1 = (bf16[192,1152]{1,0:T(8,128)(2,1)}, bf16[192,1152]{1,0:T(8,128)(2,1)}, u32[]{:S(2)}, u32[]{:S(2)}) collective-permute-start(bf16[192,1152]{1,0:T(8,128)(2,1)} %get-tuple-element.28), channel_id=1, source_target_pairs={{0,15},{1,2},{2,1},{3,4},{4,3},{5,6},{6,5},{7,8},{8,7},{9,10},{10,... | collective-permute-start | bytes 1327112 | tf_op jit(solution)/shard_map/ppermute | solution.py:155
  59.2 1.9 %collective-permute-start = (bf16[192,1152]{1,0:T(8,128)(2,1)}, bf16[192,1152]{1,0:T(8,128)(2,1)}, u32[]{:S(2)}, u32[]{:S(2)}) collective-permute-start(bf16[192,1152]{1,0:T(8,128)(2,1)} %get-tuple-element.29), channel_id=1, source_target_pairs={{0,1},{1,0},{2,3},{3,2},{4,5},{5,4},{6,7},{7,6},{8,9},{9,8},{10,11... | collective-permute-start | bytes 1327112 | tf_op jit(solution)/shard_map/ppermute | solution.py:154
  62.1 2.4 %collective-permute-start.9 = (bf16[192,768]{1,0:T(8,128)(2,1)S(1)}, bf16[192,768]{1,0:T(8,128)(2,1)S(1)}, u32[]{:S(2)}, u32[]{:S(2)}) collective-permute-start(bf16[192,768]{1,0:T(8,128)(2,1)S(1)} %pad_maximum_fusion), channel_id=1, source_target_pairs={{0,16},{16,0},{32,48},{48,32},{64,80},{80,64},{96,112},{112,96},{1... | collective-permute-start | bytes 884744 | tf_op jit(solution)/shard_map/ppermute | solution.py:16
  65.4 3.4 %collective-permute-done.near = bf16[192,1152]{1,0:T(8,128)(2,1)} collective-permute-done((bf16[192,1152]{1,0:T(8,128)(2,1)}, bf16[192,1152]{1,0:T(8,128)(2,1)}, u32[]{:S(2)}, u32[]{:S(2)}) %collective-permute-start) | collective-permute-done | bytes 442400 | tf_op jit(solution)/shard_map/ppermute | solution.py:154
  68.8 3.6 %grad_inputs.1 = (bf16[400,768]{1,0:T(8,128)(2,1)S(1)}, f32[384,768]{1,0:T(8,128)S(1)}, bf16[768,1152]{1,0:T(8,128)(2,1)S(1)}) custom-call(s32[2]{0:T(128)S(1)} %pad_add_fusion.place_ref, bf16[384,1152]{1,0:T(8,128)(2,1)S(1)} %all_gather.3.own, bf16[192,1152]{1,0:T(8,128)(2,1)} %collective-permute-done.near, bf16[192,1152]{1,0:T(8,128)(2,1)} %collective-permute-done.1.far, ...), custom_call_target="tpu_custom_call" | custom-call | flops 1358954496 | bytes 6291456 | tf_op jit(solution)/shard_map/grad_inputs/pallas_call | solution.py:167
  72.5 2.4 %collective-permute-start.2 = (bf16[400,768]{1,0:T(8,128)(2,1)S(1)}, bf16[400,768]{1,0:T(8,128)(2,1)S(1)}, u32[]{:S(2)}, u32[]{:S(2)}) collective-permute-start(bf16[400,768]{1,0:T(8,128)(2,1)S(1)} %get-tuple-element.16), channel_id=1, source_target_pairs={{0,16},{16,0},{32,48},{48,32},{64,80},{80,64},{96,112},{112,96},{1... | collective-permute-start | bytes 1843208 | tf_op jit(solution)/shard_map/ppermute | solution.py:16
  75.0 3.7 %collective-permute-start.10 = (bf16[384,768]{1,0:T(8,128)(2,1)S(1)}, bf16[384,768]{1,0:T(8,128)(2,1)S(1)}, u32[]{:S(2)}, u32[]{:S(2)}) collective-permute-start(bf16[384,768]{1,0:T(8,128)(2,1)S(1)} %constant_dynamic-update-slice_fusion.near), channel_id=1, source_target_pairs={{0,48},{16,32},{32,16},{48,0},{64,112},{80,96},{96,80},{112,64},{1... | collective-permute-start | bytes 1769480 | tf_op jit(solution)/shard_map/ppermute | solution.py:16
  78.7 4.7 %collective-permute-done.2.got = bf16[400,768]{1,0:T(8,128)(2,1)S(1)} collective-permute-done((bf16[400,768]{1,0:T(8,128)(2,1)S(1)}, bf16[400,768]{1,0:T(8,128)(2,1)S(1)}, u32[]{:S(2)}, u32[]{:S(2)}) %collective-permute-start.2) | collective-permute-done | bytes 614432 | tf_op jit(solution)/shard_map/ppermute | solution.py:16
  83.4 2.0 %shard_map.50 = (bf16[208,768]{1,0:T(8,128)(2,1)S(1)}, f32[192,768]{1,0:T(8,128)S(1)}) custom-call(f32[384,768]{1,0:T(8,128)S(1)} %get-tuple-element.15.mine, bf16[400,768]{1,0:T(8,128)(2,1)S(1)} %collective-permute-done.2.got), custom_call_target="tpu_custom_call" | custom-call | tf_op jit(solution)/shard_map/pallas_call | solution.py:112
  85.3 4.1 %collective-permute-start.3 = (bf16[208,768]{1,0:T(8,128)(2,1)S(1)}, bf16[208,768]{1,0:T(8,128)(2,1)S(1)}, u32[]{:S(2)}, u32[]{:S(2)}) collective-permute-start(bf16[208,768]{1,0:T(8,128)(2,1)S(1)} %get-tuple-element.18), channel_id=1, source_target_pairs={{0,48},{16,32},{32,16},{48,0},{64,112},{80,96},{96,80},{112,64},{1... | collective-permute-start | bytes 958472 | tf_op jit(solution)/shard_map/ppermute | solution.py:16
  89.4 8.6 %collective-permute-done.3.got._ = bf16[208,768]{1,0:T(8,128)(2,1)S(1)} collective-permute-done((bf16[208,768]{1,0:T(8,128)(2,1)S(1)}, bf16[208,768]{1,0:T(8,128)(2,1)S(1)}, u32[]{:S(2)}, u32[]{:S(2)}) %collective-permute-start.3) | collective-permute-done | bytes 319520 | tf_op jit(solution)/shard_map/ppermute | solution.py:16
  98.0 1.5 %copy-done.2 = bf16[768,1152]{1,0:T(8,128)(2,1)S(1)} copy-done((bf16[768,1152]{1,0:T(8,128)(2,1)S(1)}, bf16[768,1152]{1,0:T(8,128)(2,1)}, u32[]{:S(2)}) %copy-start.2) | copy-done | bytes 1769496
  99.5 2.0 %grad_weight.1 = (f32[384,1152]{1,0:T(8,128)S(1)}, f32[384,1152]{1,0:T(8,128)S(1)}) custom-call(s32[1]{0:T(128)} %bitcast.2.row_ref, bf16[208,768]{1,0:T(8,128)(2,1)S(1)} %collective-permute-done.3.got._, bf16[768,1152]{1,0:T(8,128)(2,1)S(1)} %copy-done.2, bf16[384,768]{1,0:T(8,128)(2,1)S(1)} %constant_dynamic-update-slice_fusion.near, ...), custom_call_target="tpu_custom_call" | custom-call | flops 1358954496 | bytes 7340032 | tf_op jit(solution)/shard_map/grad_weight/pallas_call | solution.py:182
  101.5 7.2 %collective-permute-start.11 = (f32[384,1152]{1,0:T(8,128)S(1)}, f32[384,1152]{1,0:T(8,128)S(1)}, u32[]{:S(2)}, u32[]{:S(2)}) collective-permute-start(f32[384,1152]{1,0:T(8,128)S(1)} %get-tuple-element.25), channel_id=1, source_target_pairs={{0,256},{256,0},{512,768},{768,512},{1,257},{257,1},{513,769},{769... | collective-permute-start | bytes 5308424 | tf_op jit(solution)/shard_map/ppermute | solution.py:24
  109.6 4.0 %collective-permute-start.4 = (bf16[112,768]{1,0:T(8,128)(2,1)S(1)}, bf16[112,768]{1,0:T(8,128)(2,1)S(1)}, u32[]{:S(2)}, u32[]{:S(2)}) collective-permute-start(bf16[112,768]{1,0:T(8,128)(2,1)S(1)} %get-tuple-element.20), channel_id=1, source_target_pairs={{0,64},{16,80},{32,96},{48,112},{64,0},{80,16},{96,32},{112,48},{1... | collective-permute-start | bytes 516104 | tf_op jit(solution)/shard_map/ppermute | solution.py:20
  114.4 3.2 %collective-permute-start.12 = (bf16[208,1152]{1,0:T(8,128)(2,1)S(1)}, bf16[208,1152]{1,0:T(8,128)(2,1)S(1)}, u32[]{:S(2)}, u32[]{:S(2)}) collective-permute-start(bf16[208,1152]{1,0:T(8,128)(2,1)S(1)} %get-tuple-element.27), channel_id=1, source_target_pairs={{0,512},{256,768},{512,0},{768,256},{1,513},{257,769},{513,1},{769... | collective-permute-start | bytes 1437704 | tf_op jit(solution)/shard_map/ppermute | solution.py:24
  117.6 4.6 %collective-permute-done.4.got = bf16[112,768]{1,0:T(8,128)(2,1)S(1)} collective-permute-done((bf16[112,768]{1,0:T(8,128)(2,1)S(1)}, bf16[112,768]{1,0:T(8,128)(2,1)S(1)}, u32[]{:S(2)}, u32[]{:S(2)}) %collective-permute-start.4) | collective-permute-done | bytes 172064 | tf_op jit(solution)/shard_map/ppermute | solution.py:20
  122.5 4.6 %collective-permute-start.5 = (f32[48,768]{1,0:T(8,128)S(1)}, f32[48,768]{1,0:T(8,128)S(1)}, u32[]{:S(2)}, u32[]{:S(2)}) collective-permute-start(f32[48,768]{1,0:T(8,128)S(1)} %get-tuple-element.22), channel_id=1, source_target_pairs={{0,192},{16,208},{32,224},{48,240},{64,128},{80,144},{96,160},{112... | collective-permute-start | bytes 442376 | tf_op jit(solution)/shard_map/ppermute | solution.py:20
  127.1 9.8 %collective-permute-done.5 = f32[48,768]{1,0:T(8,128)S(1)} collective-permute-done((f32[48,768]{1,0:T(8,128)S(1)}, f32[48,768]{1,0:T(8,128)S(1)}, u32[]{:S(2)}, u32[]{:S(2)}) %collective-permute-start.5) | collective-permute-done | bytes 147488 | tf_op jit(solution)/shard_map/ppermute | solution.py:20
  137.6 2.1 %shard_map.54 = bf16[192,1152]{1,0:T(8,128)(2,1)} custom-call(f32[192,1152]{1,0:T(8,128)S(1)} %get-tuple-element.26.mine, bf16[208,1152]{1,0:T(8,128)(2,1)S(1)} %collective-permute-done.12.got), custom_call_target="tpu_custom_call" | custom-call | tf_op jit(solution)/shard_map/pallas_call | solution.py:203
  (27 shorter events, 5.6 us)
Async XLA Ops:
  0.6 60.5 %copy-start.3 = (bf16[48,768]{1,0:T(8,128)(2,1)S(1)}, bf16[48,768]{1,0:T(8,128)(2,1)}, u32[]{:S(2)}) copy-start(bf16[48,768]{1,0:T(8,128)(2,1)} %param.3) | copy-start | bytes 221188
  0.6 68.2 %copy-start = (bf16[768,1152]{1,0:T(8,128)(2,1)S(1)}, bf16[768,1152]{1,0:T(8,128)(2,1)}, u32[]{:S(2)}) copy-start(bf16[768,1152]{1,0:T(8,128)(2,1)} %weight_ref.1) | copy-start | bytes 5308420
  0.6 60.5 %collective-permute-start.8 = (bf16[48,768]{1,0:T(8,128)(2,1)}, bf16[48,768]{1,0:T(8,128)(2,1)S(1)}, u32[]{:S(2)}, u32[]{:S(2)}) collective-permute-start(bf16[48,768]{1,0:T(8,128)(2,1)} %param.3), channel_id=1, source_target_pairs={{0,128},{16,144},{32,160},{48,176},{64,192},{80,208},{96,224},{112... | collective-permute-start | bytes 221192 | tf_op jit(solution)/shard_map/ppermute | solution.py:20
  9.1 52.1 %collective-permute-start.7 = (bf16[48,768]{1,0:T(8,128)(2,1)}, bf16[48,768]{1,0:T(8,128)(2,1)S(1)}, u32[]{:S(2)}, u32[]{:S(2)}) collective-permute-start(bf16[48,768]{1,0:T(8,128)(2,1)} %param.3), channel_id=1, source_target_pairs={{0,192},{16,208},{32,224},{48,240},{64,128},{80,144},{96,160},{112... | collective-permute-start | bytes 221192 | tf_op jit(solution)/shard_map/ppermute | solution.py:20
  11.0 50.2 %collective-permute-start.6 = (bf16[48,768]{1,0:T(8,128)(2,1)}, bf16[48,768]{1,0:T(8,128)(2,1)}, u32[]{:S(2)}, u32[]{:S(2)}) collective-permute-start(bf16[48,768]{1,0:T(8,128)(2,1)} %param.3), channel_id=1, source_target_pairs={{0,64},{16,80},{32,96},{48,112},{64,0},{80,16},{96,32},{112,48},{1... | collective-permute-start | bytes 221192 | tf_op jit(solution)/shard_map/ppermute | solution.py:20
  53.3 12.2 %collective-permute-start.1 = (bf16[192,1152]{1,0:T(8,128)(2,1)}, bf16[192,1152]{1,0:T(8,128)(2,1)}, u32[]{:S(2)}, u32[]{:S(2)}) collective-permute-start(bf16[192,1152]{1,0:T(8,128)(2,1)} %get-tuple-element.28), channel_id=1, source_target_pairs={{0,15},{1,2},{2,1},{3,4},{4,3},{5,6},{6,5},{7,8},{8,7},{9,10},{10,... | collective-permute-start | bytes 1327112 | tf_op jit(solution)/shard_map/ppermute | solution.py:155
  59.2 9.7 %collective-permute-start = (bf16[192,1152]{1,0:T(8,128)(2,1)}, bf16[192,1152]{1,0:T(8,128)(2,1)}, u32[]{:S(2)}, u32[]{:S(2)}) collective-permute-start(bf16[192,1152]{1,0:T(8,128)(2,1)} %get-tuple-element.29), channel_id=1, source_target_pairs={{0,1},{1,0},{2,3},{3,2},{4,5},{5,4},{6,7},{7,6},{8,9},{9,8},{10,11... | collective-permute-start | bytes 1327112 | tf_op jit(solution)/shard_map/ppermute | solution.py:154
  62.1 12.8 %collective-permute-start.9 = (bf16[192,768]{1,0:T(8,128)(2,1)S(1)}, bf16[192,768]{1,0:T(8,128)(2,1)S(1)}, u32[]{:S(2)}, u32[]{:S(2)}) collective-permute-start(bf16[192,768]{1,0:T(8,128)(2,1)S(1)} %pad_maximum_fusion), channel_id=1, source_target_pairs={{0,16},{16,0},{32,48},{48,32},{64,80},{80,64},{96,112},{112,96},{1... | collective-permute-start | bytes 884744 | tf_op jit(solution)/shard_map/ppermute | solution.py:16
  72.5 12.9 %copy-start.1 = (bf16[768,1152]{1,0:T(8,128)(2,1)}, bf16[768,1152]{1,0:T(8,128)(2,1)S(1)}, u32[]{:S(2)}) copy-start(bf16[768,1152]{1,0:T(8,128)(2,1)S(1)} %get-tuple-element.23.grads) | copy-start | bytes 5308420
  72.5 10.9 %collective-permute-start.2 = (bf16[400,768]{1,0:T(8,128)(2,1)S(1)}, bf16[400,768]{1,0:T(8,128)(2,1)S(1)}, u32[]{:S(2)}, u32[]{:S(2)}) collective-permute-start(bf16[400,768]{1,0:T(8,128)(2,1)S(1)} %get-tuple-element.16), channel_id=1, source_target_pairs={{0,16},{16,0},{32,48},{48,32},{64,80},{80,64},{96,112},{112,96},{1... | collective-permute-start | bytes 1843208 | tf_op jit(solution)/shard_map/ppermute | solution.py:16
  75.0 14.5 %collective-permute-start.10 = (bf16[384,768]{1,0:T(8,128)(2,1)S(1)}, bf16[384,768]{1,0:T(8,128)(2,1)S(1)}, u32[]{:S(2)}, u32[]{:S(2)}) collective-permute-start(bf16[384,768]{1,0:T(8,128)(2,1)S(1)} %constant_dynamic-update-slice_fusion.near), channel_id=1, source_target_pairs={{0,48},{16,32},{32,16},{48,0},{64,112},{80,96},{96,80},{112,64},{1... | collective-permute-start | bytes 1769480 | tf_op jit(solution)/shard_map/ppermute | solution.py:16
  85.3 12.7 %collective-permute-start.3 = (bf16[208,768]{1,0:T(8,128)(2,1)S(1)}, bf16[208,768]{1,0:T(8,128)(2,1)S(1)}, u32[]{:S(2)}, u32[]{:S(2)}) collective-permute-start(bf16[208,768]{1,0:T(8,128)(2,1)S(1)} %get-tuple-element.18), channel_id=1, source_target_pairs={{0,48},{16,32},{32,16},{48,0},{64,112},{80,96},{96,80},{112,64},{1... | collective-permute-start | bytes 958472 | tf_op jit(solution)/shard_map/ppermute | solution.py:16
  98.0 1.5 %copy-start.2 = (bf16[768,1152]{1,0:T(8,128)(2,1)S(1)}, bf16[768,1152]{1,0:T(8,128)(2,1)}, u32[]{:S(2)}) copy-start(bf16[768,1152]{1,0:T(8,128)(2,1)} %copy-done.1) | copy-start | bytes 5308420
  101.5 12.1 %collective-permute-start.11 = (f32[384,1152]{1,0:T(8,128)S(1)}, f32[384,1152]{1,0:T(8,128)S(1)}, u32[]{:S(2)}, u32[]{:S(2)}) collective-permute-start(f32[384,1152]{1,0:T(8,128)S(1)} %get-tuple-element.25), channel_id=1, source_target_pairs={{0,256},{256,0},{512,768},{768,512},{1,257},{257,1},{513,769},{769... | collective-permute-start | bytes 5308424 | tf_op jit(solution)/shard_map/ppermute | solution.py:24
  109.6 12.5 %collective-permute-start.4 = (bf16[112,768]{1,0:T(8,128)(2,1)S(1)}, bf16[112,768]{1,0:T(8,128)(2,1)S(1)}, u32[]{:S(2)}, u32[]{:S(2)}) collective-permute-start(bf16[112,768]{1,0:T(8,128)(2,1)S(1)} %get-tuple-element.20), channel_id=1, source_target_pairs={{0,64},{16,80},{32,96},{48,112},{64,0},{80,16},{96,32},{112,48},{1... | collective-permute-start | bytes 516104 | tf_op jit(solution)/shard_map/ppermute | solution.py:20
  114.4 23.2 %collective-permute-start.12 = (bf16[208,1152]{1,0:T(8,128)(2,1)S(1)}, bf16[208,1152]{1,0:T(8,128)(2,1)S(1)}, u32[]{:S(2)}, u32[]{:S(2)}) collective-permute-start(bf16[208,1152]{1,0:T(8,128)(2,1)S(1)} %get-tuple-element.27), channel_id=1, source_target_pairs={{0,512},{256,768},{512,0},{768,256},{1,513},{257,769},{513,1},{769... | collective-permute-start | bytes 1437704 | tf_op jit(solution)/shard_map/ppermute | solution.py:24
  122.5 14.4 %collective-permute-start.5 = (f32[48,768]{1,0:T(8,128)S(1)}, f32[48,768]{1,0:T(8,128)S(1)}, u32[]{:S(2)}, u32[]{:S(2)}) collective-permute-start(f32[48,768]{1,0:T(8,128)S(1)} %get-tuple-element.22), channel_id=1, source_target_pairs={{0,192},{16,208},{32,224},{48,240},{64,128},{80,144},{96,160},{112... | collective-permute-start | bytes 442376 | tf_op jit(solution)/shard_map/ppermute | solution.py:20

commit v10 on v9

--- a/solution.py
+++ b/solution.py
@@ -51,11 +51,12 @@
     ref[value.shape[0] :, :] = power
 
 
-def spread(depth, chunks, block, into, place):
+def spread(depth, core, chunks, block, into, place):
     parity = jnp.bitwise_and(depth, 1)
     for ref, own, lead in zip(chunks, (1, 0, 0), (0, 0, 4)):
         for k in range(ref.shape[0] // block):
-            source = 2 * (lead + k) + (parity if own else 1 - parity)
+            rank = jnp.bitwise_xor(lead + k, 7 * core)
+            source = 2 * rank + (parity if own else 1 - parity)
             at = pl.multiple_of(place(source) * block, block)
             into[pl.ds(at, block), :] = ref[pl.ds(k * block, block), :]
 
@@ -69,7 +70,7 @@
         slot = jnp.where(jx == 0, 2, jnp.where(jx == 3, 3, jx - 1))
         return slot * 4 + jnp.bitwise_xor(jy, jnp.right_shift(jy, 1))
 
-    spread(place_ref[0], (own, near, far), block, rows, place)
+    spread(place_ref[0], jnp.bitwise_and(place_ref[2], 1), (own, near, far), block, rows, place)
     half = 8 * block
     for at, ref in ((0, sent), (half, kept)):
         part = lax.dot_general(
@@ -146,10 +147,14 @@
     ring = [inputs] + [swap_y(inputs, j) for j in ORDER[1:]]
     own = lax.all_gather(
         grad_out,
-        "depth",
+        ("row", "depth"),
         axis=0,
         tiled=True,
-        axis_index_groups=[list(range(parity, 16, 2)) for parity in range(2)],
+        axis_index_groups=[
+            [r * 16 + z for z in range(parity, 16, 2)][:: 1 - 2 * (r % 2)]
+            for r in range(4)
+            for parity in range(2)
+        ],
     )
     near = lax.ppermute(own[: tokens // 4], "depth", [(i, i ^ 1) for i in range(16)])
     far = lax.ppermute(own[tokens // 4 :], "depth", [(i, ((i + 1) ^ 1) - 1 & 15) for i in range(16)])
@@ -174,7 +179,7 @@
             flops=2 * tokens * width * columns, bytes_accessed=6 << 20, transcendentals=0
         ),
         name="grad_inputs",
-    )(jnp.stack([depth, col]), *grads, weight)
+    )(jnp.stack([depth, col, row]), *grads, weight)
     got = swap_x(sent, 1)
     sent, kept = stage(x_stage_kernel, coded(tokens // 4), plain(tokens // 4), kept, got)
     got = swap_x(sent, 3)

time: 140 us -> 139 us (level)
    ppermute x2, starting transfers between devices: 10.4 us -> 8.97 us  [swap_row(): return lax.ppermute(value, 'row', [(i, i ^ j) for i in range(4)])]
    unnamed x12 -> x6, local copies, waits for them, and re-layouts: 2.4 us -> 3.57 us
  transfers between devices with their start and end apart: 13 -> 13, of which waited for: 5 -> 5; matrix products, arithmetic and copies ran while one was open for 3% -> 5% of each run, Pallas kernels for 5% -> 5%
where the time goes in v10:
time: 139 us; the launch traced here: 138 us
  starting transfers between devices  51 us (37%)
  blocking collectives  38.9 us (28%)
  waiting for transfers between devices  30.4 us (22%)
  Pallas kernels  11 us (8%)
  local copies, waits for them, and re-layouts  4.56 us (3%)
  other arithmetic  1.74 us (1%)
    all_gather x1, blocking collectives, per_device(): lax.all_gather(grad_out, ('row', 'depth'), axis=0, tiled=True, axis_index...  38.9 us
    ppermute x5, starting transfers between devices, swap_y(): return lax.ppermute(value, 'col', [(i, i ^ 4 * j) for i in range(16)])  21.4 us
    ppermute x5, waiting for transfers between devices, swap_y(): return lax.ppermute(value, 'col', [(i, i ^ 4 * j) for i in range(16)])  14.4 us
    ppermute x4, waiting for transfers between devices, swap_x(): return lax.ppermute(value, 'col', [(i, i ^ j) for i in range(16)])  13.7 us
    ppermute x4, starting transfers between devices, swap_x(): return lax.ppermute(value, 'col', [(i, i ^ j) for i in range(16)])  13 us
    ppermute x2, starting transfers between devices, swap_row(): return lax.ppermute(value, 'row', [(i, i ^ j) for i in range(4)])  8.97 us
    ppermute x1, starting transfers between devices, per_device(): lax.ppermute(own[tokens // 4:], 'depth', [(i, (i + 1 ^ 1) - 1 & 15) for i...  5.8 us
    pallas_call x4, Pallas kernels, stage(): pl.pallas_call(kernel, out_shape=[sent, kept], in_specs=[VMEM] * len(oper...  4.01 us
  transfers between devices with their start and end apart: 13, of which 5 were waited for; matrix products, arithmetic and copies ran while one was open for 5% of the time, Pallas kernels for 5%

profile of v10, /device:TPU:1, one launch (start us, length us, event | category | flops | bytes accessed | tf_op | source)
XLA Modules:
  0.0 138.5 jit_solution(9245811135682119438)
XLA Ops:
  0.6 8.4 %collective-permute-start.8 = (bf16[48,768]{1,0:T(8,128)(2,1)}, bf16[48,768]{1,0:T(8,128)(2,1)}, u32[]{:S(2)}, u32[]{:S(2)}) collective-permute-start(bf16[48,768]{1,0:T(8,128)(2,1)} %param.3), channel_id=1, source_target_pairs={{0,128},{16,144},{32,160},{48,176},{64,192},{80,208},{96,224},{112... | collective-permute-start | bytes 221192 | tf_op jit(solution)/shard_map/ppermute | solution.py:20
  9.1 2.0 %collective-permute-start.7 = (bf16[48,768]{1,0:T(8,128)(2,1)}, bf16[48,768]{1,0:T(8,128)(2,1)}, u32[]{:S(2)}, u32[]{:S(2)}) collective-permute-start(bf16[48,768]{1,0:T(8,128)(2,1)} %param.3), channel_id=1, source_target_pairs={{0,192},{16,208},{32,224},{48,240},{64,128},{80,144},{96,160},{112... | collective-permute-start | bytes 221192 | tf_op jit(solution)/shard_map/ppermute | solution.py:20
  11.0 2.4 %collective-permute-start.6 = (bf16[48,768]{1,0:T(8,128)(2,1)}, bf16[48,768]{1,0:T(8,128)(2,1)}, u32[]{:S(2)}, u32[]{:S(2)}) collective-permute-start(bf16[48,768]{1,0:T(8,128)(2,1)} %param.3), channel_id=1, source_target_pairs={{0,64},{16,80},{32,96},{48,112},{64,0},{80,16},{96,32},{112,48},{1... | collective-permute-start | bytes 221192 | tf_op jit(solution)/shard_map/ppermute | solution.py:20
  13.4 38.9 %all_gather.3.own = bf16[384,1152]{1,0:T(8,128)(2,1)S(1)} all-gather(bf16[48,1152]{1,0:T(8,128)(2,1)} %param.5), channel_id=1, replica_groups={{0,2,4,6,8,10,12,14},{1,3,5,7,9,11,13,15},{270,268,266,264,262,260,258,..., dimensions={0}, use_global_device_ids=true | all-gather | bytes 995328 | tf_op jit(solution)/shard_map/all_gather | solution.py:148
  53.3 5.8 %collective-permute-start.1 = (bf16[192,1152]{1,0:T(8,128)(2,1)}, bf16[192,1152]{1,0:T(8,128)(2,1)S(1)}, u32[]{:S(2)}, u32[]{:S(2)}) collective-permute-start(bf16[192,1152]{1,0:T(8,128)(2,1)} %get-tuple-element.28), channel_id=1, source_target_pairs={{0,15},{1,2},{2,1},{3,4},{4,3},{5,6},{6,5},{7,8},{8,7},{9,10},{10,... | collective-permute-start | bytes 1327112 | tf_op jit(solution)/shard_map/ppermute | solution.py:160
  59.1 1.9 %collective-permute-start = (bf16[192,1152]{1,0:T(8,128)(2,1)}, bf16[192,1152]{1,0:T(8,128)(2,1)S(1)}, u32[]{:S(2)}, u32[]{:S(2)}) collective-permute-start(bf16[192,1152]{1,0:T(8,128)(2,1)} %get-tuple-element.29), channel_id=1, source_target_pairs={{0,1},{1,0},{2,3},{3,2},{4,5},{5,4},{6,7},{7,6},{8,9},{9,8},{10,11... | collective-permute-start | bytes 1327112 | tf_op jit(solution)/shard_map/ppermute | solution.py:159
  62.0 1.0 pad_maximum_fusion
  63.0 2.4 %collective-permute-start.9 = (bf16[192,768]{1,0:T(8,128)(2,1)S(1)}, bf16[192,768]{1,0:T(8,128)(2,1)S(1)}, u32[]{:S(2)}, u32[]{:S(2)}) collective-permute-start(bf16[192,768]{1,0:T(8,128)(2,1)S(1)} %pad_maximum_fusion), channel_id=1, source_target_pairs={{0,16},{16,0},{32,48},{48,32},{64,80},{80,64},{96,112},{112,96},{1... | collective-permute-start | bytes 884744 | tf_op jit(solution)/shard_map/ppermute | solution.py:16
  66.4 2.3 %collective-permute-done.near = bf16[192,1152]{1,0:T(8,128)(2,1)S(1)} collective-permute-done((bf16[192,1152]{1,0:T(8,128)(2,1)}, bf16[192,1152]{1,0:T(8,128)(2,1)S(1)}, u32[]{:S(2)}, u32[]{:S(2)}) %collective-permute-start) | collective-permute-done | bytes 442400 | tf_op jit(solution)/shard_map/ppermute | solution.py:159
  68.7 3.0 %grad_inputs.1 = (bf16[400,768]{1,0:T(8,128)(2,1)S(1)}, f32[384,768]{1,0:T(8,128)S(1)}, bf16[768,1152]{1,0:T(8,128)(2,1)S(1)}) custom-call(s32[3]{0:T(128)S(1)} %pad_add_fusion.place_ref, bf16[384,1152]{1,0:T(8,128)(2,1)S(1)} %all_gather.3.own, bf16[192,1152]{1,0:T(8,128)(2,1)S(1)} %collective-permute-done.near, ...), custom_call_target="tpu_custom_call" | custom-call | flops 1358954496 | bytes 6291456 | tf_op jit(solution)/shard_map/grad_inputs/pallas_call | solution.py:172
  71.7 2.4 %collective-permute-start.2 = (bf16[400,768]{1,0:T(8,128)(2,1)S(1)}, bf16[400,768]{1,0:T(8,128)(2,1)S(1)}, u32[]{:S(2)}, u32[]{:S(2)}) collective-permute-start(bf16[400,768]{1,0:T(8,128)(2,1)S(1)} %get-tuple-element.16), channel_id=1, source_target_pairs={{0,16},{16,0},{32,48},{48,32},{64,80},{80,64},{96,112},{112,96},{1... | collective-permute-start | bytes 1843208 | tf_op jit(solution)/shard_map/ppermute | solution.py:16
  75.9 3.7 %collective-permute-start.10 = (bf16[384,768]{1,0:T(8,128)(2,1)S(1)}, bf16[384,768]{1,0:T(8,128)(2,1)S(1)}, u32[]{:S(2)}, u32[]{:S(2)}) collective-permute-start(bf16[384,768]{1,0:T(8,128)(2,1)S(1)} %constant_dynamic-update-slice_fusion.near), channel_id=1, source_target_pairs={{0,48},{16,32},{32,16},{48,0},{64,112},{80,96},{96,80},{112,64},{1... | collective-permute-start | bytes 1769480 | tf_op jit(solution)/shard_map/ppermute | solution.py:16
  79.6 5.3 %collective-permute-done.2.got = bf16[400,768]{1,0:T(8,128)(2,1)S(1)} collective-permute-done((bf16[400,768]{1,0:T(8,128)(2,1)S(1)}, bf16[400,768]{1,0:T(8,128)(2,1)S(1)}, u32[]{:S(2)}, u32[]{:S(2)}) %collective-permute-start.2) | collective-permute-done | bytes 614432 | tf_op jit(solution)/shard_map/ppermute | solution.py:16
  85.0 2.0 %shard_map.50 = (bf16[208,768]{1,0:T(8,128)(2,1)S(1)}, f32[192,768]{1,0:T(8,128)S(1)}) custom-call(f32[384,768]{1,0:T(8,128)S(1)} %get-tuple-element.15.mine, bf16[400,768]{1,0:T(8,128)(2,1)S(1)} %collective-permute-done.2.got), custom_call_target="tpu_custom_call" | custom-call | tf_op jit(solution)/shard_map/pallas_call | solution.py:113
  86.9 4.4 %collective-permute-start.3 = (bf16[208,768]{1,0:T(8,128)(2,1)S(1)}, bf16[208,768]{1,0:T(8,128)(2,1)S(1)}, u32[]{:S(2)}, u32[]{:S(2)}) collective-permute-start(bf16[208,768]{1,0:T(8,128)(2,1)S(1)} %get-tuple-element.18), channel_id=1, source_target_pairs={{0,48},{16,32},{32,16},{48,0},{64,112},{80,96},{96,80},{112,64},{1... | collective-permute-start | bytes 958472 | tf_op jit(solution)/shard_map/ppermute | solution.py:16
  91.3 8.3 %collective-permute-done.3.got._ = bf16[208,768]{1,0:T(8,128)(2,1)S(1)} collective-permute-done((bf16[208,768]{1,0:T(8,128)(2,1)S(1)}, bf16[208,768]{1,0:T(8,128)(2,1)S(1)}, u32[]{:S(2)}, u32[]{:S(2)}) %collective-permute-start.3) | collective-permute-done | bytes 319520 | tf_op jit(solution)/shard_map/ppermute | solution.py:16
  99.7 2.0 %grad_weight.1 = (f32[384,1152]{1,0:T(8,128)S(1)}, f32[384,1152]{1,0:T(8,128)S(1)}) custom-call(s32[1]{0:T(128)} %bitcast.2.row_ref, bf16[208,768]{1,0:T(8,128)(2,1)S(1)} %collective-permute-done.3.got._, bf16[768,1152]{1,0:T(8,128)(2,1)S(1)} %get-tuple-element.23.grads, bf16[384,768]{1,0:T(8,128)(2,1)S(1)} %constant_dynamic-update-slice_fusion.near, ...), custom_call_target="tpu_custom_call" | custom-call | flops 1358954496 | bytes 7340032 | tf_op jit(solution)/shard_map/grad_weight/pallas_call | solution.py:187
  101.6 5.8 %collective-permute-start.11 = (f32[384,1152]{1,0:T(8,128)S(1)}, f32[384,1152]{1,0:T(8,128)S(1)}, u32[]{:S(2)}, u32[]{:S(2)}) collective-permute-start(f32[384,1152]{1,0:T(8,128)S(1)} %get-tuple-element.25), channel_id=1, source_target_pairs={{0,256},{256,0},{512,768},{768,512},{1,257},{257,1},{513,769},{769... | collective-permute-start | bytes 5308424 | tf_op jit(solution)/shard_map/ppermute | solution.py:24
  108.3 4.0 %collective-permute-start.4 = (bf16[112,768]{1,0:T(8,128)(2,1)S(1)}, bf16[112,768]{1,0:T(8,128)(2,1)S(1)}, u32[]{:S(2)}, u32[]{:S(2)}) collective-permute-start(bf16[112,768]{1,0:T(8,128)(2,1)S(1)} %get-tuple-element.20), channel_id=1, source_target_pairs={{0,64},{16,80},{32,96},{48,112},{64,0},{80,16},{96,32},{112,48},{1... | collective-permute-start | bytes 516104 | tf_op jit(solution)/shard_map/ppermute | solution.py:20
  113.1 3.2 %collective-permute-start.12 = (bf16[208,1152]{1,0:T(8,128)(2,1)S(1)}, bf16[208,1152]{1,0:T(8,128)(2,1)S(1)}, u32[]{:S(2)}, u32[]{:S(2)}) collective-permute-start(bf16[208,1152]{1,0:T(8,128)(2,1)S(1)} %get-tuple-element.27), channel_id=1, source_target_pairs={{0,512},{256,768},{512,0},{768,256},{1,513},{257,769},{513,1},{769... | collective-permute-start | bytes 1437704 | tf_op jit(solution)/shard_map/ppermute | solution.py:24
  116.3 4.5 %collective-permute-done.4.got = bf16[112,768]{1,0:T(8,128)(2,1)S(1)} collective-permute-done((bf16[112,768]{1,0:T(8,128)(2,1)S(1)}, bf16[112,768]{1,0:T(8,128)(2,1)S(1)}, u32[]{:S(2)}, u32[]{:S(2)}) %collective-permute-start.4) | collective-permute-done | bytes 172064 | tf_op jit(solution)/shard_map/ppermute | solution.py:20
  121.2 4.6 %collective-permute-start.5 = (f32[48,768]{1,0:T(8,128)S(1)}, f32[48,768]{1,0:T(8,128)S(1)}, u32[]{:S(2)}, u32[]{:S(2)}) collective-permute-start(f32[48,768]{1,0:T(8,128)S(1)} %get-tuple-element.22), channel_id=1, source_target_pairs={{0,192},{16,208},{32,224},{48,240},{64,128},{80,144},{96,160},{112... | collective-permute-start | bytes 442376 | tf_op jit(solution)/shard_map/ppermute | solution.py:20
  125.8 9.9 %collective-permute-done.5 = f32[48,768]{1,0:T(8,128)S(1)} collective-permute-done((f32[48,768]{1,0:T(8,128)S(1)}, f32[48,768]{1,0:T(8,128)S(1)}, u32[]{:S(2)}, u32[]{:S(2)}) %collective-permute-start.5) | collective-permute-done | bytes 147488 | tf_op jit(solution)/shard_map/ppermute | solution.py:20
  136.4 2.1 %shard_map.54 = bf16[192,1152]{1,0:T(8,128)(2,1)} custom-call(f32[192,1152]{1,0:T(8,128)S(1)} %get-tuple-element.26.mine, bf16[208,1152]{1,0:T(8,128)(2,1)S(1)} %collective-permute-done.12.got), custom_call_target="tpu_custom_call" | custom-call | tf_op jit(solution)/shard_map/pallas_call | solution.py:208
  (21 shorter events, 7.4 us)
Async XLA Ops:
  0.6 68.0 %copy-start = (bf16[768,1152]{1,0:T(8,128)(2,1)S(1)}, bf16[768,1152]{1,0:T(8,128)(2,1)}, u32[]{:S(2)}) copy-start(bf16[768,1152]{1,0:T(8,128)(2,1)} %weight_ref.1) | copy-start | bytes 5308420
  0.6 61.4 %collective-permute-start.8 = (bf16[48,768]{1,0:T(8,128)(2,1)}, bf16[48,768]{1,0:T(8,128)(2,1)}, u32[]{:S(2)}, u32[]{:S(2)}) collective-permute-start(bf16[48,768]{1,0:T(8,128)(2,1)} %param.3), channel_id=1, source_target_pairs={{0,128},{16,144},{32,160},{48,176},{64,192},{80,208},{96,224},{112... | collective-permute-start | bytes 221192 | tf_op jit(solution)/shard_map/ppermute | solution.py:20
  9.1 53.0 %collective-permute-start.7 = (bf16[48,768]{1,0:T(8,128)(2,1)}, bf16[48,768]{1,0:T(8,128)(2,1)}, u32[]{:S(2)}, u32[]{:S(2)}) collective-permute-start(bf16[48,768]{1,0:T(8,128)(2,1)} %param.3), channel_id=1, source_target_pairs={{0,192},{16,208},{32,224},{48,240},{64,128},{80,144},{96,160},{112... | collective-permute-start | bytes 221192 | tf_op jit(solution)/shard_map/ppermute | solution.py:20
  11.0 51.0 %collective-permute-start.6 = (bf16[48,768]{1,0:T(8,128)(2,1)}, bf16[48,768]{1,0:T(8,128)(2,1)}, u32[]{:S(2)}, u32[]{:S(2)}) collective-permute-start(bf16[48,768]{1,0:T(8,128)(2,1)} %param.3), channel_id=1, source_target_pairs={{0,64},{16,80},{32,96},{48,112},{64,0},{80,16},{96,32},{112,48},{1... | collective-permute-start | bytes 221192 | tf_op jit(solution)/shard_map/ppermute | solution.py:20
  53.3 13.1 %collective-permute-start.1 = (bf16[192,1152]{1,0:T(8,128)(2,1)}, bf16[192,1152]{1,0:T(8,128)(2,1)S(1)}, u32[]{:S(2)}, u32[]{:S(2)}) collective-permute-start(bf16[192,1152]{1,0:T(8,128)(2,1)} %get-tuple-element.28), channel_id=1, source_target_pairs={{0,15},{1,2},{2,1},{3,4},{4,3},{5,6},{6,5},{7,8},{8,7},{9,10},{10,... | collective-permute-start | bytes 1327112 | tf_op jit(solution)/shard_map/ppermute | solution.py:160
  59.1 9.6 %collective-permute-start = (bf16[192,1152]{1,0:T(8,128)(2,1)}, bf16[192,1152]{1,0:T(8,128)(2,1)S(1)}, u32[]{:S(2)}, u32[]{:S(2)}) collective-permute-start(bf16[192,1152]{1,0:T(8,128)(2,1)} %get-tuple-element.29), channel_id=1, source_target_pairs={{0,1},{1,0},{2,3},{3,2},{4,5},{5,4},{6,7},{7,6},{8,9},{9,8},{10,11... | collective-permute-start | bytes 1327112 | tf_op jit(solution)/shard_map/ppermute | solution.py:159
  63.0 12.8 %collective-permute-start.9 = (bf16[192,768]{1,0:T(8,128)(2,1)S(1)}, bf16[192,768]{1,0:T(8,128)(2,1)S(1)}, u32[]{:S(2)}, u32[]{:S(2)}) collective-permute-start(bf16[192,768]{1,0:T(8,128)(2,1)S(1)} %pad_maximum_fusion), channel_id=1, source_target_pairs={{0,16},{16,0},{32,48},{48,32},{64,80},{80,64},{96,112},{112,96},{1... | collective-permute-start | bytes 884744 | tf_op jit(solution)/shard_map/ppermute | solution.py:16
  71.7 13.3 %collective-permute-start.2 = (bf16[400,768]{1,0:T(8,128)(2,1)S(1)}, bf16[400,768]{1,0:T(8,128)(2,1)S(1)}, u32[]{:S(2)}, u32[]{:S(2)}) collective-permute-start(bf16[400,768]{1,0:T(8,128)(2,1)S(1)} %get-tuple-element.16), channel_id=1, source_target_pairs={{0,16},{16,0},{32,48},{48,32},{64,80},{80,64},{96,112},{112,96},{1... | collective-permute-start | bytes 1843208 | tf_op jit(solution)/shard_map/ppermute | solution.py:16
  75.9 15.4 %collective-permute-start.10 = (bf16[384,768]{1,0:T(8,128)(2,1)S(1)}, bf16[384,768]{1,0:T(8,128)(2,1)S(1)}, u32[]{:S(2)}, u32[]{:S(2)}) collective-permute-start(bf16[384,768]{1,0:T(8,128)(2,1)S(1)} %constant_dynamic-update-slice_fusion.near), channel_id=1, source_target_pairs={{0,48},{16,32},{32,16},{48,0},{64,112},{80,96},{96,80},{112,64},{1... | collective-permute-start | bytes 1769480 | tf_op jit(solution)/shard_map/ppermute | solution.py:16
  86.9 12.7 %collective-permute-start.3 = (bf16[208,768]{1,0:T(8,128)(2,1)S(1)}, bf16[208,768]{1,0:T(8,128)(2,1)S(1)}, u32[]{:S(2)}, u32[]{:S(2)}) collective-permute-start(bf16[208,768]{1,0:T(8,128)(2,1)S(1)} %get-tuple-element.18), channel_id=1, source_target_pairs={{0,48},{16,32},{32,16},{48,0},{64,112},{80,96},{96,80},{112,64},{1... | collective-permute-start | bytes 958472 | tf_op jit(solution)/shard_map/ppermute | solution.py:16
  101.6 10.7 %collective-permute-start.11 = (f32[384,1152]{1,0:T(8,128)S(1)}, f32[384,1152]{1,0:T(8,128)S(1)}, u32[]{:S(2)}, u32[]{:S(2)}) collective-permute-start(f32[384,1152]{1,0:T(8,128)S(1)} %get-tuple-element.25), channel_id=1, source_target_pairs={{0,256},{256,0},{512,768},{768,512},{1,257},{257,1},{513,769},{769... | collective-permute-start | bytes 5308424 | tf_op jit(solution)/shard_map/ppermute | solution.py:24
  108.3 12.5 %collective-permute-start.4 = (bf16[112,768]{1,0:T(8,128)(2,1)S(1)}, bf16[112,768]{1,0:T(8,128)(2,1)S(1)}, u32[]{:S(2)}, u32[]{:S(2)}) collective-permute-start(bf16[112,768]{1,0:T(8,128)(2,1)S(1)} %get-tuple-element.20), channel_id=1, source_target_pairs={{0,64},{16,80},{32,96},{48,112},{64,0},{80,16},{96,32},{112,48},{1... | collective-permute-start | bytes 516104 | tf_op jit(solution)/shard_map/ppermute | solution.py:20
  113.1 23.3 %collective-permute-start.12 = (bf16[208,1152]{1,0:T(8,128)(2,1)S(1)}, bf16[208,1152]{1,0:T(8,128)(2,1)S(1)}, u32[]{:S(2)}, u32[]{:S(2)}) collective-permute-start(bf16[208,1152]{1,0:T(8,128)(2,1)S(1)} %get-tuple-element.27), channel_id=1, source_target_pairs={{0,512},{256,768},{512,0},{768,256},{1,513},{257,769},{513,1},{769... | collective-permute-start | bytes 1437704 | tf_op jit(solution)/shard_map/ppermute | solution.py:24
  121.2 14.5 %collective-permute-start.5 = (f32[48,768]{1,0:T(8,128)S(1)}, f32[48,768]{1,0:T(8,128)S(1)}, u32[]{:S(2)}, u32[]{:S(2)}) collective-permute-start(f32[48,768]{1,0:T(8,128)S(1)} %get-tuple-element.22), channel_id=1, source_target_pairs={{0,192},{16,208},{32,224},{48,240},{64,128},{80,144},{96,160},{112... | collective-permute-start | bytes 442376 | tf_op jit(solution)/shard_map/ppermute | solution.py:20

commit v11 on v10

--- a/solution.py
+++ b/solution.py
@@ -38,11 +38,8 @@
     tail = ref.shape[0] - 16
     power = ref[tail:, :].astype(F32)[:1, :1]
     code = ref[pl.ds(start, size), :].astype(F32)
-    root = jnp.abs(code)
-    for _ in range(4):
-        root = jnp.sqrt(root)
-    root = root * jnp.exp2(power - 7.5)
-    return jnp.where(code < 0, -root, root)
+    root = jnp.exp2(jnp.log2(jnp.maximum(jnp.abs(code), 1e-37)) * 0.0625 + (power - 7.5))
+    return jnp.where(code == 0, 0.0, jnp.where(code < 0, -root, root))
 
 
 def put(ref, value):
@@ -102,20 +99,31 @@
 def last_stage_kernel(mine, got, sent, kept):
     block = mine.shape[0] // 2
     kept[...] = mine[:block, :] + decode(got, 0, block)
-    sent[...] = mine[block:, :] + decode(got, block, block)
-
-
-def finish_weight_kernel(mine, got, out):
+    put(sent, mine[block:, :] + decode(got, block, block))
+
+
+def finish_kernel(mine, got, out):
     out[...] = (mine[...] + decode(got, 0, mine.shape[0])).astype(BF16)
 
 
-def stage(kernel, sent, kept, *operands):
+def finish(kept, got):
+    return pl.pallas_call(
+        finish_kernel,
+        out_shape=jax.ShapeDtypeStruct(kept.shape, BF16),
+        in_specs=[VMEM] * 2,
+        out_specs=VMEM,
+        compiler_params=pltpu.CompilerParams(vmem_limit_bytes=10 << 20),
+    )(kept, got)
+
+
+def stage(kernel, sent, kept, *operands, weight=0):
     return pl.pallas_call(
         kernel,
         out_shape=[sent, kept],
         in_specs=[VMEM] * len(operands),
         out_specs=[VMEM] * 2,
         compiler_params=pltpu.CompilerParams(vmem_limit_bytes=10 << 20),
+        cost_estimate=pl.CostEstimate(flops=weight, bytes_accessed=1 << 20, transcendentals=0),
     )(*operands)
 
 
@@ -198,21 +206,14 @@
     )(row.reshape(1), got, ordered, near_in, far_in)
     rows = width // 4
     got_w = swap_row(send_w, 1)
+    sent, kept = stage(y_stage_kernel, coded(tokens // 8), plain(tokens // 8), kept, got)
     sent_w, kept_w = stage(sum_weight_kernel, coded(rows, columns), plain(rows, columns), keep_w, got_w)
     got_w = swap_row(sent_w, 2)
-
-    sent, kept = stage(y_stage_kernel, coded(tokens // 8), plain(tokens // 8), kept, got)
     got = swap_y(sent, 1)
-    sent, kept = stage(last_stage_kernel, plain(block), plain(block), kept, got)
-    grad_inputs = (kept + swap_y(sent, 3)).astype(BF16)
-    grad_weight = pl.pallas_call(
-        finish_weight_kernel,
-        out_shape=jax.ShapeDtypeStruct((rows, columns), BF16),
-        in_specs=[VMEM] * 2,
-        out_specs=VMEM,
-        compiler_params=pltpu.CompilerParams(vmem_limit_bytes=10 << 20),
-    )(kept_w, got_w)
-    return grad_inputs, grad_weight
+    sent, kept = stage(last_stage_kernel, coded(block), plain(block), kept, got, weight=8 << 30)
+    got = swap_y(sent, 3)
+    grad_weight = finish(kept_w, got_w)
+    return finish(kept, got), grad_weight
 
 
 def solution(mesh):

time: 139 us -> 137 us (0.986)
  Pallas kernels: 11 us -> 9.54 us
    pallas_call x4, Pallas kernels: 4.01 us -> 2.55 us  [stage(): pl.pallas_call(kernel, out_shape=[sent, kept], in_specs=[VMEM] * len(oper...]
  transfers between devices with their start and end apart: 13 -> 13, of which waited for: 5 -> 5; matrix products, arithmetic and copies ran while one was open for 5% -> 4% of each run, Pallas kernels for 5% -> 5%
where the time goes in v11:
time: 137 us; the launch traced here: 136 us
  starting transfers between devices  51.9 us (38%)
  blocking collectives  38.9 us (28%)
  waiting for transfers between devices  29.4 us (21%)
  Pallas kernels  9.54 us (7%)
  local copies, waits for them, and re-layouts  4.56 us (3%)
    all_gather x1, blocking collectives, per_device(): lax.all_gather(grad_out, ('row', 'depth'), axis=0, tiled=True, axis_index...  38.9 us
    ppermute x5, starting transfers between devices, swap_y(): return lax.ppermute(value, 'col', [(i, i ^ 4 * j) for i in range(16)])  21.4 us
    ppermute x4, waiting for transfers between devices, swap_x(): return lax.ppermute(value, 'col', [(i, i ^ j) for i in range(16)])  13.7 us
    ppermute x5, waiting for transfers between devices, swap_y(): return lax.ppermute(value, 'col', [(i, i ^ 4 * j) for i in range(16)])  13.4 us
    ppermute x4, starting transfers between devices, swap_x(): return lax.ppermute(value, 'col', [(i, i ^ j) for i in range(16)])  13 us
    ppermute x2, starting transfers between devices, swap_row(): return lax.ppermute(value, 'row', [(i, i ^ j) for i in range(4)])  9.89 us
    ppermute x1, starting transfers between devices, per_device(): lax.ppermute(own[tokens // 4:], 'depth', [(i, (i + 1 ^ 1) - 1 & 15) for i...  5.8 us
    unnamed x6, local copies, waits for them, and re-layouts  3.57 us
  transfers between devices with their start and end apart: 13, of which 5 were waited for; matrix products, arithmetic and copies ran while one was open for 4% of the time, Pallas kernels for 5%

profile of v11, /device:TPU:1, one launch (start us, length us, event | category | flops | bytes accessed | tf_op | source)
XLA Modules:
  0.0 136.2 jit_solution(7744644786306659445)
XLA Ops:
  0.6 8.4 %collective-permute-start.8 = (bf16[48,768]{1,0:T(8,128)(2,1)}, bf16[48,768]{1,0:T(8,128)(2,1)}, u32[]{:S(2)}, u32[]{:S(2)}) collective-permute-start(bf16[48,768]{1,0:T(8,128)(2,1)} %param.3), channel_id=1, source_target_pairs={{0,128},{16,144},{32,160},{48,176},{64,192},{80,208},{96,224},{112... | collective-permute-start | bytes 221192 | tf_op jit(solution)/shard_map/ppermute | solution.py:20
  9.1 2.0 %collective-permute-start.7 = (bf16[48,768]{1,0:T(8,128)(2,1)}, bf16[48,768]{1,0:T(8,128)(2,1)}, u32[]{:S(2)}, u32[]{:S(2)}) collective-permute-start(bf16[48,768]{1,0:T(8,128)(2,1)} %param.3), channel_id=1, source_target_pairs={{0,192},{16,208},{32,224},{48,240},{64,128},{80,144},{96,160},{112... | collective-permute-start | bytes 221192 | tf_op jit(solution)/shard_map/ppermute | solution.py:20
  11.0 2.4 %collective-permute-start.6 = (bf16[48,768]{1,0:T(8,128)(2,1)}, bf16[48,768]{1,0:T(8,128)(2,1)}, u32[]{:S(2)}, u32[]{:S(2)}) collective-permute-start(bf16[48,768]{1,0:T(8,128)(2,1)} %param.3), channel_id=1, source_target_pairs={{0,64},{16,80},{32,96},{48,112},{64,0},{80,16},{96,32},{112,48},{1... | collective-permute-start | bytes 221192 | tf_op jit(solution)/shard_map/ppermute | solution.py:20
  13.4 38.9 %all_gather.3.own = bf16[384,1152]{1,0:T(8,128)(2,1)S(1)} all-gather(bf16[48,1152]{1,0:T(8,128)(2,1)} %param.5), channel_id=1, replica_groups={{0,2,4,6,8,10,12,14},{1,3,5,7,9,11,13,15},{270,268,266,264,262,260,258,..., dimensions={0}, use_global_device_ids=true | all-gather | bytes 995328 | tf_op jit(solution)/shard_map/all_gather | solution.py:156
  53.3 5.8 %collective-permute-start.1 = (bf16[192,1152]{1,0:T(8,128)(2,1)}, bf16[192,1152]{1,0:T(8,128)(2,1)S(1)}, u32[]{:S(2)}, u32[]{:S(2)}) collective-permute-start(bf16[192,1152]{1,0:T(8,128)(2,1)} %get-tuple-element.28), channel_id=1, source_target_pairs={{0,15},{1,2},{2,1},{3,4},{4,3},{5,6},{6,5},{7,8},{8,7},{9,10},{10,... | collective-permute-start | bytes 1327112 | tf_op jit(solution)/shard_map/ppermute | solution.py:168
  59.1 1.9 %collective-permute-start = (bf16[192,1152]{1,0:T(8,128)(2,1)}, bf16[192,1152]{1,0:T(8,128)(2,1)S(1)}, u32[]{:S(2)}, u32[]{:S(2)}) collective-permute-start(bf16[192,1152]{1,0:T(8,128)(2,1)} %get-tuple-element.29), channel_id=1, source_target_pairs={{0,1},{1,0},{2,3},{3,2},{4,5},{5,4},{6,7},{7,6},{8,9},{9,8},{10,11... | collective-permute-start | bytes 1327112 | tf_op jit(solution)/shard_map/ppermute | solution.py:167
  62.0 1.0 pad_maximum_fusion
  63.0 2.4 %collective-permute-start.9 = (bf16[192,768]{1,0:T(8,128)(2,1)S(1)}, bf16[192,768]{1,0:T(8,128)(2,1)S(1)}, u32[]{:S(2)}, u32[]{:S(2)}) collective-permute-start(bf16[192,768]{1,0:T(8,128)(2,1)S(1)} %pad_maximum_fusion), channel_id=1, source_target_pairs={{0,16},{16,0},{32,48},{48,32},{64,80},{80,64},{96,112},{112,96},{1... | collective-permute-start | bytes 884744 | tf_op jit(solution)/shard_map/ppermute | solution.py:16
  66.4 2.3 %collective-permute-done.near = bf16[192,1152]{1,0:T(8,128)(2,1)S(1)} collective-permute-done((bf16[192,1152]{1,0:T(8,128)(2,1)}, bf16[192,1152]{1,0:T(8,128)(2,1)S(1)}, u32[]{:S(2)}, u32[]{:S(2)}) %collective-permute-start) | collective-permute-done | bytes 442400 | tf_op jit(solution)/shard_map/ppermute | solution.py:167
  68.7 3.0 %grad_inputs.1 = (bf16[400,768]{1,0:T(8,128)(2,1)S(1)}, f32[384,768]{1,0:T(8,128)S(1)}, bf16[768,1152]{1,0:T(8,128)(2,1)S(1)}) custom-call(s32[3]{0:T(128)S(1)} %pad_add_fusion.place_ref, bf16[384,1152]{1,0:T(8,128)(2,1)S(1)} %all_gather.3.own, bf16[192,1152]{1,0:T(8,128)(2,1)S(1)} %collective-permute-done.near, ...), custom_call_target="tpu_custom_call" | custom-call | flops 1358954496 | bytes 6291456 | tf_op jit(solution)/shard_map/grad_inputs/pallas_call | solution.py:180
  71.7 2.4 %collective-permute-start.2 = (bf16[400,768]{1,0:T(8,128)(2,1)S(1)}, bf16[400,768]{1,0:T(8,128)(2,1)S(1)}, u32[]{:S(2)}, u32[]{:S(2)}) collective-permute-start(bf16[400,768]{1,0:T(8,128)(2,1)S(1)} %get-tuple-element.16), channel_id=1, source_target_pairs={{0,16},{16,0},{32,48},{48,32},{64,80},{80,64},{96,112},{112,96},{1... | collective-permute-start | bytes 1843208 | tf_op jit(solution)/shard_map/ppermute | solution.py:16
  75.9 3.7 %collective-permute-start.10 = (bf16[384,768]{1,0:T(8,128)(2,1)S(1)}, bf16[384,768]{1,0:T(8,128)(2,1)S(1)}, u32[]{:S(2)}, u32[]{:S(2)}) collective-permute-start(bf16[384,768]{1,0:T(8,128)(2,1)S(1)} %constant_dynamic-update-slice_fusion.near), channel_id=1, source_target_pairs={{0,48},{16,32},{32,16},{48,0},{64,112},{80,96},{96,80},{112,64},{1... | collective-permute-start | bytes 1769480 | tf_op jit(solution)/shard_map/ppermute | solution.py:16
  79.6 5.3 %collective-permute-done.2.got = bf16[400,768]{1,0:T(8,128)(2,1)S(1)} collective-permute-done((bf16[400,768]{1,0:T(8,128)(2,1)S(1)}, bf16[400,768]{1,0:T(8,128)(2,1)S(1)}, u32[]{:S(2)}, u32[]{:S(2)}) %collective-permute-start.2) | collective-permute-done | bytes 614432 | tf_op jit(solution)/shard_map/ppermute | solution.py:16
  85.0 1.0 shard_map.50
  86.0 4.4 %collective-permute-start.3 = (bf16[208,768]{1,0:T(8,128)(2,1)S(1)}, bf16[208,768]{1,0:T(8,128)(2,1)S(1)}, u32[]{:S(2)}, u32[]{:S(2)}) collective-permute-start(bf16[208,768]{1,0:T(8,128)(2,1)S(1)} %get-tuple-element.18), channel_id=1, source_target_pairs={{0,48},{16,32},{32,16},{48,0},{64,112},{80,96},{96,80},{112,64},{1... | collective-permute-start | bytes 958472 | tf_op jit(solution)/shard_map/ppermute | solution.py:16
  90.4 8.3 %collective-permute-done.3.got._ = bf16[208,768]{1,0:T(8,128)(2,1)S(1)} collective-permute-done((bf16[208,768]{1,0:T(8,128)(2,1)S(1)}, bf16[208,768]{1,0:T(8,128)(2,1)S(1)}, u32[]{:S(2)}, u32[]{:S(2)}) %collective-permute-start.3) | collective-permute-done | bytes 319520 | tf_op jit(solution)/shard_map/ppermute | solution.py:16
  98.7 2.0 %grad_weight.1 = (f32[384,1152]{1,0:T(8,128)S(1)}, f32[384,1152]{1,0:T(8,128)S(1)}) custom-call(s32[1]{0:T(128)} %bitcast.2.row_ref, bf16[208,768]{1,0:T(8,128)(2,1)S(1)} %collective-permute-done.3.got._, bf16[768,1152]{1,0:T(8,128)(2,1)S(1)} %get-tuple-element.23.grads, bf16[384,768]{1,0:T(8,128)(2,1)S(1)} %constant_dynamic-update-slice_fusion.near, ...), custom_call_target="tpu_custom_call" | custom-call | flops 1358954496 | bytes 7340032 | tf_op jit(solution)/shard_map/grad_weight/pallas_call | solution.py:195
  100.7 6.7 %collective-permute-start.11 = (f32[384,1152]{1,0:T(8,128)S(1)}, f32[384,1152]{1,0:T(8,128)S(1)}, u32[]{:S(2)}, u32[]{:S(2)}) collective-permute-start(f32[384,1152]{1,0:T(8,128)S(1)} %get-tuple-element.25), channel_id=1, source_target_pairs={{0,256},{256,0},{512,768},{768,512},{1,257},{257,1},{513,769},{769... | collective-permute-start | bytes 5308424 | tf_op jit(solution)/shard_map/ppermute | solution.py:24
  107.9 4.0 %collective-permute-start.4 = (bf16[112,768]{1,0:T(8,128)(2,1)S(1)}, bf16[112,768]{1,0:T(8,128)(2,1)S(1)}, u32[]{:S(2)}, u32[]{:S(2)}) collective-permute-start(bf16[112,768]{1,0:T(8,128)(2,1)S(1)} %get-tuple-element.20), channel_id=1, source_target_pairs={{0,64},{16,80},{32,96},{48,112},{64,0},{80,16},{96,32},{112,48},{1... | collective-permute-start | bytes 516104 | tf_op jit(solution)/shard_map/ppermute | solution.py:20
  112.7 3.2 %collective-permute-start.12 = (bf16[208,1152]{1,0:T(8,128)(2,1)S(1)}, bf16[208,1152]{1,0:T(8,128)(2,1)S(1)}, u32[]{:S(2)}, u32[]{:S(2)}) collective-permute-start(bf16[208,1152]{1,0:T(8,128)(2,1)S(1)} %get-tuple-element.27), channel_id=1, source_target_pairs={{0,512},{256,768},{512,0},{768,256},{1,513},{257,769},{513,1},{769... | collective-permute-start | bytes 1437704 | tf_op jit(solution)/shard_map/ppermute | solution.py:24
  115.9 4.5 %collective-permute-done.4.got = bf16[112,768]{1,0:T(8,128)(2,1)S(1)} collective-permute-done((bf16[112,768]{1,0:T(8,128)(2,1)S(1)}, bf16[112,768]{1,0:T(8,128)(2,1)S(1)}, u32[]{:S(2)}, u32[]{:S(2)}) %collective-permute-start.4) | collective-permute-done | bytes 172064 | tf_op jit(solution)/shard_map/ppermute | solution.py:20
  120.7 4.6 %collective-permute-start.5 = (bf16[64,768]{1,0:T(8,128)(2,1)S(1)}, bf16[64,768]{1,0:T(8,128)(2,1)S(1)}, u32[]{:S(2)}, u32[]{:S(2)}) collective-permute-start(bf16[64,768]{1,0:T(8,128)(2,1)S(1)} %get-tuple-element.22), channel_id=1, source_target_pairs={{0,192},{16,208},{32,224},{48,240},{64,128},{80,144},{96,160},{112... | collective-permute-start | bytes 294920 | tf_op jit(solution)/shard_map/ppermute | solution.py:20
  125.3 8.9 %collective-permute-done.5.got = bf16[64,768]{1,0:T(8,128)(2,1)S(1)} collective-permute-done((bf16[64,768]{1,0:T(8,128)(2,1)S(1)}, bf16[64,768]{1,0:T(8,128)(2,1)S(1)}, u32[]{:S(2)}, u32[]{:S(2)}) %collective-permute-start.5) | collective-permute-done | bytes 98336 | tf_op jit(solution)/shard_map/ppermute | solution.py:20
  134.9 1.3 shard_map.55
  (21 shorter events, 6.9 us)
Async XLA Ops:
  0.6 68.0 %copy-start = (bf16[768,1152]{1,0:T(8,128)(2,1)S(1)}, bf16[768,1152]{1,0:T(8,128)(2,1)}, u32[]{:S(2)}) copy-start(bf16[768,1152]{1,0:T(8,128)(2,1)} %weight_ref.1) | copy-start | bytes 5308420
  0.6 61.4 %collective-permute-start.8 = (bf16[48,768]{1,0:T(8,128)(2,1)}, bf16[48,768]{1,0:T(8,128)(2,1)}, u32[]{:S(2)}, u32[]{:S(2)}) collective-permute-start(bf16[48,768]{1,0:T(8,128)(2,1)} %param.3), channel_id=1, source_target_pairs={{0,128},{16,144},{32,160},{48,176},{64,192},{80,208},{96,224},{112... | collective-permute-start | bytes 221192 | tf_op jit(solution)/shard_map/ppermute | solution.py:20
  9.1 53.0 %collective-permute-start.7 = (bf16[48,768]{1,0:T(8,128)(2,1)}, bf16[48,768]{1,0:T(8,128)(2,1)}, u32[]{:S(2)}, u32[]{:S(2)}) collective-permute-start(bf16[48,768]{1,0:T(8,128)(2,1)} %param.3), channel_id=1, source_target_pairs={{0,192},{16,208},{32,224},{48,240},{64,128},{80,144},{96,160},{112... | collective-permute-start | bytes 221192 | tf_op jit(solution)/shard_map/ppermute | solution.py:20
  11.0 51.0 %collective-permute-start.6 = (bf16[48,768]{1,0:T(8,128)(2,1)}, bf16[48,768]{1,0:T(8,128)(2,1)}, u32[]{:S(2)}, u32[]{:S(2)}) collective-permute-start(bf16[48,768]{1,0:T(8,128)(2,1)} %param.3), channel_id=1, source_target_pairs={{0,64},{16,80},{32,96},{48,112},{64,0},{80,16},{96,32},{112,48},{1... | collective-permute-start | bytes 221192 | tf_op jit(solution)/shard_map/ppermute | solution.py:20
  53.3 13.1 %collective-permute-start.1 = (bf16[192,1152]{1,0:T(8,128)(2,1)}, bf16[192,1152]{1,0:T(8,128)(2,1)S(1)}, u32[]{:S(2)}, u32[]{:S(2)}) collective-permute-start(bf16[192,1152]{1,0:T(8,128)(2,1)} %get-tuple-element.28), channel_id=1, source_target_pairs={{0,15},{1,2},{2,1},{3,4},{4,3},{5,6},{6,5},{7,8},{8,7},{9,10},{10,... | collective-permute-start | bytes 1327112 | tf_op jit(solution)/shard_map/ppermute | solution.py:168
  59.1 9.6 %collective-permute-start = (bf16[192,1152]{1,0:T(8,128)(2,1)}, bf16[192,1152]{1,0:T(8,128)(2,1)S(1)}, u32[]{:S(2)}, u32[]{:S(2)}) collective-permute-start(bf16[192,1152]{1,0:T(8,128)(2,1)} %get-tuple-element.29), channel_id=1, source_target_pairs={{0,1},{1,0},{2,3},{3,2},{4,5},{5,4},{6,7},{7,6},{8,9},{9,8},{10,11... | collective-permute-start | bytes 1327112 | tf_op jit(solution)/shard_map/ppermute | solution.py:167
  63.0 12.8 %collective-permute-start.9 = (bf16[192,768]{1,0:T(8,128)(2,1)S(1)}, bf16[192,768]{1,0:T(8,128)(2,1)S(1)}, u32[]{:S(2)}, u32[]{:S(2)}) collective-permute-start(bf16[192,768]{1,0:T(8,128)(2,1)S(1)} %pad_maximum_fusion), channel_id=1, source_target_pairs={{0,16},{16,0},{32,48},{48,32},{64,80},{80,64},{96,112},{112,96},{1... | collective-permute-start | bytes 884744 | tf_op jit(solution)/shard_map/ppermute | solution.py:16
  71.7 13.3 %collective-permute-start.2 = (bf16[400,768]{1,0:T(8,128)(2,1)S(1)}, bf16[400,768]{1,0:T(8,128)(2,1)S(1)}, u32[]{:S(2)}, u32[]{:S(2)}) collective-permute-start(bf16[400,768]{1,0:T(8,128)(2,1)S(1)} %get-tuple-element.16), channel_id=1, source_target_pairs={{0,16},{16,0},{32,48},{48,32},{64,80},{80,64},{96,112},{112,96},{1... | collective-permute-start | bytes 1843208 | tf_op jit(solution)/shard_map/ppermute | solution.py:16
  75.9 14.5 %collective-permute-start.10 = (bf16[384,768]{1,0:T(8,128)(2,1)S(1)}, bf16[384,768]{1,0:T(8,128)(2,1)S(1)}, u32[]{:S(2)}, u32[]{:S(2)}) collective-permute-start(bf16[384,768]{1,0:T(8,128)(2,1)S(1)} %constant_dynamic-update-slice_fusion.near), channel_id=1, source_target_pairs={{0,48},{16,32},{32,16},{48,0},{64,112},{80,96},{96,80},{112,64},{1... | collective-permute-start | bytes 1769480 | tf_op jit(solution)/shard_map/ppermute | solution.py:16
  86.0 12.7 %collective-permute-start.3 = (bf16[208,768]{1,0:T(8,128)(2,1)S(1)}, bf16[208,768]{1,0:T(8,128)(2,1)S(1)}, u32[]{:S(2)}, u32[]{:S(2)}) collective-permute-start(bf16[208,768]{1,0:T(8,128)(2,1)S(1)} %get-tuple-element.18), channel_id=1, source_target_pairs={{0,48},{16,32},{32,16},{48,0},{64,112},{80,96},{96,80},{112,64},{1... | collective-permute-start | bytes 958472 | tf_op jit(solution)/shard_map/ppermute | solution.py:16
  100.7 11.2 %collective-permute-start.11 = (f32[384,1152]{1,0:T(8,128)S(1)}, f32[384,1152]{1,0:T(8,128)S(1)}, u32[]{:S(2)}, u32[]{:S(2)}) collective-permute-start(f32[384,1152]{1,0:T(8,128)S(1)} %get-tuple-element.25), channel_id=1, source_target_pairs={{0,256},{256,0},{512,768},{768,512},{1,257},{257,1},{513,769},{769... | collective-permute-start | bytes 5308424 | tf_op jit(solution)/shard_map/ppermute | solution.py:24
  107.9 12.5 %collective-permute-start.4 = (bf16[112,768]{1,0:T(8,128)(2,1)S(1)}, bf16[112,768]{1,0:T(8,128)(2,1)S(1)}, u32[]{:S(2)}, u32[]{:S(2)}) collective-permute-start(bf16[112,768]{1,0:T(8,128)(2,1)S(1)} %get-tuple-element.20), channel_id=1, source_target_pairs={{0,64},{16,80},{32,96},{48,112},{64,0},{80,16},{96,32},{112,48},{1... | collective-permute-start | bytes 516104 | tf_op jit(solution)/shard_map/ppermute | solution.py:20
  112.7 22.2 %collective-permute-start.12 = (bf16[208,1152]{1,0:T(8,128)(2,1)S(1)}, bf16[208,1152]{1,0:T(8,128)(2,1)S(1)}, u32[]{:S(2)}, u32[]{:S(2)}) collective-permute-start(bf16[208,1152]{1,0:T(8,128)(2,1)S(1)} %get-tuple-element.27), channel_id=1, source_target_pairs={{0,512},{256,768},{512,0},{768,256},{1,513},{257,769},{513,1},{769... | collective-permute-start | bytes 1437704 | tf_op jit(solution)/shard_map/ppermute | solution.py:24
  120.7 13.5 %collective-permute-start.5 = (bf16[64,768]{1,0:T(8,128)(2,1)S(1)}, bf16[64,768]{1,0:T(8,128)(2,1)S(1)}, u32[]{:S(2)}, u32[]{:S(2)}) collective-permute-start(bf16[64,768]{1,0:T(8,128)(2,1)S(1)} %get-tuple-element.22), channel_id=1, source_target_pairs={{0,192},{16,208},{32,224},{48,240},{64,128},{80,144},{96,160},{112... | collective-permute-start | bytes 294920 | tf_op jit(solution)/shard_map/ppermute | solution.py:20

commit v12 on v11

--- a/solution.py
+++ b/solution.py
@@ -127,10 +127,10 @@
     )(*operands)
 
 
-def grad_weight_kernel(row_ref, _, grads, near, far, sent, kept, tokens, total):
-    quarter = near.shape[0] // 2
-    for slot, (ref, at) in enumerate(((near, quarter), (far, quarter), (near, 0), (far, 0))):
-        tokens[pl.ds(slot * quarter, quarter), :] = ref[pl.ds(at, quarter), :]
+def grad_weight_kernel(row_ref, _, grads, x1, x2, x0, x3, sent, kept, tokens, total):
+    quarter = x0.shape[0]
+    for slot, ref in enumerate((x1, x2, x0, x3)):
+        tokens[pl.ds(slot * quarter, quarter), :] = ref[...]
     total[...] = lax.dot_general(
         tokens[...], grads[...], (((0,), (0,)), ((), ())), preferred_element_type=F32
     )
@@ -152,7 +152,6 @@
     columns = weight.shape[1]
     tokens = block * 16
     depth, col, row = (lax.axis_index(a) for a in ("depth", "col", "row"))
-    ring = [inputs] + [swap_y(inputs, j) for j in ORDER[1:]]
     own = lax.all_gather(
         grad_out,
         ("row", "depth"),
@@ -164,12 +163,14 @@
             for parity in range(2)
         ],
     )
+    own, inputs = lax.optimization_barrier((own, inputs))
     near = lax.ppermute(own[: tokens // 4], "depth", [(i, i ^ 1) for i in range(16)])
     far = lax.ppermute(own[tokens // 4 :], "depth", [(i, ((i + 1) ^ 1) - 1 & 15) for i in range(16)])
     grads = (own, near, far)
-    along_y = jnp.concatenate(ring)
-    near_in = jnp.concatenate([along_y, swap_x(along_y, 1)])
-    far_in = swap_x(near_in, 3)
+    ring = [inputs] + [swap_y(inputs, j) for j in ORDER[1:]]
+    x0 = jnp.concatenate(ring)
+    x1, x3 = swap_x(x0, 1), swap_x(x0, 3)
+    x2 = swap_x(x3, 1)
 
     def plain(rows, cols=width):
         return jax.ShapeDtypeStruct((rows, cols), F32)
@@ -195,7 +196,7 @@
     send_w, keep_w = pl.pallas_call(
         grad_weight_kernel,
         out_shape=[plain(width // 2, columns)] * 2,
-        in_specs=[SMEM, pl.BlockSpec(memory_space=pl.ANY)] + [VMEM] * 3,
+        in_specs=[SMEM, pl.BlockSpec(memory_space=pl.ANY)] + [VMEM] * 5,
         out_specs=[VMEM] * 2,
         scratch_shapes=[pltpu.VMEM((tokens, width), BF16), pltpu.VMEM((width, columns), F32)],
         compiler_params=pltpu.CompilerParams(vmem_limit_bytes=9 << 20),
@@ -203,14 +204,14 @@
             flops=2 * tokens * width * columns, bytes_accessed=7 << 20, transcendentals=0
         ),
         name="grad_weight",
-    )(row.reshape(1), got, ordered, near_in, far_in)
+    )(row.reshape(1), got, ordered, x1, x2, x0, x3)
     rows = width // 4
     got_w = swap_row(send_w, 1)
     sent, kept = stage(y_stage_kernel, coded(tokens // 8), plain(tokens // 8), kept, got)
     sent_w, kept_w = stage(sum_weight_kernel, coded(rows, columns), plain(rows, columns), keep_w, got_w)
     got_w = swap_row(sent_w, 2)
     got = swap_y(sent, 1)
-    sent, kept = stage(last_stage_kernel, coded(block), plain(block), kept, got, weight=8 << 30)
+    sent, kept = stage(last_stage_kernel, coded(block), plain(block), kept, got, weight=16 << 30)
     got = swap_y(sent, 3)
     grad_weight = finish(kept_w, got_w)
     return finish(kept, got), grad_weight

time: 137 us -> 137 us (level)
  waiting for transfers between devices: 29.4 us -> 19.1 us
  starting transfers between devices: 51.9 us -> 59.7 us
  blocking collectives: 38.9 us -> 42.9 us
    ppermute x4 -> x5, waiting for transfers between devices: 13.7 us -> 5.8 us  [swap_x(): return lax.ppermute(value, 'col', [(i, i ^ j) for i in range(16)])]
    ppermute x2, starting transfers between devices: 9.89 us -> 17.4 us  [swap_row(): return lax.ppermute(value, 'row', [(i, i ^ j) for i in range(4)])]
    all_gather x1, blocking collectives: 38.9 us -> 42.9 us  [per_device(): lax.all_gather(grad_out, ('row', 'depth'), axis=0, tiled=True, axis_index...]
    ppermute x4 -> x5, starting transfers between devices: 13 us -> 16.5 us  [swap_x(): return lax.ppermute(value, 'col', [(i, i ^ j) for i in range(16)])]
    ppermute x1, starting transfers between devices: 5.8 us -> 3.23 us  [per_device(): lax.ppermute(own[tokens // 4:], 'depth', [(i, (i + 1 ^ 1) - 1 & 15) for i...]
    ppermute x1, waiting for transfers between devices: 2.29 us -> 0.01 us  [per_device(): lax.ppermute(own[:tokens // 4], 'depth', [(i, i ^ 1) for i in range(16)])]
    unnamed x6 -> x5, local copies, waits for them, and re-layouts: 3.57 us -> 2.68 us
  transfers between devices with their start and end apart: 13 -> 14, of which waited for: 5 -> 5; matrix products, arithmetic and copies ran while one was open for 4% -> 3% of each run, Pallas kernels for 5% -> 5%
where the time goes in v12:
time: 137 us
  starting transfers between devices  59.7 us (44%)
  blocking collectives  42.9 us (31%)
  waiting for transfers between devices  19.1 us (14%)
  Pallas kernels  9.6 us (7%)
  local copies, waits for them, and re-layouts  4.55 us (3%)
    all_gather x1, blocking collectives, per_device(): lax.all_gather(grad_out, ('row', 'depth'), axis=0, tiled=True, axis_index...  42.9 us
    ppermute x5, starting transfers between devices, swap_y(): return lax.ppermute(value, 'col', [(i, i ^ 4 * j) for i in range(16)])  20.6 us
    ppermute x2, starting transfers between devices, swap_row(): return lax.ppermute(value, 'row', [(i, i ^ j) for i in range(4)])  17.4 us
    ppermute x5, starting transfers between devices, swap_x(): return lax.ppermute(value, 'col', [(i, i ^ j) for i in range(16)])  16.5 us
    ppermute x5, waiting for transfers between devices, swap_y(): return lax.ppermute(value, 'col', [(i, i ^ 4 * j) for i in range(16)])  13.3 us
    ppermute x5, waiting for transfers between devices, swap_x(): return lax.ppermute(value, 'col', [(i, i ^ j) for i in range(16)])  5.8 us
    ppermute x1, starting transfers between devices, per_device(): lax.ppermute(own[tokens // 4:], 'depth', [(i, (i + 1 ^ 1) - 1 & 15) for i...  3.23 us
    pallas_call x1, Pallas kernels, per_device(): pl.pallas_call(grad_inputs_kernel, out_shape=[coded(tokens // 2), plain(t...  2.98 us
  transfers between devices with their start and end apart: 14, of which 5 were waited for; matrix products, arithmetic and copies ran while one was open for 3% of the time, Pallas kernels for 5%

profile of v12, /device:TPU:1, one launch (start us, length us, event | category | flops | bytes accessed | tf_op | source)
XLA Modules:
  0.0 136.7 jit_solution(9975160046055593338)
XLA Ops:
  0.6 42.9 %all_gather.3.own = bf16[384,1152]{1,0:T(8,128)(2,1)S(1)} all-gather(bf16[48,1152]{1,0:T(8,128)(2,1)} %param.5), channel_id=1, replica_groups={{0,2,4,6,8,10,12,14},{1,3,5,7,9,11,13,15},{270,268,266,264,262,260,258,..., dimensions={0}, use_global_device_ids=true | all-gather | bytes 995328 | tf_op jit(solution)/shard_map/all_gather | solution.py:155
  43.6 1.0 fusion
  44.6 3.2 %collective-permute-start.1 = (bf16[192,1152]{1,0:T(8,128)(2,1)}, bf16[192,1152]{1,0:T(8,128)(2,1)S(1)}, u32[]{:S(2)}, u32[]{:S(2)}) collective-permute-start(bf16[192,1152]{1,0:T(8,128)(2,1)} %get-tuple-element.32), channel_id=1, source_target_pairs={{0,15},{1,2},{2,1},{3,4},{4,3},{5,6},{6,5},{7,8},{8,7},{9,10},{10,... | collective-permute-start | bytes 1327112 | tf_op jit(solution)/shard_map/ppermute | solution.py:168
  47.8 1.9 %collective-permute-start = (bf16[192,1152]{1,0:T(8,128)(2,1)}, bf16[192,1152]{1,0:T(8,128)(2,1)S(1)}, u32[]{:S(2)}, u32[]{:S(2)}) collective-permute-start(bf16[192,1152]{1,0:T(8,128)(2,1)} %get-tuple-element.33), channel_id=1, source_target_pairs={{0,1},{1,0},{2,3},{3,2},{4,5},{5,4},{6,7},{7,6},{8,9},{9,8},{10,11... | collective-permute-start | bytes 1327112 | tf_op jit(solution)/shard_map/ppermute | solution.py:167
  49.7 7.2 %collective-permute-start.8 = (bf16[48,768]{1,0:T(8,128)(2,1)}, bf16[48,768]{1,0:T(8,128)(2,1)}, u32[]{:S(2)}, u32[]{:S(2)}) collective-permute-start(bf16[48,768]{1,0:T(8,128)(2,1)} %param.3), channel_id=1, source_target_pairs={{0,128},{16,144},{32,160},{48,176},{64,192},{80,208},{96,224},{112... | collective-permute-start | bytes 221192 | tf_op jit(solution)/shard_map/ppermute | solution.py:20
  56.9 2.0 %collective-permute-start.7 = (bf16[48,768]{1,0:T(8,128)(2,1)}, bf16[48,768]{1,0:T(8,128)(2,1)}, u32[]{:S(2)}, u32[]{:S(2)}) collective-permute-start(bf16[48,768]{1,0:T(8,128)(2,1)} %param.3), channel_id=1, source_target_pairs={{0,192},{16,208},{32,224},{48,240},{64,128},{80,144},{96,160},{112... | collective-permute-start | bytes 221192 | tf_op jit(solution)/shard_map/ppermute | solution.py:20
  58.9 2.4 %collective-permute-start.6 = (bf16[48,768]{1,0:T(8,128)(2,1)}, bf16[48,768]{1,0:T(8,128)(2,1)}, u32[]{:S(2)}, u32[]{:S(2)}) collective-permute-start(bf16[48,768]{1,0:T(8,128)(2,1)} %param.3), channel_id=1, source_target_pairs={{0,64},{16,80},{32,96},{48,112},{64,0},{80,16},{96,32},{112,48},{1... | collective-permute-start | bytes 221192 | tf_op jit(solution)/shard_map/ppermute | solution.py:20
  61.3 3.0 %grad_inputs.1 = (bf16[400,768]{1,0:T(8,128)(2,1)S(1)}, f32[384,768]{1,0:T(8,128)S(1)}, bf16[768,1152]{1,0:T(8,128)(2,1)S(1)}) custom-call(s32[3]{0:T(128)S(1)} %pad_add_fusion.place_ref, bf16[384,1152]{1,0:T(8,128)(2,1)S(1)} %all_gather.3.own, bf16[192,1152]{1,0:T(8,128)(2,1)S(1)} %collective-permute-done.near, ...), custom_call_target="tpu_custom_call" | custom-call | flops 1358954496 | bytes 6291456 | tf_op jit(solution)/shard_map/grad_inputs/pallas_call | solution.py:181
  64.3 3.1 %collective-permute-start.2 = (bf16[400,768]{1,0:T(8,128)(2,1)S(1)}, bf16[400,768]{1,0:T(8,128)(2,1)S(1)}, u32[]{:S(2)}, u32[]{:S(2)}) collective-permute-start(bf16[400,768]{1,0:T(8,128)(2,1)S(1)} %get-tuple-element.19), channel_id=1, source_target_pairs={{0,16},{16,0},{32,48},{48,32},{64,80},{80,64},{96,112},{112,96},{1... | collective-permute-start | bytes 1843208 | tf_op jit(solution)/shard_map/ppermute | solution.py:16
  71.0 3.7 %collective-permute-start.10 = (bf16[192,768]{1,0:T(8,128)(2,1)S(1)}, bf16[192,768]{1,0:T(8,128)(2,1)S(1)}, u32[]{:S(2)}, u32[]{:S(2)}) collective-permute-start(bf16[192,768]{1,0:T(8,128)(2,1)S(1)} %constant_dynamic-update-slice_fusion.x0), channel_id=1, source_target_pairs={{0,48},{16,32},{32,16},{48,0},{64,112},{80,96},{96,80},{112,64},{1... | collective-permute-start | bytes 884744 | tf_op jit(solution)/shard_map/ppermute | solution.py:16
  75.2 1.0 shard_map.50
  76.3 4.4 %collective-permute-start.3 = (bf16[208,768]{1,0:T(8,128)(2,1)S(1)}, bf16[208,768]{1,0:T(8,128)(2,1)S(1)}, u32[]{:S(2)}, u32[]{:S(2)}) collective-permute-start(bf16[208,768]{1,0:T(8,128)(2,1)S(1)} %get-tuple-element.21), channel_id=1, source_target_pairs={{0,48},{16,32},{32,16},{48,0},{64,112},{80,96},{96,80},{112,64},{1... | collective-permute-start | bytes 958472 | tf_op jit(solution)/shard_map/ppermute | solution.py:16
  80.6 1.9 %collective-permute-start.9 = (bf16[192,768]{1,0:T(8,128)(2,1)S(1)}, bf16[192,768]{1,0:T(8,128)(2,1)S(1)}, u32[]{:S(2)}, u32[]{:S(2)}) collective-permute-start(bf16[192,768]{1,0:T(8,128)(2,1)S(1)} %constant_dynamic-update-slice_fusion.x0), channel_id=1, source_target_pairs={{0,16},{16,0},{32,48},{48,32},{64,80},{80,64},{96,112},{112,96},{1... | collective-permute-start | bytes 884744 | tf_op jit(solution)/shard_map/ppermute | solution.py:16
  82.6 3.4 %collective-permute-start.11 = (bf16[192,768]{1,0:T(8,128)(2,1)S(1)}, bf16[192,768]{1,0:T(8,128)(2,1)S(1)}, u32[]{:S(2)}, u32[]{:S(2)}) collective-permute-start(bf16[192,768]{1,0:T(8,128)(2,1)S(1)} %collective-permute-done.10.x3), channel_id=1, source_target_pairs={{0,16},{16,0},{32,48},{48,32},{64,80},{80,64},{96,112},{112,96},{1... | collective-permute-start | bytes 884744 | tf_op jit(solution)/shard_map/ppermute | solution.py:16
  86.0 2.5 %collective-permute-done.9.x1 = bf16[192,768]{1,0:T(8,128)(2,1)S(1)} collective-permute-done((bf16[192,768]{1,0:T(8,128)(2,1)S(1)}, bf16[192,768]{1,0:T(8,128)(2,1)S(1)}, u32[]{:S(2)}, u32[]{:S(2)}) %collective-permute-start.9) | collective-permute-done | bytes 294944 | tf_op jit(solution)/shard_map/ppermute | solution.py:16
  88.4 2.9 %collective-permute-done.11.x2 = bf16[192,768]{1,0:T(8,128)(2,1)S(1)} collective-permute-done((bf16[192,768]{1,0:T(8,128)(2,1)S(1)}, bf16[192,768]{1,0:T(8,128)(2,1)S(1)}, u32[]{:S(2)}, u32[]{:S(2)}) %collective-permute-start.11) | collective-permute-done | bytes 294944 | tf_op jit(solution)/shard_map/ppermute | solution.py:16
  91.3 2.0 %grad_weight.1 = (f32[384,1152]{1,0:T(8,128)S(1)}, f32[384,1152]{1,0:T(8,128)S(1)}) custom-call(s32[1]{0:T(128)} %bitcast.2.row_ref, bf16[208,768]{1,0:T(8,128)(2,1)S(1)} %collective-permute-done.3.got._, bf16[768,1152]{1,0:T(8,128)(2,1)S(1)} %get-tuple-element.26.grads, bf16[192,768]{1,0:T(8,128)(2,1)S(1)} %collective-permute-done.9.x1, ...), custom_call_target="tpu_custom_call" | custom-call | flops 1358954496 | bytes 7340032 | tf_op jit(solution)/shard_map/grad_weight/pallas_call | solution.py:196
  93.3 14.2 %collective-permute-start.12 = (f32[384,1152]{1,0:T(8,128)S(1)}, f32[384,1152]{1,0:T(8,128)S(1)}, u32[]{:S(2)}, u32[]{:S(2)}) collective-permute-start(f32[384,1152]{1,0:T(8,128)S(1)} %get-tuple-element.29), channel_id=1, source_target_pairs={{0,256},{256,0},{512,768},{768,512},{1,257},{257,1},{513,769},{769... | collective-permute-start | bytes 5308424 | tf_op jit(solution)/shard_map/ppermute | solution.py:24
  108.0 4.4 %collective-permute-start.4 = (bf16[112,768]{1,0:T(8,128)(2,1)S(1)}, bf16[112,768]{1,0:T(8,128)(2,1)S(1)}, u32[]{:S(2)}, u32[]{:S(2)}) collective-permute-start(bf16[112,768]{1,0:T(8,128)(2,1)S(1)} %get-tuple-element.23), channel_id=1, source_target_pairs={{0,64},{16,80},{32,96},{48,112},{64,0},{80,16},{96,32},{112,48},{1... | collective-permute-start | bytes 516104 | tf_op jit(solution)/shard_map/ppermute | solution.py:20
  113.1 3.2 %collective-permute-start.13 = (bf16[208,1152]{1,0:T(8,128)(2,1)S(1)}, bf16[208,1152]{1,0:T(8,128)(2,1)S(1)}, u32[]{:S(2)}, u32[]{:S(2)}) collective-permute-start(bf16[208,1152]{1,0:T(8,128)(2,1)S(1)} %get-tuple-element.31), channel_id=1, source_target_pairs={{0,512},{256,768},{512,0},{768,256},{1,513},{257,769},{513,1},{769... | collective-permute-start | bytes 1437704 | tf_op jit(solution)/shard_map/ppermute | solution.py:24
  116.3 4.4 %collective-permute-done.4.got = bf16[112,768]{1,0:T(8,128)(2,1)S(1)} collective-permute-done((bf16[112,768]{1,0:T(8,128)(2,1)S(1)}, bf16[112,768]{1,0:T(8,128)(2,1)S(1)}, u32[]{:S(2)}, u32[]{:S(2)}) %collective-permute-start.4) | collective-permute-done | bytes 172064 | tf_op jit(solution)/shard_map/ppermute | solution.py:20
  121.0 4.7 %collective-permute-start.5 = (bf16[64,768]{1,0:T(8,128)(2,1)S(1)}, bf16[64,768]{1,0:T(8,128)(2,1)S(1)}, u32[]{:S(2)}, u32[]{:S(2)}) collective-permute-start(bf16[64,768]{1,0:T(8,128)(2,1)S(1)} %get-tuple-element.25), channel_id=1, source_target_pairs={{0,192},{16,208},{32,224},{48,240},{64,128},{80,144},{96,160},{112... | collective-permute-start | bytes 294920 | tf_op jit(solution)/shard_map/ppermute | solution.py:20
  125.8 8.9 %collective-permute-done.5.got = bf16[64,768]{1,0:T(8,128)(2,1)S(1)} collective-permute-done((bf16[64,768]{1,0:T(8,128)(2,1)S(1)}, bf16[64,768]{1,0:T(8,128)(2,1)S(1)}, u32[]{:S(2)}, u32[]{:S(2)}) %collective-permute-start.5) | collective-permute-done | bytes 98336 | tf_op jit(solution)/shard_map/ppermute | solution.py:20
  135.4 1.4 %shard_map.55 = bf16[192,1152]{1,0:T(8,128)(2,1)} custom-call(f32[192,1152]{1,0:T(8,128)S(1)} %get-tuple-element.30.mine, bf16[208,1152]{1,0:T(8,128)(2,1)S(1)} %collective-permute-done.13.got), custom_call_target="tpu_custom_call" | custom-call | tf_op jit(solution)/shard_map/pallas_call | solution.py:110
  (21 shorter events, 6.4 us)
Async XLA Ops:
  0.6 60.7 %copy-start = (bf16[768,1152]{1,0:T(8,128)(2,1)S(1)}, bf16[768,1152]{1,0:T(8,128)(2,1)}, u32[]{:S(2)}) copy-start(bf16[768,1152]{1,0:T(8,128)(2,1)} %weight_ref.1) | copy-start | bytes 5308420
  44.6 16.8 %collective-permute-start.1 = (bf16[192,1152]{1,0:T(8,128)(2,1)}, bf16[192,1152]{1,0:T(8,128)(2,1)S(1)}, u32[]{:S(2)}, u32[]{:S(2)}) collective-permute-start(bf16[192,1152]{1,0:T(8,128)(2,1)} %get-tuple-element.32), channel_id=1, source_target_pairs={{0,15},{1,2},{2,1},{3,4},{4,3},{5,6},{6,5},{7,8},{8,7},{9,10},{10,... | collective-permute-start | bytes 1327112 | tf_op jit(solution)/shard_map/ppermute | solution.py:168
  47.8 13.5 %collective-permute-start = (bf16[192,1152]{1,0:T(8,128)(2,1)}, bf16[192,1152]{1,0:T(8,128)(2,1)S(1)}, u32[]{:S(2)}, u32[]{:S(2)}) collective-permute-start(bf16[192,1152]{1,0:T(8,128)(2,1)} %get-tuple-element.33), channel_id=1, source_target_pairs={{0,1},{1,0},{2,3},{3,2},{4,5},{5,4},{6,7},{7,6},{8,9},{9,8},{10,11... | collective-permute-start | bytes 1327112 | tf_op jit(solution)/shard_map/ppermute | solution.py:167
  49.7 20.4 %collective-permute-start.8 = (bf16[48,768]{1,0:T(8,128)(2,1)}, bf16[48,768]{1,0:T(8,128)(2,1)}, u32[]{:S(2)}, u32[]{:S(2)}) collective-permute-start(bf16[48,768]{1,0:T(8,128)(2,1)} %param.3), channel_id=1, source_target_pairs={{0,128},{16,144},{32,160},{48,176},{64,192},{80,208},{96,224},{112... | collective-permute-start | bytes 221192 | tf_op jit(solution)/shard_map/ppermute | solution.py:20
  56.9 12.4 %collective-permute-start.7 = (bf16[48,768]{1,0:T(8,128)(2,1)}, bf16[48,768]{1,0:T(8,128)(2,1)}, u32[]{:S(2)}, u32[]{:S(2)}) collective-permute-start(bf16[48,768]{1,0:T(8,128)(2,1)} %param.3), channel_id=1, source_target_pairs={{0,192},{16,208},{32,224},{48,240},{64,128},{80,144},{96,160},{112... | collective-permute-start | bytes 221192 | tf_op jit(solution)/shard_map/ppermute | solution.py:20
  58.9 9.5 %collective-permute-start.6 = (bf16[48,768]{1,0:T(8,128)(2,1)}, bf16[48,768]{1,0:T(8,128)(2,1)}, u32[]{:S(2)}, u32[]{:S(2)}) collective-permute-start(bf16[48,768]{1,0:T(8,128)(2,1)} %param.3), channel_id=1, source_target_pairs={{0,64},{16,80},{32,96},{48,112},{64,0},{80,16},{96,32},{112,48},{1... | collective-permute-start | bytes 221192 | tf_op jit(solution)/shard_map/ppermute | solution.py:20
  64.3 10.9 %collective-permute-start.2 = (bf16[400,768]{1,0:T(8,128)(2,1)S(1)}, bf16[400,768]{1,0:T(8,128)(2,1)S(1)}, u32[]{:S(2)}, u32[]{:S(2)}) collective-permute-start(bf16[400,768]{1,0:T(8,128)(2,1)S(1)} %get-tuple-element.19), channel_id=1, source_target_pairs={{0,16},{16,0},{32,48},{48,32},{64,80},{80,64},{96,112},{112,96},{1... | collective-permute-start | bytes 1843208 | tf_op jit(solution)/shard_map/ppermute | solution.py:16
  71.0 11.5 %collective-permute-start.10 = (bf16[192,768]{1,0:T(8,128)(2,1)S(1)}, bf16[192,768]{1,0:T(8,128)(2,1)S(1)}, u32[]{:S(2)}, u32[]{:S(2)}) collective-permute-start(bf16[192,768]{1,0:T(8,128)(2,1)S(1)} %constant_dynamic-update-slice_fusion.x0), channel_id=1, source_target_pairs={{0,48},{16,32},{32,16},{48,0},{64,112},{80,96},{96,80},{112,64},{1... | collective-permute-start | bytes 884744 | tf_op jit(solution)/shard_map/ppermute | solution.py:16
  76.3 15.0 %collective-permute-start.3 = (bf16[208,768]{1,0:T(8,128)(2,1)S(1)}, bf16[208,768]{1,0:T(8,128)(2,1)S(1)}, u32[]{:S(2)}, u32[]{:S(2)}) collective-permute-start(bf16[208,768]{1,0:T(8,128)(2,1)S(1)} %get-tuple-element.21), channel_id=1, source_target_pairs={{0,48},{16,32},{32,16},{48,0},{64,112},{80,96},{96,80},{112,64},{1... | collective-permute-start | bytes 958472 | tf_op jit(solution)/shard_map/ppermute | solution.py:16
  80.6 7.8 %collective-permute-start.9 = (bf16[192,768]{1,0:T(8,128)(2,1)S(1)}, bf16[192,768]{1,0:T(8,128)(2,1)S(1)}, u32[]{:S(2)}, u32[]{:S(2)}) collective-permute-start(bf16[192,768]{1,0:T(8,128)(2,1)S(1)} %constant_dynamic-update-slice_fusion.x0), channel_id=1, source_target_pairs={{0,16},{16,0},{32,48},{48,32},{64,80},{80,64},{96,112},{112,96},{1... | collective-permute-start | bytes 884744 | tf_op jit(solution)/shard_map/ppermute | solution.py:16
  82.6 8.7 %collective-permute-start.11 = (bf16[192,768]{1,0:T(8,128)(2,1)S(1)}, bf16[192,768]{1,0:T(8,128)(2,1)S(1)}, u32[]{:S(2)}, u32[]{:S(2)}) collective-permute-start(bf16[192,768]{1,0:T(8,128)(2,1)S(1)} %collective-permute-done.10.x3), channel_id=1, source_target_pairs={{0,16},{16,0},{32,48},{48,32},{64,80},{80,64},{96,112},{112,96},{1... | collective-permute-start | bytes 884744 | tf_op jit(solution)/shard_map/ppermute | solution.py:16
  93.3 19.1 %collective-permute-start.12 = (f32[384,1152]{1,0:T(8,128)S(1)}, f32[384,1152]{1,0:T(8,128)S(1)}, u32[]{:S(2)}, u32[]{:S(2)}) collective-permute-start(f32[384,1152]{1,0:T(8,128)S(1)} %get-tuple-element.29), channel_id=1, source_target_pairs={{0,256},{256,0},{512,768},{768,512},{1,257},{257,1},{513,769},{769... | collective-permute-start | bytes 5308424 | tf_op jit(solution)/shard_map/ppermute | solution.py:24
  108.0 12.8 %collective-permute-start.4 = (bf16[112,768]{1,0:T(8,128)(2,1)S(1)}, bf16[112,768]{1,0:T(8,128)(2,1)S(1)}, u32[]{:S(2)}, u32[]{:S(2)}) collective-permute-start(bf16[112,768]{1,0:T(8,128)(2,1)S(1)} %get-tuple-element.23), channel_id=1, source_target_pairs={{0,64},{16,80},{32,96},{48,112},{64,0},{80,16},{96,32},{112,48},{1... | collective-permute-start | bytes 516104 | tf_op jit(solution)/shard_map/ppermute | solution.py:20
  113.1 22.2 %collective-permute-start.13 = (bf16[208,1152]{1,0:T(8,128)(2,1)S(1)}, bf16[208,1152]{1,0:T(8,128)(2,1)S(1)}, u32[]{:S(2)}, u32[]{:S(2)}) collective-permute-start(bf16[208,1152]{1,0:T(8,128)(2,1)S(1)} %get-tuple-element.31), channel_id=1, source_target_pairs={{0,512},{256,768},{512,0},{768,256},{1,513},{257,769},{513,1},{769... | collective-permute-start | bytes 1437704 | tf_op jit(solution)/shard_map/ppermute | solution.py:24
  121.0 13.6 %collective-permute-start.5 = (bf16[64,768]{1,0:T(8,128)(2,1)S(1)}, bf16[64,768]{1,0:T(8,128)(2,1)S(1)}, u32[]{:S(2)}, u32[]{:S(2)}) collective-permute-start(bf16[64,768]{1,0:T(8,128)(2,1)S(1)} %get-tuple-element.25), channel_id=1, source_target_pairs={{0,192},{16,208},{32,224},{48,240},{64,128},{80,144},{96,160},{112... | collective-permute-start | bytes 294920 | tf_op jit(solution)/shard_map/ppermute | solution.py:20

commit v13 on v12

--- a/solution.py
+++ b/solution.py
@@ -193,6 +193,8 @@
     sent, kept = stage(x_stage_kernel, coded(tokens // 4), plain(tokens // 4), kept, got)
     got = swap_x(sent, 3)
 
+    sent, kept = stage(y_stage_kernel, coded(tokens // 8), plain(tokens // 8), kept, got)
+    got = swap_y(sent, 1)
     send_w, keep_w = pl.pallas_call(
         grad_weight_kernel,
         out_shape=[plain(width // 2, columns)] * 2,
@@ -207,10 +209,8 @@
     )(row.reshape(1), got, ordered, x1, x2, x0, x3)
     rows = width // 4
     got_w = swap_row(send_w, 1)
-    sent, kept = stage(y_stage_kernel, coded(tokens // 8), plain(tokens // 8), kept, got)
     sent_w, kept_w = stage(sum_weight_kernel, coded(rows, columns), plain(rows, columns), keep_w, got_w)
     got_w = swap_row(sent_w, 2)
-    got = swap_y(sent, 1)
     sent, kept = stage(last_stage_kernel, coded(block), plain(block), kept, got, weight=16 << 30)
     got = swap_y(sent, 3)
     grad_weight = finish(kept_w, got_w)

time: 137 us -> 144 us (1.051)
  waiting for transfers between devices: 19.1 us -> 31.9 us
  local copies, waits for them, and re-layouts: 4.55 us -> 1.01 us
  starting transfers between devices: 59.7 us -> 57.3 us
    ppermute x5, waiting for transfers between devices: 13.3 us -> 19.1 us  [swap_y(): return lax.ppermute(value, 'col', [(i, i ^ 4 * j) for i in range(16)])]
    ppermute x1, waiting for transfers between devices: 0.01 us -> 5.21 us  [per_device(): lax.ppermute(own[tokens // 4:], 'depth', [(i, (i + 1 ^ 1) - 1 & 15) for i...]
    ppermute x5, waiting for transfers between devices: 5.8 us -> 1.96 us  [swap_x(): return lax.ppermute(value, 'col', [(i, i ^ j) for i in range(16)])]
    ppermute x2, waiting for transfers between devices: 0.01 us -> 3.3 us  [swap_row(): return lax.ppermute(value, 'row', [(i, i ^ j) for i in range(4)])]
    unnamed x5 -> x7, local copies, waits for them, and re-layouts: 2.68 us -> 0.03 us
    ppermute x1, waiting for transfers between devices: 0.01 us -> 2.33 us  [per_device(): lax.ppermute(own[:tokens // 4], 'depth', [(i, i ^ 1) for i in range(16)])]
    ppermute x5, starting transfers between devices: 16.5 us -> 14.6 us  [swap_x(): return lax.ppermute(value, 'col', [(i, i ^ j) for i in range(16)])]
  transfers between devices with their start and end apart: 14 -> 14, of which waited for: 5 -> 8; matrix products, arithmetic and copies ran while one was open for 3% -> 0% of each run, Pallas kernels for 5% -> 2%
where the time goes in v13:
time: 144 us
  starting transfers between devices  57.3 us (40%)
  blocking collectives  42.9 us (30%)
  waiting for transfers between devices  31.9 us (22%)
  Pallas kernels  9.6 us (7%)
    all_gather x1, blocking collectives, per_device(): lax.all_gather(grad_out, ('row', 'depth'), axis=0, tiled=True, axis_index...  42.9 us
    ppermute x5, starting transfers between devices, swap_y(): return lax.ppermute(value, 'col', [(i, i ^ 4 * j) for i in range(16)])  20.8 us
    ppermute x5, waiting for transfers between devices, swap_y(): return lax.ppermute(value, 'col', [(i, i ^ 4 * j) for i in range(16)])  19.1 us
    ppermute x2, starting transfers between devices, swap_row(): return lax.ppermute(value, 'row', [(i, i ^ j) for i in range(4)])  16.8 us
    ppermute x5, starting transfers between devices, swap_x(): return lax.ppermute(value, 'col', [(i, i ^ j) for i in range(16)])  14.6 us
    ppermute x1, waiting for transfers between devices, per_device(): lax.ppermute(own[tokens // 4:], 'depth', [(i, (i + 1 ^ 1) - 1 & 15) for i...  5.21 us
    ppermute x2, waiting for transfers between devices, swap_row(): return lax.ppermute(value, 'row', [(i, i ^ j) for i in range(4)])  3.3 us
    ppermute x1, starting transfers between devices, per_device(): lax.ppermute(own[tokens // 4:], 'depth', [(i, (i + 1 ^ 1) - 1 & 15) for i...  3.23 us
  transfers between devices with their start and end apart: 14, of which 8 were waited for; matrix products, arithmetic and copies ran while one was open for 0% of the time, Pallas kernels for 2%

profile of v13, /device:TPU:1, one launch (start us, length us, event | category | flops | bytes accessed | tf_op | source)
XLA Modules:
  0.0 143.7 jit_solution(10964628526427022496)
XLA Ops:
  0.6 42.9 %all_gather.3.own = bf16[384,1152]{1,0:T(8,128)(2,1)S(1)} all-gather(bf16[48,1152]{1,0:T(8,128)(2,1)} %param.5), channel_id=1, replica_groups={{0,2,4,6,8,10,12,14},{1,3,5,7,9,11,13,15},{270,268,266,264,262,260,258,..., dimensions={0}, use_global_device_ids=true | all-gather | bytes 995328 | tf_op jit(solution)/shard_map/all_gather | solution.py:155
  44.5 3.2 %collective-permute-start.1 = (bf16[192,1152]{1,0:T(8,128)(2,1)}, bf16[192,1152]{1,0:T(8,128)(2,1)S(1)}, u32[]{:S(2)}, u32[]{:S(2)}) collective-permute-start(bf16[192,1152]{1,0:T(8,128)(2,1)} %get-tuple-element.32), channel_id=1, source_target_pairs={{0,15},{1,2},{2,1},{3,4},{4,3},{5,6},{6,5},{7,8},{8,7},{9,10},{10,... | collective-permute-start | bytes 1327112 | tf_op jit(solution)/shard_map/ppermute | solution.py:168
  47.8 1.9 %collective-permute-start = (bf16[192,1152]{1,0:T(8,128)(2,1)}, bf16[192,1152]{1,0:T(8,128)(2,1)S(1)}, u32[]{:S(2)}, u32[]{:S(2)}) collective-permute-start(bf16[192,1152]{1,0:T(8,128)(2,1)} %get-tuple-element.33), channel_id=1, source_target_pairs={{0,1},{1,0},{2,3},{3,2},{4,5},{5,4},{6,7},{7,6},{8,9},{9,8},{10,11... | collective-permute-start | bytes 1327112 | tf_op jit(solution)/shard_map/ppermute | solution.py:167
  49.8 5.2 %collective-permute-done.1.far = bf16[192,1152]{1,0:T(8,128)(2,1)S(1)} collective-permute-done((bf16[192,1152]{1,0:T(8,128)(2,1)}, bf16[192,1152]{1,0:T(8,128)(2,1)S(1)}, u32[]{:S(2)}, u32[]{:S(2)}) %collective-permute-start.1) | collective-permute-done | bytes 442400 | tf_op jit(solution)/shard_map/ppermute | solution.py:168
  55.0 2.3 %collective-permute-done.near = bf16[192,1152]{1,0:T(8,128)(2,1)S(1)} collective-permute-done((bf16[192,1152]{1,0:T(8,128)(2,1)}, bf16[192,1152]{1,0:T(8,128)(2,1)S(1)}, u32[]{:S(2)}, u32[]{:S(2)}) %collective-permute-start) | collective-permute-done | bytes 442400 | tf_op jit(solution)/shard_map/ppermute | solution.py:167
  57.3 3.0 %grad_inputs.1 = (bf16[400,768]{1,0:T(8,128)(2,1)S(1)}, f32[384,768]{1,0:T(8,128)S(1)}, bf16[768,1152]{1,0:T(8,128)(2,1)S(1)}) custom-call(s32[3]{0:T(128)S(1)} %pad_add_fusion.place_ref, bf16[384,1152]{1,0:T(8,128)(2,1)S(1)} %all_gather.3.own, bf16[192,1152]{1,0:T(8,128)(2,1)S(1)} %collective-permute-done.near, ...), custom_call_target="tpu_custom_call" | custom-call | flops 1358954496 | bytes 6291456 | tf_op jit(solution)/shard_map/grad_inputs/pallas_call | solution.py:181
  60.3 2.8 %collective-permute-start.2 = (bf16[400,768]{1,0:T(8,128)(2,1)S(1)}, bf16[400,768]{1,0:T(8,128)(2,1)S(1)}, u32[]{:S(2)}, u32[]{:S(2)}) collective-permute-start(bf16[400,768]{1,0:T(8,128)(2,1)S(1)} %get-tuple-element.19), channel_id=1, source_target_pairs={{0,16},{16,0},{32,48},{48,32},{64,80},{80,64},{96,112},{112,96},{1... | collective-permute-start | bytes 1843208 | tf_op jit(solution)/shard_map/ppermute | solution.py:16
  63.1 7.5 %collective-permute-start.8 = (bf16[48,768]{1,0:T(8,128)(2,1)S(1)}, bf16[48,768]{1,0:T(8,128)(2,1)S(1)}, u32[]{:S(2)}, u32[]{:S(2)}) collective-permute-start(bf16[48,768]{1,0:T(8,128)(2,1)S(1)} %copy-done.1), channel_id=1, source_target_pairs={{0,128},{16,144},{32,160},{48,176},{64,192},{80,208},{96,224},{112... | collective-permute-start | bytes 221192 | tf_op jit(solution)/shard_map/ppermute | solution.py:20
  70.6 2.0 %collective-permute-start.7 = (bf16[48,768]{1,0:T(8,128)(2,1)S(1)}, bf16[48,768]{1,0:T(8,128)(2,1)S(1)}, u32[]{:S(2)}, u32[]{:S(2)}) collective-permute-start(bf16[48,768]{1,0:T(8,128)(2,1)S(1)} %copy-done.1), channel_id=1, source_target_pairs={{0,192},{16,208},{32,224},{48,240},{64,128},{80,144},{96,160},{112... | collective-permute-start | bytes 221192 | tf_op jit(solution)/shard_map/ppermute | solution.py:20
  72.6 2.4 %collective-permute-start.6 = (bf16[48,768]{1,0:T(8,128)(2,1)S(1)}, bf16[48,768]{1,0:T(8,128)(2,1)S(1)}, u32[]{:S(2)}, u32[]{:S(2)}) collective-permute-start(bf16[48,768]{1,0:T(8,128)(2,1)S(1)} %copy-done.1), channel_id=1, source_target_pairs={{0,64},{16,80},{32,96},{48,112},{64,0},{80,16},{96,32},{112,48},{1... | collective-permute-start | bytes 221192 | tf_op jit(solution)/shard_map/ppermute | solution.py:20
  75.0 3.6 %collective-permute-done.6 = bf16[48,768]{1,0:T(8,128)(2,1)S(1)} collective-permute-done((bf16[48,768]{1,0:T(8,128)(2,1)S(1)}, bf16[48,768]{1,0:T(8,128)(2,1)S(1)}, u32[]{:S(2)}, u32[]{:S(2)}) %collective-permute-start.6) | collective-permute-done | bytes 73760 | tf_op jit(solution)/shard_map/ppermute | solution.py:20
  78.6 3.7 %collective-permute-start.10 = (bf16[192,768]{1,0:T(8,128)(2,1)S(1)}, bf16[192,768]{1,0:T(8,128)(2,1)S(1)}, u32[]{:S(2)}, u32[]{:S(2)}) collective-permute-start(bf16[192,768]{1,0:T(8,128)(2,1)S(1)} %constant_dynamic-update-slice_fusion.x0), channel_id=1, source_target_pairs={{0,48},{16,32},{32,16},{48,0},{64,112},{80,96},{96,80},{112,64},{1... | collective-permute-start | bytes 884744 | tf_op jit(solution)/shard_map/ppermute | solution.py:16
  83.4 2.8 %collective-permute-start.3 = (bf16[208,768]{1,0:T(8,128)(2,1)S(1)}, bf16[208,768]{1,0:T(8,128)(2,1)S(1)}, u32[]{:S(2)}, u32[]{:S(2)}) collective-permute-start(bf16[208,768]{1,0:T(8,128)(2,1)S(1)} %get-tuple-element.21), channel_id=1, source_target_pairs={{0,48},{16,32},{32,16},{48,0},{64,112},{80,96},{96,80},{112,64},{1... | collective-permute-start | bytes 958472 | tf_op jit(solution)/shard_map/ppermute | solution.py:16
  86.2 1.9 %collective-permute-start.9 = (bf16[192,768]{1,0:T(8,128)(2,1)S(1)}, bf16[192,768]{1,0:T(8,128)(2,1)S(1)}, u32[]{:S(2)}, u32[]{:S(2)}) collective-permute-start(bf16[192,768]{1,0:T(8,128)(2,1)S(1)} %constant_dynamic-update-slice_fusion.x0), channel_id=1, source_target_pairs={{0,16},{16,0},{32,48},{48,32},{64,80},{80,64},{96,112},{112,96},{1... | collective-permute-start | bytes 884744 | tf_op jit(solution)/shard_map/ppermute | solution.py:16
  88.1 3.4 %collective-permute-start.11 = (bf16[192,768]{1,0:T(8,128)(2,1)S(1)}, bf16[192,768]{1,0:T(8,128)(2,1)S(1)}, u32[]{:S(2)}, u32[]{:S(2)}) collective-permute-start(bf16[192,768]{1,0:T(8,128)(2,1)S(1)} %collective-permute-done.10.x3), channel_id=1, source_target_pairs={{0,16},{16,0},{32,48},{48,32},{64,80},{80,64},{96,112},{112,96},{1... | collective-permute-start | bytes 884744 | tf_op jit(solution)/shard_map/ppermute | solution.py:16
  92.8 3.2 %collective-permute-start.4 = (bf16[112,768]{1,0:T(8,128)(2,1)S(1)}, bf16[112,768]{1,0:T(8,128)(2,1)S(1)}, u32[]{:S(2)}, u32[]{:S(2)}) collective-permute-start(bf16[112,768]{1,0:T(8,128)(2,1)S(1)} %get-tuple-element.23), channel_id=1, source_target_pairs={{0,64},{16,80},{32,96},{48,112},{64,0},{80,16},{96,32},{112,48},{1... | collective-permute-start | bytes 516104 | tf_op jit(solution)/shard_map/ppermute | solution.py:20
  97.1 4.9 %collective-permute-done.4.got._ = bf16[112,768]{1,0:T(8,128)(2,1)S(1)} collective-permute-done((bf16[112,768]{1,0:T(8,128)(2,1)S(1)}, bf16[112,768]{1,0:T(8,128)(2,1)S(1)}, u32[]{:S(2)}, u32[]{:S(2)}) %collective-permute-start.4) | collective-permute-done | bytes 172064 | tf_op jit(solution)/shard_map/ppermute | solution.py:20
  102.0 2.0 %grad_weight.1 = (f32[384,1152]{1,0:T(8,128)S(1)}, f32[384,1152]{1,0:T(8,128)S(1)}) custom-call(s32[1]{0:T(128)} %bitcast.2.row_ref, bf16[112,768]{1,0:T(8,128)(2,1)S(1)} %collective-permute-done.4.got._, bf16[768,1152]{1,0:T(8,128)(2,1)S(1)} %get-tuple-element.26.grads, bf16[192,768]{1,0:T(8,128)(2,1)S(1)} %collective-permute-done.9.x1, ...), custom_call_target="tpu_custom_call" | custom-call | flops 1358954496 | bytes 7340032 | tf_op jit(solution)/shard_map/grad_weight/pallas_call | solution.py:198
  104.0 14.9 %collective-permute-start.12 = (f32[384,1152]{1,0:T(8,128)S(1)}, f32[384,1152]{1,0:T(8,128)S(1)}, u32[]{:S(2)}, u32[]{:S(2)}) collective-permute-start(f32[384,1152]{1,0:T(8,128)S(1)} %get-tuple-element.29), channel_id=1, source_target_pairs={{0,256},{256,0},{512,768},{768,512},{1,257},{257,1},{513,769},{769... | collective-permute-start | bytes 5308424 | tf_op jit(solution)/shard_map/ppermute | solution.py:24
  118.9 3.3 %collective-permute-done.12.got = f32[384,1152]{1,0:T(8,128)S(1)} collective-permute-done((f32[384,1152]{1,0:T(8,128)S(1)}, f32[384,1152]{1,0:T(8,128)S(1)}, u32[]{:S(2)}, u32[]{:S(2)}) %collective-permute-start.12) | collective-permute-done | bytes 1769504 | tf_op jit(solution)/shard_map/ppermute | solution.py:24
  123.0 1.9 %collective-permute-start.13 = (bf16[208,1152]{1,0:T(8,128)(2,1)S(1)}, bf16[208,1152]{1,0:T(8,128)(2,1)S(1)}, u32[]{:S(2)}, u32[]{:S(2)}) collective-permute-start(bf16[208,1152]{1,0:T(8,128)(2,1)S(1)} %get-tuple-element.31), channel_id=1, source_target_pairs={{0,512},{256,768},{512,0},{768,256},{1,513},{257,769},{513,1},{769... | collective-permute-start | bytes 1437704 | tf_op jit(solution)/shard_map/ppermute | solution.py:24
  125.2 5.8 %collective-permute-start.5 = (bf16[64,768]{1,0:T(8,128)(2,1)S(1)}, bf16[64,768]{1,0:T(8,128)(2,1)S(1)}, u32[]{:S(2)}, u32[]{:S(2)}) collective-permute-start(bf16[64,768]{1,0:T(8,128)(2,1)S(1)} %get-tuple-element.25), channel_id=1, source_target_pairs={{0,192},{16,208},{32,224},{48,240},{64,128},{80,144},{96,160},{112... | collective-permute-start | bytes 294920 | tf_op jit(solution)/shard_map/ppermute | solution.py:20
  131.0 10.6 %collective-permute-done.5.got = bf16[64,768]{1,0:T(8,128)(2,1)S(1)} collective-permute-done((bf16[64,768]{1,0:T(8,128)(2,1)S(1)}, bf16[64,768]{1,0:T(8,128)(2,1)S(1)}, u32[]{:S(2)}, u32[]{:S(2)}) %collective-permute-start.5) | collective-permute-done | bytes 98336 | tf_op jit(solution)/shard_map/ppermute | solution.py:20
  142.3 1.4 shard_map.55
  (23 shorter events, 6.4 us)
Async XLA Ops:
  0.6 56.7 %copy-start = (bf16[768,1152]{1,0:T(8,128)(2,1)S(1)}, bf16[768,1152]{1,0:T(8,128)(2,1)}, u32[]{:S(2)}) copy-start(bf16[768,1152]{1,0:T(8,128)(2,1)} %weight_ref.1) | copy-start | bytes 5308420
  44.5 10.5 %collective-permute-start.1 = (bf16[192,1152]{1,0:T(8,128)(2,1)}, bf16[192,1152]{1,0:T(8,128)(2,1)S(1)}, u32[]{:S(2)}, u32[]{:S(2)}) collective-permute-start(bf16[192,1152]{1,0:T(8,128)(2,1)} %get-tuple-element.32), channel_id=1, source_target_pairs={{0,15},{1,2},{2,1},{3,4},{4,3},{5,6},{6,5},{7,8},{8,7},{9,10},{10,... | collective-permute-start | bytes 1327112 | tf_op jit(solution)/shard_map/ppermute | solution.py:168
  47.8 9.6 %collective-permute-start = (bf16[192,1152]{1,0:T(8,128)(2,1)}, bf16[192,1152]{1,0:T(8,128)(2,1)S(1)}, u32[]{:S(2)}, u32[]{:S(2)}) collective-permute-start(bf16[192,1152]{1,0:T(8,128)(2,1)} %get-tuple-element.33), channel_id=1, source_target_pairs={{0,1},{1,0},{2,3},{3,2},{4,5},{5,4},{6,7},{7,6},{8,9},{9,8},{10,11... | collective-permute-start | bytes 1327112 | tf_op jit(solution)/shard_map/ppermute | solution.py:167
  49.8 13.3 %copy-start.1 = (bf16[48,768]{1,0:T(8,128)(2,1)S(1)}, bf16[48,768]{1,0:T(8,128)(2,1)}, u32[]{:S(2)}) copy-start(bf16[48,768]{1,0:T(8,128)(2,1)} %param.3) | copy-start | bytes 221188
  60.3 22.1 %collective-permute-start.2 = (bf16[400,768]{1,0:T(8,128)(2,1)S(1)}, bf16[400,768]{1,0:T(8,128)(2,1)S(1)}, u32[]{:S(2)}, u32[]{:S(2)}) collective-permute-start(bf16[400,768]{1,0:T(8,128)(2,1)S(1)} %get-tuple-element.19), channel_id=1, source_target_pairs={{0,16},{16,0},{32,48},{48,32},{64,80},{80,64},{96,112},{112,96},{1... | collective-permute-start | bytes 1843208 | tf_op jit(solution)/shard_map/ppermute | solution.py:16
  63.1 15.5 %collective-permute-start.8 = (bf16[48,768]{1,0:T(8,128)(2,1)S(1)}, bf16[48,768]{1,0:T(8,128)(2,1)S(1)}, u32[]{:S(2)}, u32[]{:S(2)}) collective-permute-start(bf16[48,768]{1,0:T(8,128)(2,1)S(1)} %copy-done.1), channel_id=1, source_target_pairs={{0,128},{16,144},{32,160},{48,176},{64,192},{80,208},{96,224},{112... | collective-permute-start | bytes 221192 | tf_op jit(solution)/shard_map/ppermute | solution.py:20
  70.6 8.0 %collective-permute-start.7 = (bf16[48,768]{1,0:T(8,128)(2,1)S(1)}, bf16[48,768]{1,0:T(8,128)(2,1)S(1)}, u32[]{:S(2)}, u32[]{:S(2)}) collective-permute-start(bf16[48,768]{1,0:T(8,128)(2,1)S(1)} %copy-done.1), channel_id=1, source_target_pairs={{0,192},{16,208},{32,224},{48,240},{64,128},{80,144},{96,160},{112... | collective-permute-start | bytes 221192 | tf_op jit(solution)/shard_map/ppermute | solution.py:20
  72.6 6.0 %collective-permute-start.6 = (bf16[48,768]{1,0:T(8,128)(2,1)S(1)}, bf16[48,768]{1,0:T(8,128)(2,1)S(1)}, u32[]{:S(2)}, u32[]{:S(2)}) collective-permute-start(bf16[48,768]{1,0:T(8,128)(2,1)S(1)} %copy-done.1), channel_id=1, source_target_pairs={{0,64},{16,80},{32,96},{48,112},{64,0},{80,16},{96,32},{112,48},{1... | collective-permute-start | bytes 221192 | tf_op jit(solution)/shard_map/ppermute | solution.py:20
  78.6 9.5 %collective-permute-start.10 = (bf16[192,768]{1,0:T(8,128)(2,1)S(1)}, bf16[192,768]{1,0:T(8,128)(2,1)S(1)}, u32[]{:S(2)}, u32[]{:S(2)}) collective-permute-start(bf16[192,768]{1,0:T(8,128)(2,1)S(1)} %constant_dynamic-update-slice_fusion.x0), channel_id=1, source_target_pairs={{0,48},{16,32},{32,16},{48,0},{64,112},{80,96},{96,80},{112,64},{1... | collective-permute-start | bytes 884744 | tf_op jit(solution)/shard_map/ppermute | solution.py:16
  83.4 8.9 %collective-permute-start.3 = (bf16[208,768]{1,0:T(8,128)(2,1)S(1)}, bf16[208,768]{1,0:T(8,128)(2,1)S(1)}, u32[]{:S(2)}, u32[]{:S(2)}) collective-permute-start(bf16[208,768]{1,0:T(8,128)(2,1)S(1)} %get-tuple-element.21), channel_id=1, source_target_pairs={{0,48},{16,32},{32,16},{48,0},{64,112},{80,96},{96,80},{112,64},{1... | collective-permute-start | bytes 958472 | tf_op jit(solution)/shard_map/ppermute | solution.py:16
  86.2 9.8 %collective-permute-start.9 = (bf16[192,768]{1,0:T(8,128)(2,1)S(1)}, bf16[192,768]{1,0:T(8,128)(2,1)S(1)}, u32[]{:S(2)}, u32[]{:S(2)}) collective-permute-start(bf16[192,768]{1,0:T(8,128)(2,1)S(1)} %constant_dynamic-update-slice_fusion.x0), channel_id=1, source_target_pairs={{0,16},{16,0},{32,48},{48,32},{64,80},{80,64},{96,112},{112,96},{1... | collective-permute-start | bytes 884744 | tf_op jit(solution)/shard_map/ppermute | solution.py:16
  88.1 9.0 %collective-permute-start.11 = (bf16[192,768]{1,0:T(8,128)(2,1)S(1)}, bf16[192,768]{1,0:T(8,128)(2,1)S(1)}, u32[]{:S(2)}, u32[]{:S(2)}) collective-permute-start(bf16[192,768]{1,0:T(8,128)(2,1)S(1)} %collective-permute-done.10.x3), channel_id=1, source_target_pairs={{0,16},{16,0},{32,48},{48,32},{64,80},{80,64},{96,112},{112,96},{1... | collective-permute-start | bytes 884744 | tf_op jit(solution)/shard_map/ppermute | solution.py:16
  92.8 9.2 %collective-permute-start.4 = (bf16[112,768]{1,0:T(8,128)(2,1)S(1)}, bf16[112,768]{1,0:T(8,128)(2,1)S(1)}, u32[]{:S(2)}, u32[]{:S(2)}) collective-permute-start(bf16[112,768]{1,0:T(8,128)(2,1)S(1)} %get-tuple-element.23), channel_id=1, source_target_pairs={{0,64},{16,80},{32,96},{48,112},{64,0},{80,16},{96,32},{112,48},{1... | collective-permute-start | bytes 516104 | tf_op jit(solution)/shard_map/ppermute | solution.py:20
  104.0 18.2 %collective-permute-start.12 = (f32[384,1152]{1,0:T(8,128)S(1)}, f32[384,1152]{1,0:T(8,128)S(1)}, u32[]{:S(2)}, u32[]{:S(2)}) collective-permute-start(f32[384,1152]{1,0:T(8,128)S(1)} %get-tuple-element.29), channel_id=1, source_target_pairs={{0,256},{256,0},{512,768},{768,512},{1,257},{257,1},{513,769},{769... | collective-permute-start | bytes 5308424 | tf_op jit(solution)/shard_map/ppermute | solution.py:24
  123.0 19.3 %collective-permute-start.13 = (bf16[208,1152]{1,0:T(8,128)(2,1)S(1)}, bf16[208,1152]{1,0:T(8,128)(2,1)S(1)}, u32[]{:S(2)}, u32[]{:S(2)}) collective-permute-start(bf16[208,1152]{1,0:T(8,128)(2,1)S(1)} %get-tuple-element.31), channel_id=1, source_target_pairs={{0,512},{256,768},{512,0},{768,256},{1,513},{257,769},{513,1},{769... | collective-permute-start | bytes 1437704 | tf_op jit(solution)/shard_map/ppermute | solution.py:24
  125.2 16.4 %collective-permute-start.5 = (bf16[64,768]{1,0:T(8,128)(2,1)S(1)}, bf16[64,768]{1,0:T(8,128)(2,1)S(1)}, u32[]{:S(2)}, u32[]{:S(2)}) collective-permute-start(bf16[64,768]{1,0:T(8,128)(2,1)S(1)} %get-tuple-element.25), channel_id=1, source_target_pairs={{0,192},{16,208},{32,224},{48,240},{64,128},{80,144},{96,160},{112... | collective-permute-start | bytes 294920 | tf_op jit(solution)/shard_map/ppermute | solution.py:20
